TPU v7x, 32 devices: a whole 2x2x4 slice. The times are simulated.
32 devices in a mesh: groups: 2 (over x), expert: 16 (over z, y, core).
Axes of the slice: x: 2, y: 2, z: 4, core: 2. Of those that a mesh axis runs over, the one named last changes fastest.
Arguments:
- tokens: bfloat16 [4096, 1664], P(('groups', 'expert')), parts along dimension 0, may hold values from -6 to 6
- expert_ids: int32 [4096, 2], P(('groups', 'expert')), parts along dimension 0, may hold values from 0 to 15, all different within a row
- priority: int32 [32, 128], P(('groups', 'expert')), parts along dimension 0, may hold values from 0 to 127, each once within a row
- gates: float32 [4096, 2], P(('groups', 'expert')), parts along dimension 0, may hold values from 0.1 to 1
- w_in: bfloat16 [16, 1664, 6144], P('expert'), may hold values from -0.15625 to 0.15625
- w_out: bfloat16 [16, 6144, 1664], P('expert'), may hold values from -0.078125 to 0.078125
- cotangent: bfloat16 [4096, 1664], P(('groups', 'expert')), parts along dimension 0, may hold values from -6 to 6
Outputs:
- mixed: bfloat16 [4096, 1664], P(('groups', 'expert')), parts along dimension 0
- d_tokens: bfloat16 [4096, 1664], P(('groups', 'expert')), parts along dimension 0
- d_gates: float32 [4096, 2], P(('groups', 'expert')), parts along dimension 0
- d_w_in: bfloat16 [32, 1664, 6144], P(('groups', 'expert')), parts along dimension 0
- d_w_out: bfloat16 [32, 6144, 1664], P(('groups', 'expert')), parts along dimension 0
There are 2 independent parts, one for each index of `groups`. A program takes and returns all parts, laid end to end along the dimension named above; an argument that names none is the same for every part. Nothing has to cross between parts.
Inputs may be any that keep to these rules, and one draw needn't show every extreme that they name: `expert_ids`: each token names two different experts. `priority`: each row holds every rank of its block once.
All inputs are finite; a program needn't handle non-finite values.
Results may differ from a plain program's by a relative error of at most 0.006.
Values may be sent and summed in bfloat16 or wider, within the bound.
No kernel may reach another device: no remote copies, remote signals or barrier semaphores. Data moves between devices by JAX's collectives and lax.ppermute only.
A program may use at most 192 MiB of HBM per device.

v0:
```python
import math

import jax
import jax.numpy as jnp
from jax import lax
from jax.sharding import PartitionSpec as P

EXPERTS = 16
CAP = 4


def gelu_parts(value):
    coef = math.sqrt(2.0 / math.pi)
    inner = coef * (value + 0.044715 * value * value * value)
    hyper = jnp.tanh(inner)
    result = 0.5 * value * (1.0 + hyper)
    slope = 0.5 * (1.0 + hyper) + 0.5 * value * (1.0 - hyper * hyper) * coef * (
        1.0 + 3.0 * 0.044715 * value * value
    )
    return (result, slope)


def slot_table(ids_blk, prio_blk, tok_count):
    expert_of = jnp.transpose(ids_blk, (1, 0)).reshape(2 * tok_count)
    key_of = jnp.concatenate([prio_blk, prio_blk + tok_count], axis=0)
    same = expert_of[:, None] == expert_of[None, :]
    before = key_of[None, :] < key_of[:, None]
    slot = jnp.sum((same & before).astype(jnp.int32), axis=1)
    place = jnp.where(slot < CAP, expert_of * CAP + slot, -1)
    columns = jnp.arange(EXPERTS * CAP, dtype=jnp.int32)
    return ((place[:, None] == columns[None, :]).astype(jnp.float32), place)


def per_device(tokens, expert_ids, priority, gates, w_in, w_out, cotangent):
    tok_count, width = tokens.shape
    slots_all = EXPERTS * CAP
    repl = lax.axis_size("expert") // EXPERTS
    w_first = w_in[0]
    w_second = w_out[0]
    dy_full = cotangent.astype(jnp.float32)
    onehot, place = slot_table(expert_ids, priority[0], tok_count)
    disp = onehot.reshape(2, tok_count, slots_all).sum(0)
    gate_of = jnp.concatenate([gates[:, 0], gates[:, 1]], axis=0)
    weighted = (onehot * gate_of[:, None]).reshape(2, tok_count, slots_all).sum(0)
    slot_gate = jnp.sum(weighted, axis=0)
    disp_low = disp.astype(jnp.bfloat16)
    contract = (((0,), (0,)), ((), ()))
    rows = lax.dot_general(disp_low, tokens, contract, preferred_element_type=jnp.float32).astype(
        jnp.bfloat16
    )
    dy_rows = lax.dot_general(disp_low, cotangent, contract, preferred_element_type=jnp.float32)
    grad_rows = (slot_gate[:, None] * dy_rows).astype(jnp.bfloat16)
    send_x = jnp.tile(rows.reshape(EXPERTS, CAP, width), (repl, 1, 1))
    send_g = jnp.tile(grad_rows.reshape(EXPERTS, CAP, width), (repl, 1, 1))
    x_items = lax.all_to_all(send_x, "expert", split_axis=0, concat_axis=0, tiled=True)
    g_items = lax.all_to_all(send_g, "expert", split_axis=0, concat_axis=0, tiled=True)
    count = x_items.shape[0]
    depth = x_items.shape[1]
    x_flat = x_items.reshape(count * depth, width)
    g_flat = g_items.reshape(count * depth, width)
    pre = jnp.dot(x_flat, w_first, preferred_element_type=jnp.float32)
    value, slope = gelu_parts(pre)
    act = value.astype(jnp.bfloat16)
    out_part = jnp.dot(act, w_second, preferred_element_type=jnp.float32).astype(jnp.bfloat16)
    d_act = lax.dot_general(
        g_flat, w_second, (((1,), (1,)), ((), ())), preferred_element_type=jnp.float32
    )
    d_pre = (d_act * slope).astype(jnp.bfloat16)
    back_part = lax.dot_general(
        d_pre, w_first, (((1,), (1,)), ((), ())), preferred_element_type=jnp.float32
    ).astype(jnp.bfloat16)
    hidden = act.shape[1]
    out_part, back_part, act, d_pre, x_recv, g_recv = (
        out_part.reshape(count, depth, width),
        back_part.reshape(count, depth, width),
        act.reshape(count, depth, hidden),
        d_pre.reshape(count, depth, hidden),
        x_items,
        g_items,
    )
    hidden = act.shape[2]
    d_w_in = lax.dot_general(
        x_recv.reshape(-1, width),
        d_pre.reshape(-1, hidden),
        contract,
        preferred_element_type=jnp.float32,
    ).astype(jnp.bfloat16)
    d_w_out = lax.dot_general(
        act.reshape(-1, hidden),
        g_recv.reshape(-1, width),
        contract,
        preferred_element_type=jnp.float32,
    ).astype(jnp.bfloat16)
    ret_out, ret_back = (
        lax.all_to_all(out_part, "expert", split_axis=0, concat_axis=0, tiled=True),
        lax.all_to_all(back_part, "expert", split_axis=0, concat_axis=0, tiled=True),
    )
    out_rows = (
        ret_out.reshape(repl, EXPERTS, CAP, width)
        .astype(jnp.float32)
        .sum(0)
        .reshape(slots_all, width)
    )
    back_rows = (
        ret_back.reshape(repl, EXPERTS, CAP, width)
        .astype(jnp.float32)
        .sum(0)
        .reshape(slots_all, width)
    )
    kept = (place >= 0)[:, None]
    index_of = jnp.maximum(place, 0)
    picked = jnp.where(kept, jnp.take(out_rows, index_of, axis=0), 0.0).reshape(2, tok_count, width)
    mixed = (gates[:, 0, None] * picked[0] + gates[:, 1, None] * picked[1]).astype(jnp.bfloat16)
    d_gates = jnp.stack(
        [jnp.sum(dy_full * picked[0], axis=-1), jnp.sum(dy_full * picked[1], axis=-1)], axis=-1
    )
    backs = jnp.where(kept, jnp.take(back_rows, index_of, axis=0), 0.0).reshape(2, tok_count, width)
    d_tokens = (backs[0] + backs[1]).astype(jnp.bfloat16)
    return (mixed, d_tokens, d_gates, d_w_in[None], d_w_out[None])


def solution(mesh):
    placed = (
        P(("groups", "expert"), None),
        P(("groups", "expert"), None),
        P(("groups", "expert"), None),
        P(("groups", "expert"), None),
        P("expert", None, None),
        P("expert", None, None),
        P(("groups", "expert"), None),
    )
    return jax.shard_map(
        per_device,
        mesh=mesh,
        in_specs=placed,
        out_specs=(
            P(("groups", "expert"), None),
            P(("groups", "expert"), None),
            P(("groups", "expert"), None),
            P(("groups", "expert"), None, None),
            P(("groups", "expert"), None, None),
        ),
        check_vma=False,
    )
```

profile of v0, /device:TPU:0, one launch (start us, length us, event | category | flops | bytes accessed | tf_op | source)
XLA Modules:
  0.0 107.1 jit_solution(6087695565086886932)
XLA Ops:
  0.7 0.7 broadcast_add_fusion
  2.1 1.0 convert_reduce_fusion
  3.0 0.7 compare_select_fusion
  3.7 0.8 slice_bitcast_fusion.1
  4.8 0.7 tile_reshape.6
  5.5 7.4 %all-to-all-start = ((bf16[16,4,1664]{2,1,0:T(4,128)(2,1)}), bf16[16,4,1664]{2,1,0:T(4,128)(2,1)S(1)}, u32[]{:S(2)}, u32[]{:S(2)}) async-start(bf16[16,4,1664]{2,1,0:T(4,128)(2,1)} %tile_reshape.6), calls=%async_computation | async-start | bytes 425984 | tf_op jit(solution)/shard_map/all_to_all | solution.py:55
  13.8 0.7 tile_reshape.7
  14.6 7.6 %all-to-all-done = bf16[16,4,1664]{2,1,0:T(4,128)(2,1)S(1)} async-done(((bf16[16,4,1664]{2,1,0:T(4,128)(2,1)}), bf16[16,4,1664]{2,1,0:T(4,128)(2,1)S(1)}, u32[]{:S(2)}, u32[]{:S(2)}) %all-to-all-start) | async-done | bytes 213024 | tf_op jit(solution)/shard_map/all_to_all | solution.py:55
  22.2 3.5 %all-to-all-start.2 = ((bf16[16,4,1664]{2,1,0:T(4,128)(2,1)}), bf16[16,4,1664]{2,1,0:T(4,128)(2,1)S(1)}, u32[]{:S(2)}, u32[]{:S(2)}) async-start(bf16[16,4,1664]{2,1,0:T(4,128)(2,1)} %tile_reshape.7), calls=%async_computation.2 | async-start | bytes 425984 | tf_op jit(solution)/shard_map/all_to_all | solution.py:56
  25.8 8.7 %fusion.6 = f32[64,6144]{1,0:T(8,128)S(1)} fusion(bf16[64,1664]{1,0:T(8,128)(2,1)S(1)} %reshape.107, bf16[1,1664,6144]{2,1,0:T(8,128)(2,1)} %param.13), kind=kOutput, calls=%fused_computation.10 | convolution fusion | flops 1308622848 | bytes 22233088 | tf_op jit(solution)/shard_map/dot_general | solution.py:61
  35.0 10.4 %fusion.13 = bf16[64,6144]{1,0:T(8,128)(2,1)S(1)} fusion(bf16[64,1664]{1,0:T(8,128)(2,1)S(1)} %reshape.111, bf16[1,6144,1664]{2,1,0:T(8,128)(2,1)} %param.14, f32[64,6144]{1,0:T(8,128)S(1)} %fusion.6), kind=kOutput, calls=%fused_computation.15 | convolution fusion | flops 1316093952 | bytes 23019520 | tf_op jit(solution)/shard_map/dot_general | solution.py:65
  45.4 10.3 %fusion.17 = bf16[64,1664]{1,0:T(8,128)(2,1)S(1)} fusion(bf16[64,6144]{1,0:T(8,128)(2,1)S(1)} %fusion.13, bf16[1,1664,6144]{2,1,0:T(8,128)(2,1)} %param.13), kind=kOutput, calls=%fused_computation.20 | convolution fusion | flops 1308729344 | bytes 21446656 | tf_op jit(solution)/shard_map/dot_general | solution.py:69
  55.7 0.7 reshape.112
  56.5 5.6 %all-to-all-start.3 = ((bf16[16,4,1664]{2,1,0:T(4,128)(2,1)}), bf16[16,4,1664]{2,1,0:T(4,128)(2,1)}, u32[]{:S(2)}, u32[]{:S(2)}) async-start(bf16[16,4,1664]{2,1,0:T(4,128)(2,1)} %reshape.112), calls=%async_computation.3 | async-start | bytes 425984 | tf_op jit(solution)/shard_map/all_to_all | solution.py:96
  62.1 8.7 %fusion.20 = bf16[64,1664]{1,0:T(8,128)(2,1)S(1)} fusion(bf16[1,6144,1664]{2,1,0:T(8,128)(2,1)} %param.14, f32[64,6144]{1,0:T(8,128)S(1)} %fusion.6), kind=kOutput, calls=%fused_computation.21 | convolution fusion | flops 1312268288 | bytes 22233088 | tf_op jit(solution)/shard_map/dot_general | solution.py:64
  70.8 0.7 reshape.108
  71.6 6.0 %all-to-all-start.1 = ((bf16[16,4,1664]{2,1,0:T(4,128)(2,1)}), bf16[16,4,1664]{2,1,0:T(4,128)(2,1)S(1)}, u32[]{:S(2)}, u32[]{:S(2)}) async-start(bf16[16,4,1664]{2,1,0:T(4,128)(2,1)} %reshape.108), calls=%async_computation.1 | async-start | bytes 425984 | tf_op jit(solution)/shard_map/all_to_all | solution.py:95
  77.6 10.3 %fusion.9 = bf16[1,6144,1664]{2,1,0:T(8,128)(2,1)} fusion(bf16[64,1664]{1,0:T(8,128)(2,1)S(1)} %reshape.111, f32[64,6144]{1,0:T(8,128)S(1)} %fusion.6), kind=kOutput, calls=%fused_computation.13 | convolution fusion | flops 1322385408 | bytes 22233088 | tf_op jit(solution)/shard_map/dot_general | solution.py:88
  87.8 10.2 %fusion.8 = bf16[1,1664,6144]{2,1,0:T(8,128)(2,1)} fusion(bf16[64,1664]{1,0:T(8,128)(2,1)S(1)} %reshape.107, bf16[64,6144]{1,0:T(8,128)(2,1)S(1)} %fusion.13), kind=kOutput, calls=%fused_computation.12 | convolution fusion | flops 1318846464 | bytes 21446656 | tf_op jit(solution)/shard_map/dot_general | solution.py:82
  98.1 1.0 reshape.118
  99.0 1.5 %gather_fusion.1 = f32[256,1664]{1,0:T(8,128)S(1)} fusion(f32[64,1664]{1,0:T(8,128)S(1)} %reshape.118, s32[1024]{0:T(1024)S(1)} %pad_clamp_fusion), kind=kCustom, calls=%fused_computation.1.clone | custom fusion | bytes 3408896 | tf_op jit(solution)/shard_map/jit(_take)/gather | solution.py:117
  100.5 2.6 %gather_fusion = f32[256,1664]{1,0:T(8,128)} fusion(f32[64,1664]{1,0:T(8,128)S(1)} %reshape.116, s32[1024]{0:T(1024)S(1)} %pad_clamp_fusion), kind=kCustom, calls=%fused_computation.clone | custom fusion | bytes 3408896 | tf_op jit(solution)/shard_map/jit(_take)/gather | solution.py:112
  103.1 1.9 %select_select_fusion = (f32[256,1664]{1,0:T(8,128)S(1)}, f32[256,1664]{1,0:T(8,128)S(1)}) fusion(f32[256,1664]{1,0:T(8,128)S(1)} %gather_fusion.1, pred[256]{0:T(512)(128)(4,1)S(1)} %broadcast_compare_fusion, pred[256]{0:T(512)(128)(4,1)S(1)} %get-tuple-element.10, f32[256,1664]{1,0:T(8,128)} %gather_fusion), kind=kLoop, calls=%fused_computation.23 | loop fusion | flops 1703936 | bytes 6816256 | tf_op jit(solution)/shard_map/jit(_where)/select_n | solution.py:117
  105.1 1.4 %fusion.28 = (f32[128]{0:T(128)S(1)}, f32[128]{0:T(128)S(1)}, bf16[128,1664]{1,0:T(8,128)(2,1)}, bf16[128,1664]{1,0:T(8,128)(2,1)}) fusion(bf16[128,1664]{1,0:T(8,128)(2,1)S(1)} %copy-done.2, f32[256,1664]{1,0:T(8,128)S(1)} %get-tuple-element.14, f32[128]{0:T(128)S(1)} %get-tuple-element.16, f32[128]{0:T(128)S(1)} %get-tuple-element.15, ...), kind=kLoop, calls=%fused_computation.33 | loop fusion | flops 2342656 | bytes 4687872 | tf_op jit(solution)/shard_map/reduce_sum | solution.py:115
  (22 shorter events, 3.0 us)
Async XLA Ops:
  0.6 4.0 %copy-start = (bf16[128,1664]{1,0:T(8,128)(2,1)S(1)}, bf16[128,1664]{1,0:T(8,128)(2,1)}, u32[]{:S(2)}) copy-start(bf16[128,1664]{1,0:T(8,128)(2,1)} %param.9) | copy-start | bytes 1277956
  0.6 13.0 %copy-start.2 = (bf16[128,1664]{1,0:T(8,128)(2,1)S(1)}, bf16[128,1664]{1,0:T(8,128)(2,1)}, u32[]{:S(2)}) copy-start(bf16[128,1664]{1,0:T(8,128)(2,1)} %param.15) | copy-start | bytes 1277956
  5.5 16.7 %all-to-all-start = ((bf16[16,4,1664]{2,1,0:T(4,128)(2,1)}), bf16[16,4,1664]{2,1,0:T(4,128)(2,1)S(1)}, u32[]{:S(2)}, u32[]{:S(2)}) async-start(bf16[16,4,1664]{2,1,0:T(4,128)(2,1)} %tile_reshape.6), calls=%async_computation | async-start | bytes 425984 | tf_op jit(solution)/shard_map/all_to_all | solution.py:55
  22.2 12.7 %all-to-all-start.2 = ((bf16[16,4,1664]{2,1,0:T(4,128)(2,1)}), bf16[16,4,1664]{2,1,0:T(4,128)(2,1)S(1)}, u32[]{:S(2)}, u32[]{:S(2)}) async-start(bf16[16,4,1664]{2,1,0:T(4,128)(2,1)} %tile_reshape.7), calls=%async_computation.2 | async-start | bytes 425984 | tf_op jit(solution)/shard_map/all_to_all | solution.py:56
  56.5 15.1 %all-to-all-start.3 = ((bf16[16,4,1664]{2,1,0:T(4,128)(2,1)}), bf16[16,4,1664]{2,1,0:T(4,128)(2,1)}, u32[]{:S(2)}, u32[]{:S(2)}) async-start(bf16[16,4,1664]{2,1,0:T(4,128)(2,1)} %reshape.112), calls=%async_computation.3 | async-start | bytes 425984 | tf_op jit(solution)/shard_map/all_to_all | solution.py:96
  71.6 28.9 %all-to-all-start.1 = ((bf16[16,4,1664]{2,1,0:T(4,128)(2,1)}), bf16[16,4,1664]{2,1,0:T(4,128)(2,1)S(1)}, u32[]{:S(2)}, u32[]{:S(2)}) async-start(bf16[16,4,1664]{2,1,0:T(4,128)(2,1)} %reshape.108), calls=%async_computation.1 | async-start | bytes 425984 | tf_op jit(solution)/shard_map/all_to_all | solution.py:95
  105.1 2.0 %copy-start.1 = (bf16[128,1664]{1,0:T(8,128)(2,1)S(1)}, bf16[128,1664]{1,0:T(8,128)(2,1)}, u32[]{:S(2)}) copy-start(bf16[128,1664]{1,0:T(8,128)(2,1)} %param.9) | copy-start | bytes 1277956
where the time goes:
time: 108 us; the launch traced here: 107 us
  matrix products  59.1 us (55%)
  starting transfers between devices  22.5 us (21%)
  local copies, waits for them, and re-layouts  8.86 us (8%)
  waiting for transfers between devices  8 us (7%)
  other arithmetic  7.79 us (7%)
    dot_general x1, matrix products, per_device(): lax.dot_general(g_flat, w_second, (((1,), (1,)), ((), ())), preferred_ele...  10.4 us
    dot_general x1, matrix products, per_device(): lax.dot_general(d_pre, w_first, (((1,), (1,)), ((), ())), preferred_eleme...  10.3 us
    dot_general x1, matrix products, per_device(): lax.dot_general(act.reshape(-1, hidden), g_recv.reshape(-1, width), contr...  10.3 us
    dot_general x1, matrix products, per_device(): lax.dot_general(x_recv.reshape(-1, width), d_pre.reshape(-1, hidden), con...  10.2 us
    dot_general x1, matrix products, per_device(): pre = jnp.dot(x_flat, w_first, preferred_element_type=jnp.float32)  8.75 us
    dot_general x1, matrix products, per_device(): jnp.dot(act, w_second, preferred_element_type=jnp.float32)  8.74 us
    all_to_all x1, waiting for transfers between devices, per_device(): lax.all_to_all(send_x, 'expert', split_axis=0, concat_axis=0, tiled=True)  7.59 us
    all_to_all x1, starting transfers between devices, per_device(): lax.all_to_all(send_x, 'expert', split_axis=0, concat_axis=0, tiled=True)  7.39 us
  transfers between devices with their start and end apart: 4, of which 2 were waited for; matrix products, arithmetic and copies ran while one was open for 40% of the time, Pallas kernels for 0%

commit v1 on v0

v1 whole, which is shorter than its diff:
```python
import functools
import math

import jax
import jax.numpy as jnp
from jax import lax
from jax.experimental import pallas as pl
from jax.experimental.pallas import tpu as pltpu
from jax.sharding import PartitionSpec as P

EXPERTS = 16
CAP = 4
PAIR = 2 * CAP
VMEM_BYTES = 60 * 1024 * 1024
ROWS_DIM = (((0,), (0,)), ((), ()))
LAST_DIM = (((1,), (1,)), ((), ()))


def gelu_parts(value):
    coef = math.sqrt(2.0 / math.pi)
    square = value * value
    hyper = jnp.tanh(coef * value * (1.0 + 0.044715 * square))
    half = 0.5 * (1.0 + hyper)
    slope = half + 0.5 * value * (1.0 - hyper * hyper) * coef * (1.0 + 3.0 * 0.044715 * square)
    return (value * half, slope)


def place_rows(ids_t, prio):
    count = ids_t.shape[1]
    first = ids_t[0:1, :]
    second = ids_t[1:2, :]
    stack = jnp.concatenate([first, second, prio, jnp.zeros((5, count), jnp.int32)], axis=0)
    columns = jnp.transpose(stack.astype(jnp.float32), (1, 0)).astype(jnp.int32)
    first_c, second_c, prio_c = columns[:, 0:1], columns[:, 1:2], columns[:, 2:3]
    ahead = prio_c < prio
    one = jnp.float32(1.0)
    zero = jnp.float32(0.0)
    slot_0 = jnp.sum(jnp.where((first_c == first) & ahead, one, zero), axis=0, keepdims=True)
    slot_1 = jnp.sum(
        jnp.where((first_c == second) | ((second_c == second) & ahead), one, zero),
        axis=0,
        keepdims=True,
    )
    slot_0 = slot_0.astype(jnp.int32)
    slot_1 = slot_1.astype(jnp.int32)
    place_0 = jnp.where(slot_0 < CAP, first * CAP + slot_0, -1)
    place_1 = jnp.where(slot_1 < CAP, second * CAP + slot_1, -1)
    return place_0, place_1


def dispatch_kernel(ids_ref, prio_ref, gates_ref, tok_ref, cot_ref, send_ref):
    place_0, place_1 = place_rows(ids_ref[...], prio_ref[...])
    count = tok_ref.shape[0]
    rows = EXPERTS * PAIR
    row = lax.broadcasted_iota(jnp.int32, (rows, count), 0)
    slot = row // PAIR * CAP + row % CAP
    is_x = row % PAIR < CAP
    hit_0 = slot == place_0
    hit_1 = slot == place_1
    hit = jnp.where(hit_0 | hit_1, 1.0, 0.0)
    pick = jnp.concatenate(
        [jnp.where(is_x, hit, 0.0), jnp.where(is_x, 0.0, hit)], axis=1
    ).astype(jnp.bfloat16)
    gate = jnp.where(hit_0, gates_ref[0:1, :], 0.0) + jnp.where(hit_1, gates_ref[1:2, :], 0.0)
    scale = jnp.sum(gate, axis=1, keepdims=True)
    scale = jnp.where(is_x[:, 0:1], 1.0, scale)
    both = jnp.concatenate([tok_ref[...], cot_ref[...]], axis=0)
    found = jnp.dot(pick, both, preferred_element_type=jnp.float32)
    send_ref[...] = (found * scale).astype(jnp.bfloat16)


def tables_kernel(ids_ref, prio_ref, gates_ref, pick_ref, gate_ref):
    place_0, place_1 = place_rows(ids_ref[...], prio_ref[...])
    count = place_0.shape[1]
    rows = EXPERTS * PAIR
    row = lax.broadcasted_iota(jnp.int32, (rows, count), 0)
    slot = row // PAIR * CAP + row % CAP
    is_x = row % PAIR < CAP
    hit_0 = jnp.where(slot == place_0, 1.0, 0.0)
    hit_1 = jnp.where(slot == place_1, 1.0, 0.0)
    pick_0 = jnp.transpose(jnp.where(is_x, hit_0, 0.0), (1, 0))
    pick_1 = jnp.transpose(jnp.where(is_x, hit_1, 0.0), (1, 0))
    pick_b = jnp.transpose(jnp.where(is_x, 0.0, hit_0 + hit_1), (1, 0))
    pick_ref[...] = jnp.concatenate([pick_0, pick_1, pick_b], axis=0).astype(jnp.bfloat16)
    gates = jnp.concatenate([gates_ref[...], jnp.zeros((6, count), jnp.float32)], axis=0)
    gate_ref[...] = jnp.transpose(gates, (1, 0))


def row_picks(rows):
    half = rows // 2
    out = lax.broadcasted_iota(jnp.int32, (half, rows), 0)
    col = lax.broadcasted_iota(jnp.int32, (half, rows), 1)
    source = out // CAP * PAIR + out % CAP
    x_pick = jnp.where(col == source, 1.0, 0.0).astype(jnp.bfloat16)
    g_pick = jnp.where(col == source + CAP, 1.0, 0.0).astype(jnp.bfloat16)
    return x_pick, g_pick


def forward_kernel(
    steps, recv_ref, w_in_hbm, w_out_hbm, ret_ref, x_ref, g_ref, act_ref, d_pre_ref,
    w_in_ref, w_out_ref, out_acc, back_acc, sem_in, sem_out,
):
    depth = w_in_ref.shape[2]

    def copies(step):
        cols = pl.ds(pl.multiple_of(step * depth, depth), depth)
        return (
            pltpu.make_async_copy(w_in_hbm.at[:, cols], w_in_ref.at[step], sem_in.at[step]),
            pltpu.make_async_copy(w_out_hbm.at[cols, :], w_out_ref.at[step], sem_out.at[step]),
        )

    def begin(step, carry):
        for copy in copies(step):
            copy.start()
        return carry

    lax.fori_loop(0, steps, begin, 0)
    rows = recv_ref.shape[0]
    x_pick, g_pick = row_picks(rows)
    x_ref[...] = jnp.dot(x_pick, recv_ref[...], preferred_element_type=jnp.float32).astype(
        jnp.bfloat16
    )
    g_ref[...] = jnp.dot(g_pick, recv_ref[...], preferred_element_type=jnp.float32).astype(
        jnp.bfloat16
    )
    out_acc[...] = jnp.zeros_like(out_acc)
    back_acc[...] = jnp.zeros_like(back_acc)

    def front(step):
        for copy in copies(step):
            copy.wait()
        pre = jnp.dot(x_ref[...], w_in_ref[step], preferred_element_type=jnp.float32)
        d_act = lax.dot_general(
            g_ref[...], w_out_ref[step], LAST_DIM, preferred_element_type=jnp.float32
        )
        value, slope = gelu_parts(pre)
        act_ref[step] = value.astype(jnp.bfloat16)
        d_pre_ref[step] = (d_act * slope).astype(jnp.bfloat16)

    def back(step):
        out_acc[...] += jnp.dot(
            act_ref[step], w_out_ref[step], preferred_element_type=jnp.float32
        )
        back_acc[...] += lax.dot_general(
            d_pre_ref[step], w_in_ref[step], LAST_DIM, preferred_element_type=jnp.float32
        )

    front(0)

    def body(step, carry):
        back(step - 1)
        front(step)
        return carry

    lax.fori_loop(1, steps, body, 0)
    back(steps - 1)
    ret = lax.dot_general(
        x_pick, out_acc[...].astype(jnp.bfloat16), ROWS_DIM, preferred_element_type=jnp.float32
    ) + lax.dot_general(
        g_pick, back_acc[...].astype(jnp.bfloat16), ROWS_DIM, preferred_element_type=jnp.float32
    )
    ret_ref[...] = ret.astype(jnp.bfloat16)


def grads_kernel(x_ref, g_ref, act_ref, d_pre_ref, d_in_ref, d_out_ref):
    d_in_ref[...] = lax.dot_general(
        x_ref[...], d_pre_ref[0], ROWS_DIM, preferred_element_type=jnp.float32
    ).astype(jnp.bfloat16)
    d_out_ref[...] = lax.dot_general(
        act_ref[0], g_ref[...], ROWS_DIM, preferred_element_type=jnp.float32
    ).astype(jnp.bfloat16)


def combine_kernel(ret_ref, pick_ref, gate_ref, cot_ref, mixed_ref, d_tok_ref, d_gate_ref):
    count = cot_ref.shape[0]
    rows = pick_ref.shape[1]
    found = None
    for first in range(0, ret_ref.shape[0], rows):
        part = jnp.dot(
            pick_ref[...], ret_ref[first:first + rows, :], preferred_element_type=jnp.float32
        )
        found = part if found is None else found + part
    o_0, o_1 = found[:count], found[count:2 * count]
    mixed_ref[...] = (gate_ref[:, 0:1] * o_0 + gate_ref[:, 1:2] * o_1).astype(jnp.bfloat16)
    d_tok_ref[...] = found[2 * count:].astype(jnp.bfloat16)
    cot = cot_ref[...].astype(jnp.float32)
    d_0 = jnp.sum(cot * o_0, axis=1, keepdims=True)
    d_1 = jnp.sum(cot * o_1, axis=1, keepdims=True)
    lane = lax.broadcasted_iota(jnp.int32, (count, 8), 1)
    both = jnp.where(lane == 0, d_0, jnp.where(lane == 1, d_1, 0.0))
    d_gate_ref[...] = jnp.transpose(both, (1, 0))[0:2, :]


def params():
    return pltpu.CompilerParams(vmem_limit_bytes=VMEM_BYTES)


def chunk_of(hidden, want):
    return max(size for size in range(128, want + 1, 128) if hidden % size == 0)


def per_device(tokens, expert_ids, priority, gates, w_in, w_out, cotangent):
    count, width = tokens.shape
    repl = lax.axis_size("expert") // EXPERTS
    slots = EXPERTS * PAIR
    hidden = w_in.shape[2]
    ids_t = jnp.transpose(expert_ids, (1, 0))
    gates_t = jnp.transpose(gates, (1, 0))
    send = pl.pallas_call(
        dispatch_kernel,
        out_shape=jax.ShapeDtypeStruct((slots, width), jnp.bfloat16),
        compiler_params=params(),
        name="dispatch",
    )(ids_t, priority, gates_t, tokens, cotangent)
    pick, gate_cols = pl.pallas_call(
        tables_kernel,
        out_shape=(
            jax.ShapeDtypeStruct((3 * count, slots), jnp.bfloat16),
            jax.ShapeDtypeStruct((count, 8), jnp.float32),
        ),
        compiler_params=params(),
        name="tables",
    )(ids_t, priority, gates_t)
    send = jnp.tile(send.reshape(EXPERTS, PAIR, width), (repl, 1, 1))
    recv = lax.all_to_all(send, "expert", split_axis=0, concat_axis=0, tiled=True)
    rows = recv.shape[0] * PAIR
    recv = recv.reshape(rows, width)
    half = rows // 2
    chunk = chunk_of(hidden, 512)
    steps = hidden // chunk
    vmem = pl.BlockSpec(memory_space=pltpu.VMEM)
    hbm = pl.BlockSpec(memory_space=pl.ANY)
    low = jnp.bfloat16
    ret, x_rows, g_rows, act, d_pre = pl.pallas_call(
        functools.partial(forward_kernel, steps),
        out_shape=(
            jax.ShapeDtypeStruct((rows, width), low),
            jax.ShapeDtypeStruct((half, width), low),
            jax.ShapeDtypeStruct((half, width), low),
            jax.ShapeDtypeStruct((steps, half, chunk), low),
            jax.ShapeDtypeStruct((steps, half, chunk), low),
        ),
        in_specs=[vmem, hbm, hbm],
        out_specs=(vmem,) * 5,
        scratch_shapes=[
            pltpu.VMEM((steps, width, chunk), low),
            pltpu.VMEM((steps, chunk, width), low),
            pltpu.VMEM((half, width), jnp.float32),
            pltpu.VMEM((half, width), jnp.float32),
            pltpu.SemaphoreType.DMA((steps,)),
            pltpu.SemaphoreType.DMA((steps,)),
        ],
        compiler_params=params(),
        cost_estimate=pl.CostEstimate(
            flops=8 * half * width * hidden,
            bytes_accessed=4 * width * hidden,
            transcendentals=half * hidden,
        ),
        name="forward",
    )(recv, w_in[0], w_out[0])
    ret = lax.all_to_all(
        ret.reshape(rows // PAIR, PAIR, width), "expert", split_axis=0, concat_axis=0, tiled=True
    ).reshape(rows, width)
    whole = lambda i: (0, 0)
    d_w_in, d_w_out = pl.pallas_call(
        grads_kernel,
        grid=(steps,),
        out_shape=(
            jax.ShapeDtypeStruct((width, hidden), low),
            jax.ShapeDtypeStruct((hidden, width), low),
        ),
        in_specs=[
            pl.BlockSpec((half, width), whole),
            pl.BlockSpec((half, width), whole),
            pl.BlockSpec((1, half, chunk), lambda i: (i, 0, 0)),
            pl.BlockSpec((1, half, chunk), lambda i: (i, 0, 0)),
        ],
        out_specs=(
            pl.BlockSpec((width, chunk), lambda i: (0, i)),
            pl.BlockSpec((chunk, width), lambda i: (i, 0)),
        ),
        compiler_params=params(),
        cost_estimate=pl.CostEstimate(
            flops=4 * half * width * hidden,
            bytes_accessed=4 * width * hidden,
            transcendentals=0,
        ),
        name="grads",
    )(x_rows, g_rows, act, d_pre)
    mixed, d_tokens, d_gates_t = pl.pallas_call(
        combine_kernel,
        out_shape=(
            jax.ShapeDtypeStruct((count, width), low),
            jax.ShapeDtypeStruct((count, width), low),
            jax.ShapeDtypeStruct((2, count), jnp.float32),
        ),
        compiler_params=params(),
        name="combine",
    )(ret, pick, gate_cols, cotangent)
    return (mixed, d_tokens, jnp.transpose(d_gates_t, (1, 0)), d_w_in[None], d_w_out[None])


def solution(mesh):
    rows = P(("groups", "expert"), None)
    return jax.shard_map(
        per_device,
        mesh=mesh,
        in_specs=(rows, rows, rows, rows, P("expert", None, None), P("expert", None, None), rows),
        out_specs=(
            rows,
            rows,
            rows,
            P(("groups", "expert"), None, None),
            P(("groups", "expert"), None, None),
        ),
        check_vma=False,
    )
```

time: 108 us -> 75.7 us (0.70)
  matrix products: 59.1 us -> 0 us
  Pallas kernels: 0 us -> 49.9 us
  blocking collectives: 0 us -> 20.2 us
  starting transfers between devices: 22.5 us -> 3.7 us
  local copies, waits for them, and re-layouts: 8.86 us -> 0.75 us
  waiting for transfers between devices: 8 us -> 0.01 us
  other arithmetic: 7.79 us -> 0 us
    dot_general x8 -> x0, matrix products: 59.1 us -> none  [the longest x1 10.4 us: per_device(): lax.dot_general(g_flat, w_second, (((1,), (1,)), ((), ())), preferred_ele...]
    pallas_call x0 -> x5, Pallas kernels: none -> 49.9 us  [the longest x1 26.5 us: per_device(): pl.pallas_call(functools.partial(forward_kernel, steps), out_shape=(jax.S...]
    all_to_all x0 -> x1, blocking collectives: none -> 20.2 us  [per_device(): lax.all_to_all(send, 'expert', split_axis=0, concat_axis=0, tiled=True)]
    all_to_all x4 -> x1, starting transfers between devices: 22.5 us -> 3.7 us  [per_device(): lax.all_to_all(ret.reshape(rows // PAIR, PAIR, width), 'expert', split_ax...]
    all_to_all x4 -> x1, waiting for transfers between devices: 8 us -> 0.01 us  [per_device(): lax.all_to_all(ret.reshape(rows // PAIR, PAIR, width), 'expert', split_ax...]
    gather x2 -> x0, local copies, waits for them, and re-layouts: 4.03 us -> none  [the longest x1 2.58 us: per_device(): jnp.take(out_rows, index_of, axis=0)]
    select_n x2 -> x0, other arithmetic: 2.63 us -> none  [the longest x1 1.94 us: per_device(): jnp.where(kept, jnp.take(back_rows, index_of, axis=0), 0.0)]
    reshape x6 -> x0, local copies, waits for them, and re-layouts: 2.58 us -> none  [the longest x1 0.96 us: per_device(): back_rows = ret_back.reshape(repl, EXPERTS, CAP, width).astype(jnp.float3...]
  transfers between devices with their start and end apart: 4 -> 1, of which waited for: 2 -> 0; matrix products, arithmetic and copies ran while one was open for 40% -> 0% of each run, Pallas kernels for 0% -> 24%
where the time goes in v1:
time: 75.7 us; the launch traced here: 75.3 us
  Pallas kernels  49.9 us (66%)
  blocking collectives  20.2 us (27%)
  starting transfers between devices  3.7 us (5%)
    pallas_call x1, Pallas kernels, per_device(): pl.pallas_call(functools.partial(forward_kernel, steps), out_shape=(jax.S...  26.5 us
    all_to_all x1, blocking collectives, per_device(): lax.all_to_all(send, 'expert', split_axis=0, concat_axis=0, tiled=True)  20.2 us
    pallas_call x1, Pallas kernels, per_device(): pl.pallas_call(grads_kernel, grid=(steps,), out_shape=(jax.ShapeDtypeStru...  16.5 us
    all_to_all x1, starting transfers between devices, per_device(): lax.all_to_all(ret.reshape(rows // PAIR, PAIR, width), 'expert', split_ax...  3.7 us
    pallas_call x1, Pallas kernels, per_device(): pl.pallas_call(combine_kernel, out_shape=(jax.ShapeDtypeStruct((count, wi...  2.72 us
    pallas_call x1, Pallas kernels, per_device(): pl.pallas_call(dispatch_kernel, out_shape=jax.ShapeDtypeStruct((slots, wi...  2.46 us
    pallas_call x1, Pallas kernels, per_device(): pl.pallas_call(tables_kernel, out_shape=(jax.ShapeDtypeStruct((3 * count,...  1.74 us
  transfers between devices with their start and end apart: 1, of which 0 were waited for; matrix products, arithmetic and copies ran while one was open for 0% of the time, Pallas kernels for 24%

profile of v1, /device:TPU:0, one launch (start us, length us, event | category | flops | bytes accessed | tf_op | source)
XLA Modules:
  0.0 75.3 jit_solution(13910920972916986011)
XLA Ops:
  0.6 2.5 %dispatch.1 = bf16[128,1664]{1,0:T(8,128)(2,1)} custom-call(s32[2,128]{1,0:T(2,128)} %bitcast.17, s32[1,128]{1,0:T(1,128)} %prio_ref.3, f32[2,128]{1,0:T(2,128)} %bitcast.19, bf16[128,1664]{1,0:T(8,128)(2,1)} %tok_ref.1, bf16[128,1664]{1,0:T(8,128)(2,1)} %cot_ref.3), custom_call_target="tpu_custom_call" | custom-call | tf_op jit(solution)/shard_map/dispatch/pallas_call | solution.py:209
  3.1 20.2 %all_to_all.10 = bf16[16,8,1664]{2,1,0:T(8,128)(2,1)} all-to-all(bf16[16,8,1664]{2,1,0:T(8,128)(2,1)} %bitcast.14), channel_id=1, replica_groups=mesh['groups'=2,'expert'=16] {'expert'}, dimensions={0} | all-to-all | bytes 851968 | tf_op jit(solution)/shard_map/all_to_all | solution.py:225
  23.3 26.5 %forward.1 = (bf16[128,1664]{1,0:T(8,128)(2,1)}, bf16[64,1664]{1,0:T(8,128)(2,1)}, bf16[64,1664]{1,0:T(8,128)(2,1)}, bf16[12,64,512]{2,1,0:T(8,128)(2,1)}, bf16[12,64,512]{2,1,0:T(8,128)(2,1)}) custom-call(bf16[128,1664]{1,0:T(8,128)(2,1)} %bitcast.15, bf16[1664,6144]{1,0:T(8,128)(2,1)} %bitcast.11, bf16[6144,1664]{1,0:T(8,128)(2,1)} %bitcast.12), custom_call_target="tpu_custom_call" | custom-call | flops 5234491392 | bytes 40894464 | tf_op jit(solution)/shard_map/forward/pallas_call | solution.py:234
  49.8 3.7 %all-to-all-start.1 = ((bf16[16,8,1664]{2,1,0:T(8,128)(2,1)}), bf16[16,8,1664]{2,1,0:T(8,128)(2,1)S(1)}, u32[]{:S(2)}, u32[]{:S(2)}) async-start(bf16[16,8,1664]{2,1,0:T(8,128)(2,1)} %bitcast.16), calls=%async_computation.1 | async-start | bytes 851968 | tf_op jit(solution)/shard_map/all_to_all | solution.py:261
  53.5 1.7 %tables.1 = (bf16[384,128]{1,0:T(8,128)(2,1)}, f32[128,8]{1,0:T(8,128)}) custom-call(s32[2,128]{1,0:T(2,128)} %bitcast.18, s32[1,128]{1,0:T(1,128)} %prio_ref.3, f32[2,128]{1,0:T(2,128)} %bitcast.20), custom_call_target="tpu_custom_call" | custom-call | tf_op jit(solution)/shard_map/tables/pallas_call | solution.py:215
  55.3 16.5 %grads.1 = (bf16[1664,6144]{1,0:T(8,128)(2,1)}, bf16[6144,1664]{1,0:T(8,128)(2,1)}) custom-call(bf16[64,1664]{1,0:T(8,128)(2,1)} %get-tuple-element.23.x_ref, bf16[64,1664]{1,0:T(8,128)(2,1)} %get-tuple-element.24.g_ref, bf16[12,64,512]{2,1,0:T(8,128)(2,1)} %get-tuple-element.25.act_ref, bf16[12,64,512]{2,1,0:T(8,128)(2,1)} %get-tuple-element.26.d_pre_ref), custom_call_target="tpu_custom_call" | custom-call | flops 2617245696 | bytes 40894464 | tf_op jit(solution)/shard_map/grads/pallas_call | solution.py:265
  71.8 0.0 all-to-all-done.1
  71.8 0.0 copy-start
  71.8 0.8 copy-done
  72.5 2.7 %combine.1 = (bf16[128,1664]{1,0:T(8,128)(2,1)}, bf16[128,1664]{1,0:T(8,128)(2,1)}, f32[2,128]{1,0:T(2,128)}) custom-call(bf16[128,1664]{1,0:T(8,128)(2,1)} %bitcast.13, bf16[384,128]{1,0:T(8,128)(2,1)} %get-tuple-element.18.pick_ref, f32[128,8]{1,0:T(8,128)} %get-tuple-element.19.gate_ref, bf16[128,1664]{1,0:T(8,128)(2,1)} %cot_ref.3), custom_call_target="tpu_custom_call" | custom-call | tf_op jit(solution)/shard_map/combine/pallas_call | solution.py:290
Async XLA Ops:
  49.8 21.9 %all-to-all-start.1 = ((bf16[16,8,1664]{2,1,0:T(8,128)(2,1)}), bf16[16,8,1664]{2,1,0:T(8,128)(2,1)S(1)}, u32[]{:S(2)}, u32[]{:S(2)}) async-start(bf16[16,8,1664]{2,1,0:T(8,128)(2,1)} %bitcast.16), calls=%async_computation.1 | async-start | bytes 851968 | tf_op jit(solution)/shard_map/all_to_all | solution.py:261
  71.8 0.8 %copy-start = (bf16[16,8,1664]{2,1,0:T(8,128)(2,1)}, bf16[16,8,1664]{2,1,0:T(8,128)(2,1)S(1)}, u32[]{:S(2)}) copy-start(bf16[16,8,1664]{2,1,0:T(8,128)(2,1)S(1)} %all-to-all-done.1) | copy-start | bytes 1277956

commit v2 on v1

--- a/solution.py
+++ b/solution.py
@@ -48,13 +48,32 @@
     return place_0, place_1
 
 
-def dispatch_kernel(ids_ref, prio_ref, gates_ref, tok_ref, cot_ref, send_ref):
+def row_slots(count, pairwise):
+    row = lax.broadcasted_iota(jnp.int32, (EXPERTS * PAIR, count), 0)
+    block = row // PAIR
+    if pairwise:
+        block = block ^ lax.axis_index("expert")
+    return block * CAP + row % CAP, row % PAIR < CAP
+
+
+def joined(refs):
+    if len(refs) == 1:
+        return refs[0][...]
+    return jnp.concatenate([ref[...].astype(jnp.float32) for ref in refs], axis=0).astype(
+        jnp.bfloat16
+    )
+
+
+def store_blocks(refs, rows):
+    depth = refs[0].shape[0]
+    for block, ref in enumerate(refs):
+        ref[...] = rows[block * depth:(block + 1) * depth].astype(jnp.bfloat16)
+
+
+def dispatch_kernel(pairwise, ids_ref, prio_ref, gates_ref, tok_ref, cot_ref, *send_refs):
     place_0, place_1 = place_rows(ids_ref[...], prio_ref[...])
     count = tok_ref.shape[0]
-    rows = EXPERTS * PAIR
-    row = lax.broadcasted_iota(jnp.int32, (rows, count), 0)
-    slot = row // PAIR * CAP + row % CAP
-    is_x = row % PAIR < CAP
+    slot, is_x = row_slots(count, pairwise)
     hit_0 = slot == place_0
     hit_1 = slot == place_1
     hit = jnp.where(hit_0 | hit_1, 1.0, 0.0)
@@ -66,16 +85,13 @@
     scale = jnp.where(is_x[:, 0:1], 1.0, scale)
     both = jnp.concatenate([tok_ref[...], cot_ref[...]], axis=0)
     found = jnp.dot(pick, both, preferred_element_type=jnp.float32)
-    send_ref[...] = (found * scale).astype(jnp.bfloat16)
-
-
-def tables_kernel(ids_ref, prio_ref, gates_ref, pick_ref, gate_ref):
+    store_blocks(send_refs, found * scale)
+
+
+def tables(pairwise, ids_ref, prio_ref, gates_ref, pick_ref, gate_ref):
     place_0, place_1 = place_rows(ids_ref[...], prio_ref[...])
     count = place_0.shape[1]
-    rows = EXPERTS * PAIR
-    row = lax.broadcasted_iota(jnp.int32, (rows, count), 0)
-    slot = row // PAIR * CAP + row % CAP
-    is_x = row % PAIR < CAP
+    slot, is_x = row_slots(count, pairwise)
     hit_0 = jnp.where(slot == place_0, 1.0, 0.0)
     hit_1 = jnp.where(slot == place_1, 1.0, 0.0)
     pick_0 = jnp.transpose(jnp.where(is_x, hit_0, 0.0), (1, 0))
@@ -96,10 +112,12 @@
     return x_pick, g_pick
 
 
-def forward_kernel(
-    steps, recv_ref, w_in_hbm, w_out_hbm, ret_ref, x_ref, g_ref, act_ref, d_pre_ref,
-    w_in_ref, w_out_ref, out_acc, back_acc, sem_in, sem_out,
-):
+def forward_kernel(steps, blocks, pairwise, *refs):
+    recv_refs, refs = refs[:blocks], refs[blocks:]
+    ids_ref, prio_ref, gates_ref, w_in_hbm, w_out_hbm = refs[:5]
+    ret_refs, refs = refs[5:5 + blocks], refs[5 + blocks:]
+    x_t_ref, g_ref, act_ref, d_pre_ref, pick_ref, gate_ref = refs[:6]
+    w_in_ref, w_out_ref, x_ref, out_acc, back_acc, sem_in, sem_out = refs[6:]
     depth = w_in_ref.shape[2]
 
     def copies(step):
@@ -115,14 +133,13 @@
         return carry
 
     lax.fori_loop(0, steps, begin, 0)
-    rows = recv_ref.shape[0]
-    x_pick, g_pick = row_picks(rows)
-    x_ref[...] = jnp.dot(x_pick, recv_ref[...], preferred_element_type=jnp.float32).astype(
-        jnp.bfloat16
-    )
-    g_ref[...] = jnp.dot(g_pick, recv_ref[...], preferred_element_type=jnp.float32).astype(
-        jnp.bfloat16
-    )
+    recv = joined(recv_refs)
+    x_pick, g_pick = row_picks(recv.shape[0])
+    x_rows = jnp.dot(x_pick, recv, preferred_element_type=jnp.float32)
+    x_ref[...] = x_rows.astype(jnp.bfloat16)
+    x_t_ref[...] = jnp.transpose(x_rows, (1, 0)).astype(jnp.bfloat16)
+    g_ref[...] = jnp.dot(g_pick, recv, preferred_element_type=jnp.float32).astype(jnp.bfloat16)
+    tables(pairwise, ids_ref, prio_ref, gates_ref, pick_ref, gate_ref)
     out_acc[...] = jnp.zeros_like(out_acc)
     back_acc[...] = jnp.zeros_like(back_acc)
 
@@ -130,8 +147,11 @@
         for copy in copies(step):
             copy.wait()
         pre = jnp.dot(x_ref[...], w_in_ref[step], preferred_element_type=jnp.float32)
-        d_act = lax.dot_general(
-            g_ref[...], w_out_ref[step], LAST_DIM, preferred_element_type=jnp.float32
+        d_act = jnp.transpose(
+            lax.dot_general(
+                w_out_ref[step], g_ref[...], LAST_DIM, preferred_element_type=jnp.float32
+            ),
+            (1, 0),
         )
         value, slope = gelu_parts(pre)
         act_ref[step] = value.astype(jnp.bfloat16)
@@ -142,7 +162,7 @@
             act_ref[step], w_out_ref[step], preferred_element_type=jnp.float32
         )
         back_acc[...] += lax.dot_general(
-            d_pre_ref[step], w_in_ref[step], LAST_DIM, preferred_element_type=jnp.float32
+            w_in_ref[step], d_pre_ref[step], LAST_DIM, preferred_element_type=jnp.float32
         )
 
     front(0)
@@ -157,27 +177,29 @@
     ret = lax.dot_general(
         x_pick, out_acc[...].astype(jnp.bfloat16), ROWS_DIM, preferred_element_type=jnp.float32
     ) + lax.dot_general(
-        g_pick, back_acc[...].astype(jnp.bfloat16), ROWS_DIM, preferred_element_type=jnp.float32
-    )
-    ret_ref[...] = ret.astype(jnp.bfloat16)
-
-
-def grads_kernel(x_ref, g_ref, act_ref, d_pre_ref, d_in_ref, d_out_ref):
-    d_in_ref[...] = lax.dot_general(
-        x_ref[...], d_pre_ref[0], ROWS_DIM, preferred_element_type=jnp.float32
+        g_pick, jnp.transpose(back_acc[...], (1, 0)).astype(jnp.bfloat16), ROWS_DIM, preferred_element_type=jnp.float32
+    )
+    store_blocks(ret_refs, ret)
+
+
+def grads_kernel(x_t_ref, g_ref, act_ref, d_pre_ref, d_in_ref, d_out_ref):
+    d_in_ref[...] = jnp.dot(
+        x_t_ref[...], d_pre_ref[0], preferred_element_type=jnp.float32
     ).astype(jnp.bfloat16)
     d_out_ref[...] = lax.dot_general(
         act_ref[0], g_ref[...], ROWS_DIM, preferred_element_type=jnp.float32
     ).astype(jnp.bfloat16)
 
 
-def combine_kernel(ret_ref, pick_ref, gate_ref, cot_ref, mixed_ref, d_tok_ref, d_gate_ref):
+def combine_kernel(blocks, *refs):
+    pick_ref, gate_ref, cot_ref, mixed_ref, d_tok_ref, d_gate_ref = refs[blocks:]
     count = cot_ref.shape[0]
     rows = pick_ref.shape[1]
+    ret = joined(refs[:blocks])
     found = None
-    for first in range(0, ret_ref.shape[0], rows):
+    for first in range(0, ret.shape[0], rows):
         part = jnp.dot(
-            pick_ref[...], ret_ref[first:first + rows, :], preferred_element_type=jnp.float32
+            pick_ref[...], ret[first:first + rows, :], preferred_element_type=jnp.float32
         )
         found = part if found is None else found + part
     o_0, o_1 = found[:count], found[count:2 * count]
@@ -199,6 +221,20 @@
     return max(size for size in range(128, want + 1, 128) if hidden % size == 0)
 
 
+def exchange(parts):
+    if len(parts) > 1:
+        return [parts[0]] + [
+            lax.ppermute(part, "expert", [(i, i ^ k) for i in range(len(parts))])
+            for k, part in enumerate(parts)
+            if k
+        ]
+    rows, width = parts[0].shape
+    moved = lax.all_to_all(
+        parts[0].reshape(rows // PAIR, PAIR, width), "expert", split_axis=0, concat_axis=0, tiled=True
+    )
+    return [moved.reshape(rows, width)]
+
+
 def per_device(tokens, expert_ids, priority, gates, w_in, w_out, cotangent):
     count, width = tokens.shape
     repl = lax.axis_size("expert") // EXPERTS
@@ -206,47 +242,43 @@
     hidden = w_in.shape[2]
     ids_t = jnp.transpose(expert_ids, (1, 0))
     gates_t = jnp.transpose(gates, (1, 0))
+    pairwise = repl == 1
+    low = jnp.bfloat16
+    parts = EXPERTS if pairwise else 1
     send = pl.pallas_call(
-        dispatch_kernel,
-        out_shape=jax.ShapeDtypeStruct((slots, width), jnp.bfloat16),
+        functools.partial(dispatch_kernel, pairwise),
+        out_shape=(jax.ShapeDtypeStruct((slots // parts, width), low),) * parts,
         compiler_params=params(),
         name="dispatch",
     )(ids_t, priority, gates_t, tokens, cotangent)
-    pick, gate_cols = pl.pallas_call(
-        tables_kernel,
-        out_shape=(
-            jax.ShapeDtypeStruct((3 * count, slots), jnp.bfloat16),
-            jax.ShapeDtypeStruct((count, 8), jnp.float32),
-        ),
-        compiler_params=params(),
-        name="tables",
-    )(ids_t, priority, gates_t)
-    send = jnp.tile(send.reshape(EXPERTS, PAIR, width), (repl, 1, 1))
-    recv = lax.all_to_all(send, "expert", split_axis=0, concat_axis=0, tiled=True)
-    rows = recv.shape[0] * PAIR
-    recv = recv.reshape(rows, width)
+    if not pairwise:
+        send = (jnp.tile(send[0], (repl, 1)),)
+    recv = exchange(send)
+    rows = slots * repl
     half = rows // 2
     chunk = chunk_of(hidden, 512)
     steps = hidden // chunk
     vmem = pl.BlockSpec(memory_space=pltpu.VMEM)
     hbm = pl.BlockSpec(memory_space=pl.ANY)
-    low = jnp.bfloat16
-    ret, x_rows, g_rows, act, d_pre = pl.pallas_call(
-        functools.partial(forward_kernel, steps),
-        out_shape=(
-            jax.ShapeDtypeStruct((rows, width), low),
-            jax.ShapeDtypeStruct((half, width), low),
+    *ret, x_t, g_rows, act, d_pre, pick, gate_cols = pl.pallas_call(
+        functools.partial(forward_kernel, steps, parts, pairwise),
+        out_shape=(jax.ShapeDtypeStruct((rows // parts, width), low),) * parts
+        + (
+            jax.ShapeDtypeStruct((width, half), low),
             jax.ShapeDtypeStruct((half, width), low),
             jax.ShapeDtypeStruct((steps, half, chunk), low),
             jax.ShapeDtypeStruct((steps, half, chunk), low),
-        ),
-        in_specs=[vmem, hbm, hbm],
-        out_specs=(vmem,) * 5,
+            jax.ShapeDtypeStruct((3 * count, slots), low),
+            jax.ShapeDtypeStruct((count, 8), jnp.float32),
+        ),
+        in_specs=[vmem] * (parts + 3) + [hbm, hbm],
+        out_specs=(vmem,) * (parts + 6),
         scratch_shapes=[
             pltpu.VMEM((steps, width, chunk), low),
             pltpu.VMEM((steps, chunk, width), low),
+            pltpu.VMEM((half, width), low),
             pltpu.VMEM((half, width), jnp.float32),
-            pltpu.VMEM((half, width), jnp.float32),
+            pltpu.VMEM((width, half), jnp.float32),
             pltpu.SemaphoreType.DMA((steps,)),
             pltpu.SemaphoreType.DMA((steps,)),
         ],
@@ -257,10 +289,8 @@
             transcendentals=half * hidden,
         ),
         name="forward",
-    )(recv, w_in[0], w_out[0])
-    ret = lax.all_to_all(
-        ret.reshape(rows // PAIR, PAIR, width), "expert", split_axis=0, concat_axis=0, tiled=True
-    ).reshape(rows, width)
+    )(*recv, ids_t, priority, gates_t, w_in[0], w_out[0])
+    ret = exchange(ret)
     whole = lambda i: (0, 0)
     d_w_in, d_w_out = pl.pallas_call(
         grads_kernel,
@@ -270,7 +300,7 @@
             jax.ShapeDtypeStruct((hidden, width), low),
         ),
         in_specs=[
-            pl.BlockSpec((half, width), whole),
+            pl.BlockSpec((width, half), whole),
             pl.BlockSpec((half, width), whole),
             pl.BlockSpec((1, half, chunk), lambda i: (i, 0, 0)),
             pl.BlockSpec((1, half, chunk), lambda i: (i, 0, 0)),
@@ -286,9 +316,9 @@
             transcendentals=0,
         ),
         name="grads",
-    )(x_rows, g_rows, act, d_pre)
+    )(x_t, g_rows, act, d_pre)
     mixed, d_tokens, d_gates_t = pl.pallas_call(
-        combine_kernel,
+        functools.partial(combine_kernel, parts),
         out_shape=(
             jax.ShapeDtypeStruct((count, width), low),
             jax.ShapeDtypeStruct((count, width), low),
@@ -296,7 +326,7 @@
         ),
         compiler_params=params(),
         name="combine",
-    )(ret, pick, gate_cols, cotangent)
+    )(*ret, pick, gate_cols, cotangent)
     return (mixed, d_tokens, jnp.transpose(d_gates_t, (1, 0)), d_w_in[None], d_w_out[None])
 
 

time: 75.7 us -> 106 us (1.40)
  starting transfers between devices: 3.7 us -> 43.8 us
  blocking collectives: 20.2 us -> 0 us
  Pallas kernels: 49.9 us -> 55.4 us
  waiting for transfers between devices: 0.01 us -> 4.56 us
    ppermute x0 -> x30, starting transfers between devices: none -> 43.8 us  [exchange(): lax.ppermute(part, 'expert', [(i, i ^ k) for i in range(len(parts))])]
    all_to_all x1 -> x0, blocking collectives: 20.2 us -> none  [per_device(): lax.all_to_all(send, 'expert', split_axis=0, concat_axis=0, tiled=True)]
    pallas_call x4 -> x3, Pallas kernels: 33.4 us -> 39.2 us  [the longest x1 33.9 us: per_device(): pl.pallas_call(functools.partial(forward_kernel, steps, parts, pairwise),...]
    ppermute x0 -> x30, waiting for transfers between devices: none -> 4.56 us  [exchange(): lax.ppermute(part, 'expert', [(i, i ^ k) for i in range(len(parts))])]
    all_to_all x1 -> x0, starting transfers between devices: 3.7 us -> none  [per_device(): lax.all_to_all(ret.reshape(rows // PAIR, PAIR, width), 'expert', split_ax...]
  transfers between devices with their start and end apart: 1 -> 30, of which waited for: 0 -> 4; matrix products, arithmetic and copies ran while one was open for 0% -> 0% of each run, Pallas kernels for 24% -> 15%
where the time goes in v2:
time: 106 us
  Pallas kernels  55.4 us (52%)
  starting transfers between devices  43.8 us (41%)
  waiting for transfers between devices  4.56 us (4%)
  local copies, waits for them, and re-layouts  1.07 us (1%)
    ppermute x30, starting transfers between devices, exchange(): lax.ppermute(part, 'expert', [(i, i ^ k) for i in range(len(parts))])  43.8 us
    pallas_call x1, Pallas kernels, per_device(): pl.pallas_call(functools.partial(forward_kernel, steps, parts, pairwise),...  33.9 us
    pallas_call x1, Pallas kernels, per_device(): pl.pallas_call(grads_kernel, grid=(steps,), out_shape=(jax.ShapeDtypeStru...  16.2 us
    ppermute x30, waiting for transfers between devices, exchange(): lax.ppermute(part, 'expert', [(i, i ^ k) for i in range(len(parts))])  4.56 us
    pallas_call x1, Pallas kernels, per_device(): pl.pallas_call(functools.partial(combine_kernel, parts), out_shape=(jax.S...  2.85 us
    pallas_call x1, Pallas kernels, per_device(): pl.pallas_call(functools.partial(dispatch_kernel, pairwise), out_shape=(j...  2.44 us
  transfers between devices with their start and end apart: 30, of which 4 were waited for; matrix products, arithmetic and copies ran while one was open for 0% of the time, Pallas kernels for 15%

profile of v2, /device:TPU:0, one launch (start us, length us, event | category | flops | bytes accessed | tf_op | source)
XLA Modules:
  0.0 105.7 jit_solution(1895448523217203907)
XLA Ops:
  0.6 2.4 %dispatch.1 = (bf16[8,1664]{1,0:T(8,128)(2,1)}, bf16[8,1664]{1,0:T(8,128)(2,1)}, bf16[8,1664]{1,0:T(8,128)(2,1)}, bf16[8,1664]{1,0:T(8,128)(2,1)}, bf16[8,1664]{...) custom-call(s32[2,128]{1,0:T(2,128)} %bitcast.9, ...), custom_call_target="tpu_custom_call" | custom-call | tf_op jit(solution)/shard_map/dispatch/pallas_call | solution.py:248
  3.6 2.6 %collective-permute-start.1 = (bf16[8,1664]{1,0:T(8,128)(2,1)}, bf16[8,1664]{1,0:T(8,128)(2,1)S(1)}, u32[]{:S(2)}, u32[]{:S(2)}) collective-permute-start(bf16[8,1664]{1,0:T(8,128)(2,1)} %get-tuple-element.50), channel_id=1, source_target_pairs={{0,2},{1,3},{2,0},{3,1},{4,6},{5,7},{6,4},{7,5},{8,10},{9,11},{10,... | collective-permute-start | bytes 79880 | tf_op jit(solution)/shard_map/ppermute | solution.py:227
  6.2 2.3 %collective-permute-start.10 = (bf16[8,1664]{1,0:T(8,128)(2,1)}, bf16[8,1664]{1,0:T(8,128)(2,1)S(1)}, u32[]{:S(2)}, u32[]{:S(2)}) collective-permute-start(bf16[8,1664]{1,0:T(8,128)(2,1)} %get-tuple-element.59), channel_id=1, source_target_pairs={{0,11},{1,10},{2,9},{3,8},{4,15},{5,14},{6,13},{7,12},{8,3},{9,2},... | collective-permute-start | bytes 79880 | tf_op jit(solution)/shard_map/ppermute | solution.py:227
  8.5 1.3 %collective-permute-start.11 = (bf16[8,1664]{1,0:T(8,128)(2,1)}, bf16[8,1664]{1,0:T(8,128)(2,1)S(1)}, u32[]{:S(2)}, u32[]{:S(2)}) collective-permute-start(bf16[8,1664]{1,0:T(8,128)(2,1)} %get-tuple-element.60), channel_id=1, source_target_pairs={{0,12},{1,13},{2,14},{3,15},{4,8},{5,9},{6,10},{7,11},{8,4},{9,5},... | collective-permute-start | bytes 79880 | tf_op jit(solution)/shard_map/ppermute | solution.py:227
  9.8 2.1 %collective-permute-start.12 = (bf16[8,1664]{1,0:T(8,128)(2,1)}, bf16[8,1664]{1,0:T(8,128)(2,1)S(1)}, u32[]{:S(2)}, u32[]{:S(2)}) collective-permute-start(bf16[8,1664]{1,0:T(8,128)(2,1)} %get-tuple-element.61), channel_id=1, source_target_pairs={{0,13},{1,12},{2,15},{3,14},{4,9},{5,8},{6,11},{7,10},{8,5},{9,4},... | collective-permute-start | bytes 79880 | tf_op jit(solution)/shard_map/ppermute | solution.py:227
  12.0 2.3 %collective-permute-start.13 = (bf16[8,1664]{1,0:T(8,128)(2,1)}, bf16[8,1664]{1,0:T(8,128)(2,1)S(1)}, u32[]{:S(2)}, u32[]{:S(2)}) collective-permute-start(bf16[8,1664]{1,0:T(8,128)(2,1)} %get-tuple-element.62), channel_id=1, source_target_pairs={{0,14},{1,15},{2,12},{3,13},{4,10},{5,11},{6,8},{7,9},{8,6},{9,7},... | collective-permute-start | bytes 79880 | tf_op jit(solution)/shard_map/ppermute | solution.py:227
  14.3 2.2 %collective-permute-start.14 = (bf16[8,1664]{1,0:T(8,128)(2,1)}, bf16[8,1664]{1,0:T(8,128)(2,1)S(1)}, u32[]{:S(2)}, u32[]{:S(2)}) collective-permute-start(bf16[8,1664]{1,0:T(8,128)(2,1)} %get-tuple-element.63), channel_id=1, source_target_pairs={{0,15},{1,14},{2,13},{3,12},{4,11},{5,10},{6,9},{7,8},{8,7},{9,6},... | collective-permute-start | bytes 79880 | tf_op jit(solution)/shard_map/ppermute | solution.py:227
  16.5 1.5 %collective-permute-start.2 = (bf16[8,1664]{1,0:T(8,128)(2,1)}, bf16[8,1664]{1,0:T(8,128)(2,1)S(1)}, u32[]{:S(2)}, u32[]{:S(2)}) collective-permute-start(bf16[8,1664]{1,0:T(8,128)(2,1)} %get-tuple-element.51), channel_id=1, source_target_pairs={{0,3},{1,2},{2,1},{3,0},{4,7},{5,6},{6,5},{7,4},{8,11},{9,10},{10,... | collective-permute-start | bytes 79880 | tf_op jit(solution)/shard_map/ppermute | solution.py:227
  18.0 1.5 %collective-permute-start.4 = (bf16[8,1664]{1,0:T(8,128)(2,1)}, bf16[8,1664]{1,0:T(8,128)(2,1)S(1)}, u32[]{:S(2)}, u32[]{:S(2)}) collective-permute-start(bf16[8,1664]{1,0:T(8,128)(2,1)} %get-tuple-element.53), channel_id=1, source_target_pairs={{0,5},{1,4},{2,7},{3,6},{4,1},{5,0},{6,3},{7,2},{8,13},{9,12},{10,... | collective-permute-start | bytes 79880 | tf_op jit(solution)/shard_map/ppermute | solution.py:227
  20.5 1.9 %collective-permute-start.6 = (bf16[8,1664]{1,0:T(8,128)(2,1)}, bf16[8,1664]{1,0:T(8,128)(2,1)S(1)}, u32[]{:S(2)}, u32[]{:S(2)}) collective-permute-start(bf16[8,1664]{1,0:T(8,128)(2,1)} %get-tuple-element.55), channel_id=1, source_target_pairs={{0,7},{1,6},{2,5},{3,4},{4,3},{5,2},{6,1},{7,0},{8,15},{9,14},{10,... | collective-permute-start | bytes 79880 | tf_op jit(solution)/shard_map/ppermute | solution.py:227
  23.3 1.5 %collective-permute-start.8 = (bf16[8,1664]{1,0:T(8,128)(2,1)}, bf16[8,1664]{1,0:T(8,128)(2,1)S(1)}, u32[]{:S(2)}, u32[]{:S(2)}) collective-permute-start(bf16[8,1664]{1,0:T(8,128)(2,1)} %get-tuple-element.57), channel_id=1, source_target_pairs={{0,9},{1,8},{2,11},{3,10},{4,13},{5,12},{6,15},{7,14},{8,1},{9,0},... | collective-permute-start | bytes 79880 | tf_op jit(solution)/shard_map/ppermute | solution.py:227
  24.8 2.1 %collective-permute-start.9 = (bf16[8,1664]{1,0:T(8,128)(2,1)}, bf16[8,1664]{1,0:T(8,128)(2,1)S(1)}, u32[]{:S(2)}, u32[]{:S(2)}) collective-permute-start(bf16[8,1664]{1,0:T(8,128)(2,1)} %get-tuple-element.58), channel_id=1, source_target_pairs={{0,10},{1,11},{2,8},{3,9},{4,14},{5,15},{6,12},{7,13},{8,2},{9,3},... | collective-permute-start | bytes 79880 | tf_op jit(solution)/shard_map/ppermute | solution.py:227
  27.7 3.2 %collective-permute-done.9.refs_10_ = bf16[8,1664]{1,0:T(8,128)(2,1)S(1)} collective-permute-done((bf16[8,1664]{1,0:T(8,128)(2,1)}, bf16[8,1664]{1,0:T(8,128)(2,1)S(1)}, u32[]{:S(2)}, u32[]{:S(2)}) %collective-permute-start.9) | collective-permute-done | bytes 26656 | tf_op jit(solution)/shard_map/ppermute | solution.py:227
  31.6 33.9 %forward.1 = (bf16[8,1664]{1,0:T(8,128)(2,1)}, bf16[8,1664]{1,0:T(8,128)(2,1)}, bf16[8,1664]{1,0:T(8,128)(2,1)}, bf16[8,1664]{1,0:T(8,128)(2,1)}, bf16[8,1664]{1...) custom-call(bf16[8,1664]{1,0:T(8,128)(2,1)} %get-tuple-element.48.re, ...), custom_call_target="tpu_custom_call" | custom-call | flops 5234491392 | bytes 40894464 | tf_op jit(solution)/shard_map/forward/pallas_call | solution.py:263
  70.0 1.8 %collective-permute-start.21 = (bf16[8,1664]{1,0:T(8,128)(2,1)}, bf16[8,1664]{1,0:T(8,128)(2,1)S(1)}, u32[]{:S(2)}, u32[]{:S(2)}) collective-permute-start(bf16[8,1664]{1,0:T(8,128)(2,1)} %get-tuple-element.71), channel_id=1, source_target_pairs={{0,7},{1,6},{2,5},{3,4},{4,3},{5,2},{6,1},{7,0},{8,15},{9,14},{10,... | collective-permute-start | bytes 79880 | tf_op jit(solution)/shard_map/ppermute | solution.py:227
  72.7 1.7 %collective-permute-start.23 = (bf16[8,1664]{1,0:T(8,128)(2,1)}, bf16[8,1664]{1,0:T(8,128)(2,1)S(1)}, u32[]{:S(2)}, u32[]{:S(2)}) collective-permute-start(bf16[8,1664]{1,0:T(8,128)(2,1)} %get-tuple-element.73), channel_id=1, source_target_pairs={{0,9},{1,8},{2,11},{3,10},{4,13},{5,12},{6,15},{7,14},{8,1},{9,0},... | collective-permute-start | bytes 79880 | tf_op jit(solution)/shard_map/ppermute | solution.py:227
  74.4 1.8 %collective-permute-start.24 = (bf16[8,1664]{1,0:T(8,128)(2,1)}, bf16[8,1664]{1,0:T(8,128)(2,1)S(1)}, u32[]{:S(2)}, u32[]{:S(2)}) collective-permute-start(bf16[8,1664]{1,0:T(8,128)(2,1)} %get-tuple-element.74), channel_id=1, source_target_pairs={{0,10},{1,11},{2,8},{3,9},{4,14},{5,15},{6,12},{7,13},{8,2},{9,3},... | collective-permute-start | bytes 79880 | tf_op jit(solution)/shard_map/ppermute | solution.py:227
  76.2 1.8 %collective-permute-start.25 = (bf16[8,1664]{1,0:T(8,128)(2,1)}, bf16[8,1664]{1,0:T(8,128)(2,1)S(1)}, u32[]{:S(2)}, u32[]{:S(2)}) collective-permute-start(bf16[8,1664]{1,0:T(8,128)(2,1)} %get-tuple-element.75), channel_id=1, source_target_pairs={{0,11},{1,10},{2,9},{3,8},{4,15},{5,14},{6,13},{7,12},{8,3},{9,2},... | collective-permute-start | bytes 79880 | tf_op jit(solution)/shard_map/ppermute | solution.py:227
  78.0 1.3 %collective-permute-start.26 = (bf16[8,1664]{1,0:T(8,128)(2,1)}, bf16[8,1664]{1,0:T(8,128)(2,1)S(1)}, u32[]{:S(2)}, u32[]{:S(2)}) collective-permute-start(bf16[8,1664]{1,0:T(8,128)(2,1)} %get-tuple-element.76), channel_id=1, source_target_pairs={{0,12},{1,13},{2,14},{3,15},{4,8},{5,9},{6,10},{7,11},{8,4},{9,5},... | collective-permute-start | bytes 79880 | tf_op jit(solution)/shard_map/ppermute | solution.py:227
  79.4 2.1 %collective-permute-start.27 = (bf16[8,1664]{1,0:T(8,128)(2,1)}, bf16[8,1664]{1,0:T(8,128)(2,1)S(1)}, u32[]{:S(2)}, u32[]{:S(2)}) collective-permute-start(bf16[8,1664]{1,0:T(8,128)(2,1)} %get-tuple-element.77), channel_id=1, source_target_pairs={{0,13},{1,12},{2,15},{3,14},{4,9},{5,8},{6,11},{7,10},{8,5},{9,4},... | collective-permute-start | bytes 79880 | tf_op jit(solution)/shard_map/ppermute | solution.py:227
  81.5 1.7 %collective-permute-start.28 = (bf16[8,1664]{1,0:T(8,128)(2,1)}, bf16[8,1664]{1,0:T(8,128)(2,1)S(1)}, u32[]{:S(2)}, u32[]{:S(2)}) collective-permute-start(bf16[8,1664]{1,0:T(8,128)(2,1)} %get-tuple-element.78), channel_id=1, source_target_pairs={{0,14},{1,15},{2,12},{3,13},{4,10},{5,11},{6,8},{7,9},{8,6},{9,7},... | collective-permute-start | bytes 79880 | tf_op jit(solution)/shard_map/ppermute | solution.py:227
  83.2 2.8 %collective-permute-start.29 = (bf16[8,1664]{1,0:T(8,128)(2,1)}, bf16[8,1664]{1,0:T(8,128)(2,1)S(1)}, u32[]{:S(2)}, u32[]{:S(2)}) collective-permute-start(bf16[8,1664]{1,0:T(8,128)(2,1)} %get-tuple-element.79), channel_id=1, source_target_pairs={{0,15},{1,14},{2,13},{3,12},{4,11},{5,10},{6,9},{7,8},{8,7},{9,6},... | collective-permute-start | bytes 79880 | tf_op jit(solution)/shard_map/ppermute | solution.py:227
  86.0 16.2 %grads.1 = (bf16[1664,6144]{1,0:T(8,128)(2,1)}, bf16[6144,1664]{1,0:T(8,128)(2,1)}) custom-call(bf16[1664,64]{1,0:T(8,128)(2,1)} %get-tuple-element.85.x_t_ref, bf16[64,1664]{1,0:T(8,128)(2,1)} %get-tuple-element.86.g_ref, bf16[12,64,512]{2,1,0:T(8,128)(2,1)} %get-tuple-element.87.act_ref, bf16[12,64,512]{2,1,0:T(8,128)(2,1)} %get-tuple-element.88.d_pre_ref), custom_call_target="tpu_custom_call" | custom-call | flops 2617245696 | bytes 40894464 | tf_op jit(solution)/shard_map/grads/pallas_call | solution.py:295
  102.9 2.9 %combine.1 = (bf16[128,1664]{1,0:T(8,128)(2,1)}, bf16[128,1664]{1,0:T(8,128)(2,1)}, f32[2,128]{1,0:T(2,128)}) custom-call(bf16[8,1664]{1,0:T(8,128)(2,1)} %get-tuple-element.64.refs_0_, bf16[8,1664]{1,0:T(8,128)(2,1)} %copy-done.15, bf16[8,1664]{1,0:T(8,128)(2,1)} %copy-done.16, bf16[8,1664]{1,0:T(8,128)(2,1)} %copy-done.17, bf16[8,1664]{1,0:T(8,128)(2,1)} %copy-done.18, ...), custom_call_target="tpu_custom_call" | custom-call | tf_op jit(solution)/shard_map/combine/pallas_call | solution.py:320
  (100 shorter events, 9.8 us)
Async XLA Ops:
  3.1 8.9 %collective-permute-start = (bf16[8,1664]{1,0:T(8,128)(2,1)}, bf16[8,1664]{1,0:T(8,128)(2,1)S(1)}, u32[]{:S(2)}, u32[]{:S(2)}) collective-permute-start(bf16[8,1664]{1,0:T(8,128)(2,1)} %get-tuple-element.49), channel_id=1, source_target_pairs={{0,1},{1,0},{2,3},{3,2},{4,5},{5,4},{6,7},{7,6},{8,9},{9,8},{10,11... | collective-permute-start | bytes 79880 | tf_op jit(solution)/shard_map/ppermute | solution.py:227
  3.6 10.7 %collective-permute-start.1 = (bf16[8,1664]{1,0:T(8,128)(2,1)}, bf16[8,1664]{1,0:T(8,128)(2,1)S(1)}, u32[]{:S(2)}, u32[]{:S(2)}) collective-permute-start(bf16[8,1664]{1,0:T(8,128)(2,1)} %get-tuple-element.50), channel_id=1, source_target_pairs={{0,2},{1,3},{2,0},{3,1},{4,6},{5,7},{6,4},{7,5},{8,10},{9,11},{10,... | collective-permute-start | bytes 79880 | tf_op jit(solution)/shard_map/ppermute | solution.py:227
  6.2 10.3 %collective-permute-start.10 = (bf16[8,1664]{1,0:T(8,128)(2,1)}, bf16[8,1664]{1,0:T(8,128)(2,1)S(1)}, u32[]{:S(2)}, u32[]{:S(2)}) collective-permute-start(bf16[8,1664]{1,0:T(8,128)(2,1)} %get-tuple-element.59), channel_id=1, source_target_pairs={{0,11},{1,10},{2,9},{3,8},{4,15},{5,14},{6,13},{7,12},{8,3},{9,2},... | collective-permute-start | bytes 79880 | tf_op jit(solution)/shard_map/ppermute | solution.py:227
  8.5 9.5 %collective-permute-start.11 = (bf16[8,1664]{1,0:T(8,128)(2,1)}, bf16[8,1664]{1,0:T(8,128)(2,1)S(1)}, u32[]{:S(2)}, u32[]{:S(2)}) collective-permute-start(bf16[8,1664]{1,0:T(8,128)(2,1)} %get-tuple-element.60), channel_id=1, source_target_pairs={{0,12},{1,13},{2,14},{3,15},{4,8},{5,9},{6,10},{7,11},{8,4},{9,5},... | collective-permute-start | bytes 79880 | tf_op jit(solution)/shard_map/ppermute | solution.py:227
  9.8 8.1 %collective-permute-start.12 = (bf16[8,1664]{1,0:T(8,128)(2,1)}, bf16[8,1664]{1,0:T(8,128)(2,1)S(1)}, u32[]{:S(2)}, u32[]{:S(2)}) collective-permute-start(bf16[8,1664]{1,0:T(8,128)(2,1)} %get-tuple-element.61), channel_id=1, source_target_pairs={{0,13},{1,12},{2,15},{3,14},{4,9},{5,8},{6,11},{7,10},{8,5},{9,4},... | collective-permute-start | bytes 79880 | tf_op jit(solution)/shard_map/ppermute | solution.py:227
  12.0 7.5 %collective-permute-start.13 = (bf16[8,1664]{1,0:T(8,128)(2,1)}, bf16[8,1664]{1,0:T(8,128)(2,1)S(1)}, u32[]{:S(2)}, u32[]{:S(2)}) collective-permute-start(bf16[8,1664]{1,0:T(8,128)(2,1)} %get-tuple-element.62), channel_id=1, source_target_pairs={{0,14},{1,15},{2,12},{3,13},{4,10},{5,11},{6,8},{7,9},{8,6},{9,7},... | collective-permute-start | bytes 79880 | tf_op jit(solution)/shard_map/ppermute | solution.py:227
  14.3 6.2 %collective-permute-start.14 = (bf16[8,1664]{1,0:T(8,128)(2,1)}, bf16[8,1664]{1,0:T(8,128)(2,1)S(1)}, u32[]{:S(2)}, u32[]{:S(2)}) collective-permute-start(bf16[8,1664]{1,0:T(8,128)(2,1)} %get-tuple-element.63), channel_id=1, source_target_pairs={{0,15},{1,14},{2,13},{3,12},{4,11},{5,10},{6,9},{7,8},{8,7},{9,6},... | collective-permute-start | bytes 79880 | tf_op jit(solution)/shard_map/ppermute | solution.py:227
  16.5 5.9 %collective-permute-start.2 = (bf16[8,1664]{1,0:T(8,128)(2,1)}, bf16[8,1664]{1,0:T(8,128)(2,1)S(1)}, u32[]{:S(2)}, u32[]{:S(2)}) collective-permute-start(bf16[8,1664]{1,0:T(8,128)(2,1)} %get-tuple-element.51), channel_id=1, source_target_pairs={{0,3},{1,2},{2,1},{3,0},{4,7},{5,6},{6,5},{7,4},{8,11},{9,10},{10,... | collective-permute-start | bytes 79880 | tf_op jit(solution)/shard_map/ppermute | solution.py:227
  18.0 5.4 %collective-permute-start.3 = (bf16[8,1664]{1,0:T(8,128)(2,1)}, bf16[8,1664]{1,0:T(8,128)(2,1)S(1)}, u32[]{:S(2)}, u32[]{:S(2)}) collective-permute-start(bf16[8,1664]{1,0:T(8,128)(2,1)} %get-tuple-element.52), channel_id=1, source_target_pairs={{0,4},{1,5},{2,6},{3,7},{4,0},{5,1},{6,2},{7,3},{8,12},{9,13},{10,... | collective-permute-start | bytes 79880 | tf_op jit(solution)/shard_map/ppermute | solution.py:227
  18.0 6.8 %collective-permute-start.4 = (bf16[8,1664]{1,0:T(8,128)(2,1)}, bf16[8,1664]{1,0:T(8,128)(2,1)S(1)}, u32[]{:S(2)}, u32[]{:S(2)}) collective-permute-start(bf16[8,1664]{1,0:T(8,128)(2,1)} %get-tuple-element.53), channel_id=1, source_target_pairs={{0,5},{1,4},{2,7},{3,6},{4,1},{5,0},{6,3},{7,2},{8,13},{9,12},{10,... | collective-permute-start | bytes 79880 | tf_op jit(solution)/shard_map/ppermute | solution.py:227
  19.5 7.4 %collective-permute-start.5 = (bf16[8,1664]{1,0:T(8,128)(2,1)}, bf16[8,1664]{1,0:T(8,128)(2,1)S(1)}, u32[]{:S(2)}, u32[]{:S(2)}) collective-permute-start(bf16[8,1664]{1,0:T(8,128)(2,1)} %get-tuple-element.54), channel_id=1, source_target_pairs={{0,6},{1,7},{2,4},{3,5},{4,2},{5,3},{6,0},{7,1},{8,14},{9,15},{10,... | collective-permute-start | bytes 79880 | tf_op jit(solution)/shard_map/ppermute | solution.py:227
  20.5 6.4 %collective-permute-start.6 = (bf16[8,1664]{1,0:T(8,128)(2,1)}, bf16[8,1664]{1,0:T(8,128)(2,1)S(1)}, u32[]{:S(2)}, u32[]{:S(2)}) collective-permute-start(bf16[8,1664]{1,0:T(8,128)(2,1)} %get-tuple-element.55), channel_id=1, source_target_pairs={{0,7},{1,6},{2,5},{3,4},{4,3},{5,2},{6,1},{7,0},{8,15},{9,14},{10,... | collective-permute-start | bytes 79880 | tf_op jit(solution)/shard_map/ppermute | solution.py:227
  24.8 6.1 %collective-permute-start.9 = (bf16[8,1664]{1,0:T(8,128)(2,1)}, bf16[8,1664]{1,0:T(8,128)(2,1)S(1)}, u32[]{:S(2)}, u32[]{:S(2)}) collective-permute-start(bf16[8,1664]{1,0:T(8,128)(2,1)} %get-tuple-element.58), channel_id=1, source_target_pairs={{0,10},{1,11},{2,8},{3,9},{4,14},{5,15},{6,12},{7,13},{8,2},{9,3},... | collective-permute-start | bytes 79880 | tf_op jit(solution)/shard_map/ppermute | solution.py:227
  67.8 6.6 %collective-permute-start.19 = (bf16[8,1664]{1,0:T(8,128)(2,1)}, bf16[8,1664]{1,0:T(8,128)(2,1)S(1)}, u32[]{:S(2)}, u32[]{:S(2)}) collective-permute-start(bf16[8,1664]{1,0:T(8,128)(2,1)} %get-tuple-element.69), channel_id=1, source_target_pairs={{0,5},{1,4},{2,7},{3,6},{4,1},{5,0},{6,3},{7,2},{8,13},{9,12},{10,... | collective-permute-start | bytes 79880 | tf_op jit(solution)/shard_map/ppermute | solution.py:227
  69.1 7.1 %collective-permute-start.20 = (bf16[8,1664]{1,0:T(8,128)(2,1)}, bf16[8,1664]{1,0:T(8,128)(2,1)S(1)}, u32[]{:S(2)}, u32[]{:S(2)}) collective-permute-start(bf16[8,1664]{1,0:T(8,128)(2,1)} %get-tuple-element.70), channel_id=1, source_target_pairs={{0,6},{1,7},{2,4},{3,5},{4,2},{5,3},{6,0},{7,1},{8,14},{9,15},{10,... | collective-permute-start | bytes 79880 | tf_op jit(solution)/shard_map/ppermute | solution.py:227
  70.0 8.0 %collective-permute-start.21 = (bf16[8,1664]{1,0:T(8,128)(2,1)}, bf16[8,1664]{1,0:T(8,128)(2,1)S(1)}, u32[]{:S(2)}, u32[]{:S(2)}) collective-permute-start(bf16[8,1664]{1,0:T(8,128)(2,1)} %get-tuple-element.71), channel_id=1, source_target_pairs={{0,7},{1,6},{2,5},{3,4},{4,3},{5,2},{6,1},{7,0},{8,15},{9,14},{10,... | collective-permute-start | bytes 79880 | tf_op jit(solution)/shard_map/ppermute | solution.py:227
  71.8 7.6 %collective-permute-start.22 = (bf16[8,1664]{1,0:T(8,128)(2,1)}, bf16[8,1664]{1,0:T(8,128)(2,1)S(1)}, u32[]{:S(2)}, u32[]{:S(2)}) collective-permute-start(bf16[8,1664]{1,0:T(8,128)(2,1)} %get-tuple-element.72), channel_id=1, source_target_pairs={{0,8},{1,9},{2,10},{3,11},{4,12},{5,13},{6,14},{7,15},{8,0},{9,1},... | collective-permute-start | bytes 79880 | tf_op jit(solution)/shard_map/ppermute | solution.py:227
  72.7 8.9 %collective-permute-start.23 = (bf16[8,1664]{1,0:T(8,128)(2,1)}, bf16[8,1664]{1,0:T(8,128)(2,1)S(1)}, u32[]{:S(2)}, u32[]{:S(2)}) collective-permute-start(bf16[8,1664]{1,0:T(8,128)(2,1)} %get-tuple-element.73), channel_id=1, source_target_pairs={{0,9},{1,8},{2,11},{3,10},{4,13},{5,12},{6,15},{7,14},{8,1},{9,0},... | collective-permute-start | bytes 79880 | tf_op jit(solution)/shard_map/ppermute | solution.py:227
  74.4 8.8 %collective-permute-start.24 = (bf16[8,1664]{1,0:T(8,128)(2,1)}, bf16[8,1664]{1,0:T(8,128)(2,1)S(1)}, u32[]{:S(2)}, u32[]{:S(2)}) collective-permute-start(bf16[8,1664]{1,0:T(8,128)(2,1)} %get-tuple-element.74), channel_id=1, source_target_pairs={{0,10},{1,11},{2,8},{3,9},{4,14},{5,15},{6,12},{7,13},{8,2},{9,3},... | collective-permute-start | bytes 79880 | tf_op jit(solution)/shard_map/ppermute | solution.py:227
  76.2 26.0 %collective-permute-start.25 = (bf16[8,1664]{1,0:T(8,128)(2,1)}, bf16[8,1664]{1,0:T(8,128)(2,1)S(1)}, u32[]{:S(2)}, u32[]{:S(2)}) collective-permute-start(bf16[8,1664]{1,0:T(8,128)(2,1)} %get-tuple-element.75), channel_id=1, source_target_pairs={{0,11},{1,10},{2,9},{3,8},{4,15},{5,14},{6,13},{7,12},{8,3},{9,2},... | collective-permute-start | bytes 79880 | tf_op jit(solution)/shard_map/ppermute | solution.py:227
  78.0 24.2 %collective-permute-start.26 = (bf16[8,1664]{1,0:T(8,128)(2,1)}, bf16[8,1664]{1,0:T(8,128)(2,1)S(1)}, u32[]{:S(2)}, u32[]{:S(2)}) collective-permute-start(bf16[8,1664]{1,0:T(8,128)(2,1)} %get-tuple-element.76), channel_id=1, source_target_pairs={{0,12},{1,13},{2,14},{3,15},{4,8},{5,9},{6,10},{7,11},{8,4},{9,5},... | collective-permute-start | bytes 79880 | tf_op jit(solution)/shard_map/ppermute | solution.py:227
  79.4 22.9 %collective-permute-start.27 = (bf16[8,1664]{1,0:T(8,128)(2,1)}, bf16[8,1664]{1,0:T(8,128)(2,1)S(1)}, u32[]{:S(2)}, u32[]{:S(2)}) collective-permute-start(bf16[8,1664]{1,0:T(8,128)(2,1)} %get-tuple-element.77), channel_id=1, source_target_pairs={{0,13},{1,12},{2,15},{3,14},{4,9},{5,8},{6,11},{7,10},{8,5},{9,4},... | collective-permute-start | bytes 79880 | tf_op jit(solution)/shard_map/ppermute | solution.py:227
  81.5 20.7 %collective-permute-start.28 = (bf16[8,1664]{1,0:T(8,128)(2,1)}, bf16[8,1664]{1,0:T(8,128)(2,1)S(1)}, u32[]{:S(2)}, u32[]{:S(2)}) collective-permute-start(bf16[8,1664]{1,0:T(8,128)(2,1)} %get-tuple-element.78), channel_id=1, source_target_pairs={{0,14},{1,15},{2,12},{3,13},{4,10},{5,11},{6,8},{7,9},{8,6},{9,7},... | collective-permute-start | bytes 79880 | tf_op jit(solution)/shard_map/ppermute | solution.py:227
  83.2 19.1 %collective-permute-start.29 = (bf16[8,1664]{1,0:T(8,128)(2,1)}, bf16[8,1664]{1,0:T(8,128)(2,1)S(1)}, u32[]{:S(2)}, u32[]{:S(2)}) collective-permute-start(bf16[8,1664]{1,0:T(8,128)(2,1)} %get-tuple-element.79), channel_id=1, source_target_pairs={{0,15},{1,14},{2,13},{3,12},{4,11},{5,10},{6,9},{7,8},{8,7},{9,6},... | collective-permute-start | bytes 79880 | tf_op jit(solution)/shard_map/ppermute | solution.py:227
  (36 other events, 434.4 us)

commit v3 on v1

--- a/solution.py
+++ b/solution.py
@@ -11,7 +11,6 @@
 EXPERTS = 16
 CAP = 4
 PAIR = 2 * CAP
-VMEM_BYTES = 60 * 1024 * 1024
 ROWS_DIM = (((0,), (0,)), ((), ()))
 LAST_DIM = (((1,), (1,)), ((), ()))
 
@@ -48,7 +47,7 @@
     return place_0, place_1
 
 
-def dispatch_kernel(ids_ref, prio_ref, gates_ref, tok_ref, cot_ref, send_ref):
+def dispatch_kernel(ids_ref, prio_ref, gates_ref, tok_ref, cot_ref, send_ref, plan_ref):
     place_0, place_1 = place_rows(ids_ref[...], prio_ref[...])
     count = tok_ref.shape[0]
     rows = EXPERTS * PAIR
@@ -67,10 +66,20 @@
     both = jnp.concatenate([tok_ref[...], cot_ref[...]], axis=0)
     found = jnp.dot(pick, both, preferred_element_type=jnp.float32)
     send_ref[...] = (found * scale).astype(jnp.bfloat16)
-
-
-def tables_kernel(ids_ref, prio_ref, gates_ref, pick_ref, gate_ref):
-    place_0, place_1 = place_rows(ids_ref[...], prio_ref[...])
+    plan_ref[...] = jnp.concatenate(
+        [
+            place_0.astype(jnp.float32),
+            place_1.astype(jnp.float32),
+            gates_ref[...],
+            jnp.zeros((4, count), jnp.float32),
+        ],
+        axis=0,
+    )
+
+
+def tables(plan_ref, pick_ref, gate_ref):
+    place_0 = plan_ref[0:1, :].astype(jnp.int32)
+    place_1 = plan_ref[1:2, :].astype(jnp.int32)
     count = place_0.shape[1]
     rows = EXPERTS * PAIR
     row = lax.broadcasted_iota(jnp.int32, (rows, count), 0)
@@ -82,8 +91,7 @@
     pick_1 = jnp.transpose(jnp.where(is_x, hit_1, 0.0), (1, 0))
     pick_b = jnp.transpose(jnp.where(is_x, 0.0, hit_0 + hit_1), (1, 0))
     pick_ref[...] = jnp.concatenate([pick_0, pick_1, pick_b], axis=0).astype(jnp.bfloat16)
-    gates = jnp.concatenate([gates_ref[...], jnp.zeros((6, count), jnp.float32)], axis=0)
-    gate_ref[...] = jnp.transpose(gates, (1, 0))
+    gate_ref[...] = jnp.transpose(plan_ref[...], (1, 0))
 
 
 def row_picks(rows):
@@ -97,8 +105,9 @@
 
 
 def forward_kernel(
-    steps, recv_ref, w_in_hbm, w_out_hbm, ret_ref, x_ref, g_ref, act_ref, d_pre_ref,
-    w_in_ref, w_out_ref, out_acc, back_acc, sem_in, sem_out,
+    steps, recv_ref, plan_ref, w_in_hbm, w_out_hbm,
+    ret_ref, x_t_ref, g_ref, act_ref, d_pre_ref, pick_ref, gate_ref,
+    w_in_ref, w_out_ref, x_ref, out_acc, back_acc, sem_in, sem_out,
 ):
     depth = w_in_ref.shape[2]
 
@@ -115,45 +124,51 @@
         return carry
 
     lax.fori_loop(0, steps, begin, 0)
-    rows = recv_ref.shape[0]
-    x_pick, g_pick = row_picks(rows)
-    x_ref[...] = jnp.dot(x_pick, recv_ref[...], preferred_element_type=jnp.float32).astype(
-        jnp.bfloat16
-    )
-    g_ref[...] = jnp.dot(g_pick, recv_ref[...], preferred_element_type=jnp.float32).astype(
-        jnp.bfloat16
-    )
+    recv = recv_ref[...]
+    x_pick, g_pick = row_picks(recv.shape[0])
+    x_rows = jnp.dot(x_pick, recv, preferred_element_type=jnp.float32)
+    x_ref[...] = x_rows.astype(jnp.bfloat16)
+    x_t_ref[...] = jnp.transpose(x_rows, (1, 0)).astype(jnp.bfloat16)
+    g_ref[...] = jnp.dot(g_pick, recv, preferred_element_type=jnp.float32).astype(jnp.bfloat16)
+    tables(plan_ref, pick_ref, gate_ref)
     out_acc[...] = jnp.zeros_like(out_acc)
     back_acc[...] = jnp.zeros_like(back_acc)
 
     def front(step):
-        for copy in copies(step):
-            copy.wait()
         pre = jnp.dot(x_ref[...], w_in_ref[step], preferred_element_type=jnp.float32)
         d_act = lax.dot_general(
             g_ref[...], w_out_ref[step], LAST_DIM, preferred_element_type=jnp.float32
         )
+        return pre, d_act
+
+    def middle(step, pre, d_act):
         value, slope = gelu_parts(pre)
         act_ref[step] = value.astype(jnp.bfloat16)
         d_pre_ref[step] = (d_act * slope).astype(jnp.bfloat16)
 
-    def back(step):
-        out_acc[...] += jnp.dot(
-            act_ref[step], w_out_ref[step], preferred_element_type=jnp.float32
+    def back(step, act, d_pre):
+        out_acc[...] += jnp.dot(act, w_out_ref[step], preferred_element_type=jnp.float32)
+        back_acc[...] += lax.dot_general(
+            d_pre, w_in_ref[step], LAST_DIM, preferred_element_type=jnp.float32
         )
-        back_acc[...] += lax.dot_general(
-            d_pre_ref[step], w_in_ref[step], LAST_DIM, preferred_element_type=jnp.float32
-        )
-
-    front(0)
+
+    def arrive(step):
+        for copy in copies(step):
+            copy.wait()
+
+    arrive(0)
+    middle(0, *front(0))
 
     def body(step, carry):
-        back(step - 1)
-        front(step)
+        arrive(step)
+        act, d_pre = act_ref[step - 1], d_pre_ref[step - 1]
+        found = front(step)
+        back(step - 1, act, d_pre)
+        middle(step, *found)
         return carry
 
     lax.fori_loop(1, steps, body, 0)
-    back(steps - 1)
+    back(steps - 1, act_ref[steps - 1], d_pre_ref[steps - 1])
     ret = lax.dot_general(
         x_pick, out_acc[...].astype(jnp.bfloat16), ROWS_DIM, preferred_element_type=jnp.float32
     ) + lax.dot_general(
@@ -162,13 +177,24 @@
     ret_ref[...] = ret.astype(jnp.bfloat16)
 
 
-def grads_kernel(x_ref, g_ref, act_ref, d_pre_ref, d_in_ref, d_out_ref):
-    d_in_ref[...] = lax.dot_general(
-        x_ref[...], d_pre_ref[0], ROWS_DIM, preferred_element_type=jnp.float32
-    ).astype(jnp.bfloat16)
-    d_out_ref[...] = lax.dot_general(
-        act_ref[0], g_ref[...], ROWS_DIM, preferred_element_type=jnp.float32
-    ).astype(jnp.bfloat16)
+def grads_kernel(steps, x_t_ref, g_ref, act_ref, d_pre_ref, d_in_ref, d_out_ref):
+    depth = act_ref.shape[2]
+    piece = 128
+
+    for step in range(steps):
+        d_in_ref[:, step * depth:(step + 1) * depth] = jnp.dot(
+            x_t_ref[...], d_pre_ref[step], preferred_element_type=jnp.float32
+        ).astype(jnp.bfloat16)
+
+    @pl.when(pl.program_id(0) < steps)
+    def _():
+        for first in range(0, depth, piece):
+            d_out_ref[first:first + piece, :] = lax.dot_general(
+                act_ref[0, :, first:first + piece],
+                g_ref[...],
+                ROWS_DIM,
+                preferred_element_type=jnp.float32,
+            ).astype(jnp.bfloat16)
 
 
 def combine_kernel(ret_ref, pick_ref, gate_ref, cot_ref, mixed_ref, d_tok_ref, d_gate_ref):
@@ -181,7 +207,7 @@
         )
         found = part if found is None else found + part
     o_0, o_1 = found[:count], found[count:2 * count]
-    mixed_ref[...] = (gate_ref[:, 0:1] * o_0 + gate_ref[:, 1:2] * o_1).astype(jnp.bfloat16)
+    mixed_ref[...] = (gate_ref[:, 2:3] * o_0 + gate_ref[:, 3:4] * o_1).astype(jnp.bfloat16)
     d_tok_ref[...] = found[2 * count:].astype(jnp.bfloat16)
     cot = cot_ref[...].astype(jnp.float32)
     d_0 = jnp.sum(cot * o_0, axis=1, keepdims=True)
@@ -191,8 +217,8 @@
     d_gate_ref[...] = jnp.transpose(both, (1, 0))[0:2, :]
 
 
-def params():
-    return pltpu.CompilerParams(vmem_limit_bytes=VMEM_BYTES)
+def params(mib):
+    return pltpu.CompilerParams(vmem_limit_bytes=mib * 1024 * 1024)
 
 
 def chunk_of(hidden, want):
@@ -206,21 +232,15 @@
     hidden = w_in.shape[2]
     ids_t = jnp.transpose(expert_ids, (1, 0))
     gates_t = jnp.transpose(gates, (1, 0))
-    send = pl.pallas_call(
+    send, plan = pl.pallas_call(
         dispatch_kernel,
-        out_shape=jax.ShapeDtypeStruct((slots, width), jnp.bfloat16),
-        compiler_params=params(),
+        out_shape=(
+            jax.ShapeDtypeStruct((slots, width), jnp.bfloat16),
+            jax.ShapeDtypeStruct((8, count), jnp.float32),
+        ),
+        compiler_params=params(60),
         name="dispatch",
     )(ids_t, priority, gates_t, tokens, cotangent)
-    pick, gate_cols = pl.pallas_call(
-        tables_kernel,
-        out_shape=(
-            jax.ShapeDtypeStruct((3 * count, slots), jnp.bfloat16),
-            jax.ShapeDtypeStruct((count, 8), jnp.float32),
-        ),
-        compiler_params=params(),
-        name="tables",
-    )(ids_t, priority, gates_t)
     send = jnp.tile(send.reshape(EXPERTS, PAIR, width), (repl, 1, 1))
     recv = lax.all_to_all(send, "expert", split_axis=0, concat_axis=0, tiled=True)
     rows = recv.shape[0] * PAIR
@@ -231,62 +251,65 @@
     vmem = pl.BlockSpec(memory_space=pltpu.VMEM)
     hbm = pl.BlockSpec(memory_space=pl.ANY)
     low = jnp.bfloat16
-    ret, x_rows, g_rows, act, d_pre = pl.pallas_call(
+    ret, x_t, g_rows, act, d_pre, pick, gate_cols = pl.pallas_call(
         functools.partial(forward_kernel, steps),
         out_shape=(
             jax.ShapeDtypeStruct((rows, width), low),
-            jax.ShapeDtypeStruct((half, width), low),
+            jax.ShapeDtypeStruct((width, half), low),
             jax.ShapeDtypeStruct((half, width), low),
             jax.ShapeDtypeStruct((steps, half, chunk), low),
             jax.ShapeDtypeStruct((steps, half, chunk), low),
-        ),
-        in_specs=[vmem, hbm, hbm],
-        out_specs=(vmem,) * 5,
+            jax.ShapeDtypeStruct((3 * count, slots), low),
+            jax.ShapeDtypeStruct((count, 8), jnp.float32),
+        ),
+        in_specs=[vmem] * 2 + [hbm] * 2,
+        out_specs=(vmem,) * 7,
         scratch_shapes=[
             pltpu.VMEM((steps, width, chunk), low),
             pltpu.VMEM((steps, chunk, width), low),
+            pltpu.VMEM((half, width), low),
             pltpu.VMEM((half, width), jnp.float32),
             pltpu.VMEM((half, width), jnp.float32),
             pltpu.SemaphoreType.DMA((steps,)),
             pltpu.SemaphoreType.DMA((steps,)),
         ],
-        compiler_params=params(),
+        compiler_params=params(50),
         cost_estimate=pl.CostEstimate(
             flops=8 * half * width * hidden,
             bytes_accessed=4 * width * hidden,
             transcendentals=half * hidden,
         ),
         name="forward",
-    )(recv, w_in[0], w_out[0])
+    )(recv, plan, w_in[0], w_out[0])
     ret = lax.all_to_all(
         ret.reshape(rows // PAIR, PAIR, width), "expert", split_axis=0, concat_axis=0, tiled=True
     ).reshape(rows, width)
-    whole = lambda i: (0, 0)
+    strip = 128
     d_w_in, d_w_out = pl.pallas_call(
-        grads_kernel,
-        grid=(steps,),
+        functools.partial(grads_kernel, steps),
+        grid=(width // strip,),
         out_shape=(
             jax.ShapeDtypeStruct((width, hidden), low),
             jax.ShapeDtypeStruct((hidden, width), low),
         ),
         in_specs=[
-            pl.BlockSpec((half, width), whole),
-            pl.BlockSpec((half, width), whole),
-            pl.BlockSpec((1, half, chunk), lambda i: (i, 0, 0)),
-            pl.BlockSpec((1, half, chunk), lambda i: (i, 0, 0)),
+            pl.BlockSpec((strip, half), lambda i: (i, 0)),
+            pl.BlockSpec((half, width), lambda i: (0, 0)),
+            pl.BlockSpec((1, half, chunk), lambda i: (jnp.minimum(i, steps - 1), 0, 0)),
+            pl.BlockSpec((steps, half, chunk), lambda i: (0, 0, 0)),
         ],
         out_specs=(
-            pl.BlockSpec((width, chunk), lambda i: (0, i)),
-            pl.BlockSpec((chunk, width), lambda i: (i, 0)),
-        ),
-        compiler_params=params(),
+            pl.BlockSpec((strip, hidden), lambda i: (i, 0)),
+            pl.BlockSpec((chunk, width), lambda i: (jnp.minimum(i, steps - 1), 0)),
+        ),
+        compiler_params=params(24),
         cost_estimate=pl.CostEstimate(
             flops=4 * half * width * hidden,
             bytes_accessed=4 * width * hidden,
             transcendentals=0,
         ),
         name="grads",
-    )(x_rows, g_rows, act, d_pre)
+    )(x_t, g_rows, act, d_pre)
     mixed, d_tokens, d_gates_t = pl.pallas_call(
         combine_kernel,
         out_shape=(
@@ -294,7 +317,7 @@
             jax.ShapeDtypeStruct((count, width), low),
             jax.ShapeDtypeStruct((2, count), jnp.float32),
         ),
-        compiler_params=params(),
+        compiler_params=params(12),
         name="combine",
     )(ret, pick, gate_cols, cotangent)
     return (mixed, d_tokens, jnp.transpose(d_gates_t, (1, 0)), d_w_in[None], d_w_out[None])

time: 75.7 us -> 72.9 us (0.963)
  Pallas kernels: 49.9 us -> 47.4 us
    pallas_call x1, Pallas kernels: 26.5 us -> 24.3 us  [per_device(): pl.pallas_call(functools.partial(forward_kernel, steps), out_shape=(jax.S...]
    pallas_call x1, Pallas kernels: 2.72 us -> 1.51 us  [per_device(): pl.pallas_call(combine_kernel, out_shape=(jax.ShapeDtypeStruct((count, wi...]
    pallas_call x3 -> x2, Pallas kernels: 20.7 us -> 21.6 us  [the longest x1 19.1 us: per_device(): pl.pallas_call(functools.partial(grads_kernel, steps), grid=(width // str...]
  transfers between devices with their start and end apart: 1 -> 1, of which waited for: 0 -> 0; matrix products, arithmetic and copies ran while one was open for 0% -> 0% of each run, Pallas kernels for 24% -> 26%
where the time goes in v3:
time: 72.9 us; the launch traced here: 72.5 us
  Pallas kernels  47.4 us (65%)
  blocking collectives  20.1 us (28%)
  starting transfers between devices  3.71 us (5%)
    pallas_call x1, Pallas kernels, per_device(): pl.pallas_call(functools.partial(forward_kernel, steps), out_shape=(jax.S...  24.3 us
    all_to_all x1, blocking collectives, per_device(): lax.all_to_all(send, 'expert', split_axis=0, concat_axis=0, tiled=True)  20.1 us
    pallas_call x1, Pallas kernels, per_device(): pl.pallas_call(functools.partial(grads_kernel, steps), grid=(width // str...  19.1 us
    all_to_all x1, starting transfers between devices, per_device(): lax.all_to_all(ret.reshape(rows // PAIR, PAIR, width), 'expert', split_ax...  3.71 us
    pallas_call x1, Pallas kernels, per_device(): pl.pallas_call(dispatch_kernel, out_shape=(jax.ShapeDtypeStruct((slots, w...  2.46 us
    pallas_call x1, Pallas kernels, per_device(): pl.pallas_call(combine_kernel, out_shape=(jax.ShapeDtypeStruct((count, wi...  1.51 us
  transfers between devices with their start and end apart: 1, of which 0 were waited for; matrix products, arithmetic and copies ran while one was open for 0% of the time, Pallas kernels for 26%

profile of v3, /device:TPU:0, one launch (start us, length us, event | category | flops | bytes accessed | tf_op | source)
XLA Modules:
  0.0 72.5 jit_solution(2963085043923203746)
XLA Ops:
  0.6 2.5 %dispatch.1 = (bf16[128,1664]{1,0:T(8,128)(2,1)}, f32[8,128]{1,0:T(8,128)}) custom-call(s32[2,128]{1,0:T(2,128)} %bitcast.16, s32[1,128]{1,0:T(1,128)} %prio_ref.1, f32[2,128]{1,0:T(2,128)} %bitcast.17, bf16[128,1664]{1,0:T(8,128)(2,1)} %tok_ref.1, bf16[128,1664]{1,0:T(8,128)(2,1)} %cot_ref.3), custom_call_target="tpu_custom_call" | custom-call | tf_op jit(solution)/shard_map/dispatch/pallas_call | solution.py:235
  3.1 20.1 %all_to_all.10 = bf16[16,8,1664]{2,1,0:T(8,128)(2,1)S(1)} all-to-all(bf16[16,8,1664]{2,1,0:T(8,128)(2,1)} %bitcast.15), channel_id=1, replica_groups=mesh['groups'=2,'expert'=16] {'expert'}, dimensions={0} | all-to-all | bytes 851968 | tf_op jit(solution)/shard_map/all_to_all | solution.py:245
  23.2 0.0 copy-start.1
  23.2 0.7 copy-done.1
  23.9 0.0 copy-start
  23.9 24.3 %forward.1 = (bf16[128,1664]{1,0:T(8,128)(2,1)}, bf16[1664,64]{1,0:T(8,128)(2,1)S(1)}, bf16[64,1664]{1,0:T(8,128)(2,1)S(1)}, bf16[12,64,512]{2,1,0:T(8,128)(2,1)...) custom-call(bf16[128,1664]{1,0:T(8,128)(2,1)S(1)} %bitcast.11, ...), custom_call_target="tpu_custom_call" | custom-call | flops 5234491392 | bytes 40894464 | tf_op jit(solution)/shard_map/forward/pallas_call | solution.py:254
  48.2 3.7 %all-to-all-start.1 = ((bf16[16,8,1664]{2,1,0:T(8,128)(2,1)}), bf16[16,8,1664]{2,1,0:T(8,128)(2,1)S(1)}, u32[]{:S(2)}, u32[]{:S(2)}) async-start(bf16[16,8,1664]{2,1,0:T(8,128)(2,1)} %bitcast.6), calls=%async_computation.1 | async-start | bytes 851968 | tf_op jit(solution)/shard_map/all_to_all | solution.py:284
  51.9 19.1 %grads.1 = (bf16[1664,6144]{1,0:T(8,128)(2,1)}, bf16[6144,1664]{1,0:T(8,128)(2,1)}) custom-call(bf16[1664,64]{1,0:T(8,128)(2,1)S(1)} %get-tuple-element.27.x_t_ref, bf16[64,1664]{1,0:T(8,128)(2,1)S(1)} %get-tuple-element.28.g_ref, bf16[12,64,512]{2,1,0:T(8,128)(2,1)S(1)} %get-tuple-element.29.act_ref, bf16[12,64,512]{2,1,0:T(8,128)(2,1)S(1)} %get-tuple-element.30.d_pre_ref), custom_call_target="tpu_custom_call" | custom-call | flops 2617245696 | bytes 40894464 | tf_op jit(solution)/shard_map/grads/pallas_call | solution.py:288
  71.0 0.0 all-to-all-done.1
  71.0 0.0 copy-done
  71.0 1.5 %combine.1 = (bf16[128,1664]{1,0:T(8,128)(2,1)}, bf16[128,1664]{1,0:T(8,128)(2,1)}, f32[2,128]{1,0:T(2,128)}) custom-call(bf16[128,1664]{1,0:T(8,128)(2,1)S(1)} %bitcast.12, bf16[384,128]{1,0:T(8,128)(2,1)S(1)} %get-tuple-element.22.pick_ref, f32[128,8]{1,0:T(8,128)S(1)} %get-tuple-element.23.gate_ref, bf16[128,1664]{1,0:T(8,128)(2,1)S(1)} %copy-done), custom_call_target="tpu_custom_call" | custom-call | tf_op jit(solution)/shard_map/combine/pallas_call | solution.py:313
Async XLA Ops:
  23.2 0.7 copy-start.1
  23.9 47.1 %copy-start = (bf16[128,1664]{1,0:T(8,128)(2,1)S(1)}, bf16[128,1664]{1,0:T(8,128)(2,1)}, u32[]{:S(2)}) copy-start(bf16[128,1664]{1,0:T(8,128)(2,1)} %cot_ref.3) | copy-start | bytes 1277956
  48.2 22.9 %all-to-all-start.1 = ((bf16[16,8,1664]{2,1,0:T(8,128)(2,1)}), bf16[16,8,1664]{2,1,0:T(8,128)(2,1)S(1)}, u32[]{:S(2)}, u32[]{:S(2)}) async-start(bf16[16,8,1664]{2,1,0:T(8,128)(2,1)} %bitcast.6), calls=%async_computation.1 | async-start | bytes 851968 | tf_op jit(solution)/shard_map/all_to_all | solution.py:284

commit v4 on v3

--- a/solution.py
+++ b/solution.py
@@ -11,6 +11,7 @@
 EXPERTS = 16
 CAP = 4
 PAIR = 2 * CAP
+AHEAD = 2
 ROWS_DIM = (((0,), (0,)), ((), ()))
 LAST_DIM = (((1,), (1,)), ((), ()))
 
@@ -118,12 +119,12 @@
             pltpu.make_async_copy(w_out_hbm.at[cols, :], w_out_ref.at[step], sem_out.at[step]),
         )
 
-    def begin(step, carry):
+    def begin(step):
         for copy in copies(step):
             copy.start()
-        return carry
-
-    lax.fori_loop(0, steps, begin, 0)
+
+    for step in range(min(AHEAD, steps)):
+        begin(step)
     recv = recv_ref[...]
     x_pick, g_pick = row_picks(recv.shape[0])
     x_rows = jnp.dot(x_pick, recv, preferred_element_type=jnp.float32)
@@ -157,10 +158,17 @@
             copy.wait()
 
     arrive(0)
+    if steps > AHEAD:
+        begin(AHEAD)
     middle(0, *front(0))
 
     def body(step, carry):
         arrive(step)
+
+        @pl.when(step + AHEAD < steps)
+        def _():
+            begin(step + AHEAD)
+
         act, d_pre = act_ref[step - 1], d_pre_ref[step - 1]
         found = front(step)
         back(step - 1, act, d_pre)
@@ -177,24 +185,21 @@
     ret_ref[...] = ret.astype(jnp.bfloat16)
 
 
-def grads_kernel(steps, x_t_ref, g_ref, act_ref, d_pre_ref, d_in_ref, d_out_ref):
-    depth = act_ref.shape[2]
-    piece = 128
-
-    for step in range(steps):
-        d_in_ref[:, step * depth:(step + 1) * depth] = jnp.dot(
-            x_t_ref[...], d_pre_ref[step], preferred_element_type=jnp.float32
-        ).astype(jnp.bfloat16)
-
-    @pl.when(pl.program_id(0) < steps)
-    def _():
-        for first in range(0, depth, piece):
-            d_out_ref[first:first + piece, :] = lax.dot_general(
-                act_ref[0, :, first:first + piece],
-                g_ref[...],
-                ROWS_DIM,
-                preferred_element_type=jnp.float32,
+def product(out_ref, left, right, tall, wide):
+    rows, cols = out_ref.shape
+    for col in range(0, cols, wide):
+        col_end = min(col + wide, cols)
+        for row in range(0, rows, tall):
+            row_end = min(row + tall, rows)
+            out_ref[row:row_end, col:col_end] = jnp.dot(
+                left[row:row_end], right[:, col:col_end], preferred_element_type=jnp.float32
             ).astype(jnp.bfloat16)
+
+
+def grads_kernel(x_t_ref, g_ref, act_ref, d_pre_ref, d_in_ref, d_out_ref):
+    act_t = jnp.transpose(act_ref[0].astype(jnp.float32), (1, 0)).astype(jnp.bfloat16)
+    product(d_in_ref, x_t_ref[...], d_pre_ref[0], 208, 256)
+    product(d_out_ref, act_t, g_ref[...], 256, 256)
 
 
 def combine_kernel(ret_ref, pick_ref, gate_ref, cot_ref, mixed_ref, d_tok_ref, d_gate_ref):
@@ -236,7 +241,7 @@
         dispatch_kernel,
         out_shape=(
             jax.ShapeDtypeStruct((slots, width), jnp.bfloat16),
-            jax.ShapeDtypeStruct((8, count), jnp.float32),
+            pltpu.VMEM((8, count), jnp.float32),
         ),
         compiler_params=params(60),
         name="dispatch",
@@ -284,23 +289,22 @@
     ret = lax.all_to_all(
         ret.reshape(rows // PAIR, PAIR, width), "expert", split_axis=0, concat_axis=0, tiled=True
     ).reshape(rows, width)
-    strip = 128
     d_w_in, d_w_out = pl.pallas_call(
-        functools.partial(grads_kernel, steps),
-        grid=(width // strip,),
+        grads_kernel,
+        grid=(steps,),
         out_shape=(
             jax.ShapeDtypeStruct((width, hidden), low),
             jax.ShapeDtypeStruct((hidden, width), low),
         ),
         in_specs=[
-            pl.BlockSpec((strip, half), lambda i: (i, 0)),
+            pl.BlockSpec((width, half), lambda i: (0, 0)),
             pl.BlockSpec((half, width), lambda i: (0, 0)),
-            pl.BlockSpec((1, half, chunk), lambda i: (jnp.minimum(i, steps - 1), 0, 0)),
-            pl.BlockSpec((steps, half, chunk), lambda i: (0, 0, 0)),
+            pl.BlockSpec((1, half, chunk), lambda i: (i, 0, 0)),
+            pl.BlockSpec((1, half, chunk), lambda i: (i, 0, 0)),
         ],
         out_specs=(
-            pl.BlockSpec((strip, hidden), lambda i: (i, 0)),
-            pl.BlockSpec((chunk, width), lambda i: (jnp.minimum(i, steps - 1), 0)),
+            pl.BlockSpec((width, chunk), lambda i: (0, i)),
+            pl.BlockSpec((chunk, width), lambda i: (i, 0)),
         ),
         compiler_params=params(24),
         cost_estimate=pl.CostEstimate(

time: 72.9 us -> 68.5 us (0.940)
  Pallas kernels: 47.4 us -> 43.7 us
    pallas_call x1, Pallas kernels: 19.1 us -> 14.9 us  [per_device(): pl.pallas_call(grads_kernel, grid=(steps,), out_shape=(jax.ShapeDtypeStru...]
  transfers between devices with their start and end apart: 1 -> 1, of which waited for: 0 -> 0; matrix products, arithmetic and copies ran while one was open for 0% -> 0% of each run, Pallas kernels for 26% -> 22%
where the time goes in v4:
time: 68.5 us; the launch traced here: 68.2 us
  Pallas kernels  43.7 us (64%)
  blocking collectives  20.1 us (29%)
  starting transfers between devices  3.71 us (5%)
    pallas_call x1, Pallas kernels, per_device(): pl.pallas_call(functools.partial(forward_kernel, steps), out_shape=(jax.S...  24.9 us
    all_to_all x1, blocking collectives, per_device(): lax.all_to_all(send, 'expert', split_axis=0, concat_axis=0, tiled=True)  20.1 us
    pallas_call x1, Pallas kernels, per_device(): pl.pallas_call(grads_kernel, grid=(steps,), out_shape=(jax.ShapeDtypeStru...  14.9 us
    all_to_all x1, starting transfers between devices, per_device(): lax.all_to_all(ret.reshape(rows // PAIR, PAIR, width), 'expert', split_ax...  3.71 us
    pallas_call x1, Pallas kernels, per_device(): pl.pallas_call(dispatch_kernel, out_shape=(jax.ShapeDtypeStruct((slots, w...  2.46 us
    pallas_call x1, Pallas kernels, per_device(): pl.pallas_call(combine_kernel, out_shape=(jax.ShapeDtypeStruct((count, wi...  1.51 us
  transfers between devices with their start and end apart: 1, of which 0 were waited for; matrix products, arithmetic and copies ran while one was open for 0% of the time, Pallas kernels for 22%

profile of v4, /device:TPU:0, one launch (start us, length us, event | category | flops | bytes accessed | tf_op | source)
XLA Modules:
  0.0 68.2 jit_solution(5422867798360487013)
XLA Ops:
  0.6 2.5 %dispatch.1 = (bf16[128,1664]{1,0:T(8,128)(2,1)}, f32[8,128]{1,0:T(8,128)S(1)}) custom-call(s32[2,128]{1,0:T(2,128)} %bitcast.16, s32[1,128]{1,0:T(1,128)} %prio_ref.1, f32[2,128]{1,0:T(2,128)} %bitcast.17, bf16[128,1664]{1,0:T(8,128)(2,1)} %tok_ref.1, bf16[128,1664]{1,0:T(8,128)(2,1)} %cot_ref.3), custom_call_target="tpu_custom_call" | custom-call | tf_op jit(solution)/shard_map/dispatch/pallas_call | solution.py:240
  3.1 20.1 %all_to_all.10 = bf16[16,8,1664]{2,1,0:T(8,128)(2,1)S(1)} all-to-all(bf16[16,8,1664]{2,1,0:T(8,128)(2,1)} %bitcast.15), channel_id=1, replica_groups=mesh['groups'=2,'expert'=16] {'expert'}, dimensions={0} | all-to-all | bytes 851968 | tf_op jit(solution)/shard_map/all_to_all | solution.py:250
  23.2 0.0 copy-start
  23.2 24.9 %forward.1 = (bf16[128,1664]{1,0:T(8,128)(2,1)}, bf16[1664,64]{1,0:T(8,128)(2,1)S(1)}, bf16[64,1664]{1,0:T(8,128)(2,1)S(1)}, bf16[12,64,512]{2,1,0:T(8,128)(2,1)...) custom-call(bf16[128,1664]{1,0:T(8,128)(2,1)S(1)} %bitcast.11, ...), custom_call_target="tpu_custom_call" | custom-call | flops 5234491392 | bytes 40894464 | tf_op jit(solution)/shard_map/forward/pallas_call | solution.py:259
  48.1 3.7 %all-to-all-start.1 = ((bf16[16,8,1664]{2,1,0:T(8,128)(2,1)}), bf16[16,8,1664]{2,1,0:T(8,128)(2,1)S(1)}, u32[]{:S(2)}, u32[]{:S(2)}) async-start(bf16[16,8,1664]{2,1,0:T(8,128)(2,1)} %bitcast.6), calls=%async_computation.1 | async-start | bytes 851968 | tf_op jit(solution)/shard_map/all_to_all | solution.py:289
  51.8 14.9 %grads.1 = (bf16[1664,6144]{1,0:T(8,128)(2,1)}, bf16[6144,1664]{1,0:T(8,128)(2,1)}) custom-call(bf16[1664,64]{1,0:T(8,128)(2,1)S(1)} %get-tuple-element.27.x_t_ref, bf16[64,1664]{1,0:T(8,128)(2,1)S(1)} %get-tuple-element.28.g_ref, bf16[12,64,512]{2,1,0:T(8,128)(2,1)S(1)} %get-tuple-element.29.act_ref, bf16[12,64,512]{2,1,0:T(8,128)(2,1)S(1)} %get-tuple-element.30.d_pre_ref), custom_call_target="tpu_custom_call" | custom-call | flops 2617245696 | bytes 40894464 | tf_op jit(solution)/shard_map/grads/pallas_call | solution.py:292
  66.7 0.0 all-to-all-done.1
  66.7 0.0 copy-done
  66.7 1.5 %combine.1 = (bf16[128,1664]{1,0:T(8,128)(2,1)}, bf16[128,1664]{1,0:T(8,128)(2,1)}, f32[2,128]{1,0:T(2,128)}) custom-call(bf16[128,1664]{1,0:T(8,128)(2,1)S(1)} %bitcast.12, bf16[384,128]{1,0:T(8,128)(2,1)S(1)} %get-tuple-element.22.pick_ref, f32[128,8]{1,0:T(8,128)S(1)} %get-tuple-element.23.gate_ref, bf16[128,1664]{1,0:T(8,128)(2,1)S(1)} %copy-done), custom_call_target="tpu_custom_call" | custom-call | tf_op jit(solution)/shard_map/combine/pallas_call | solution.py:317
Async XLA Ops:
  23.2 43.5 %copy-start = (bf16[128,1664]{1,0:T(8,128)(2,1)S(1)}, bf16[128,1664]{1,0:T(8,128)(2,1)}, u32[]{:S(2)}) copy-start(bf16[128,1664]{1,0:T(8,128)(2,1)} %cot_ref.3) | copy-start | bytes 1277956
  48.1 18.6 %all-to-all-start.1 = ((bf16[16,8,1664]{2,1,0:T(8,128)(2,1)}), bf16[16,8,1664]{2,1,0:T(8,128)(2,1)S(1)}, u32[]{:S(2)}, u32[]{:S(2)}) async-start(bf16[16,8,1664]{2,1,0:T(8,128)(2,1)} %bitcast.6), calls=%async_computation.1 | async-start | bytes 851968 | tf_op jit(solution)/shard_map/all_to_all | solution.py:289

commit v5 on v4

--- a/solution.py
+++ b/solution.py
@@ -11,7 +11,6 @@
 EXPERTS = 16
 CAP = 4
 PAIR = 2 * CAP
-AHEAD = 2
 ROWS_DIM = (((0,), (0,)), ((), ()))
 LAST_DIM = (((1,), (1,)), ((), ()))
 
@@ -48,9 +47,17 @@
     return place_0, place_1
 
 
-def dispatch_kernel(ids_ref, prio_ref, gates_ref, tok_ref, cot_ref, send_ref, plan_ref):
+def dispatch_kernel(
+    ids_ref, prio_ref, gates_ref, tok_hbm, cot_hbm, send_ref, plan_ref, both_ref, sem
+):
+    count = tok_hbm.shape[0]
+    copies = (
+        pltpu.make_async_copy(tok_hbm, both_ref.at[0:count], sem.at[0]),
+        pltpu.make_async_copy(cot_hbm, both_ref.at[count:2 * count], sem.at[1]),
+    )
+    for copy in copies:
+        copy.start()
     place_0, place_1 = place_rows(ids_ref[...], prio_ref[...])
-    count = tok_ref.shape[0]
     rows = EXPERTS * PAIR
     row = lax.broadcasted_iota(jnp.int32, (rows, count), 0)
     slot = row // PAIR * CAP + row % CAP
@@ -64,9 +71,6 @@
     gate = jnp.where(hit_0, gates_ref[0:1, :], 0.0) + jnp.where(hit_1, gates_ref[1:2, :], 0.0)
     scale = jnp.sum(gate, axis=1, keepdims=True)
     scale = jnp.where(is_x[:, 0:1], 1.0, scale)
-    both = jnp.concatenate([tok_ref[...], cot_ref[...]], axis=0)
-    found = jnp.dot(pick, both, preferred_element_type=jnp.float32)
-    send_ref[...] = (found * scale).astype(jnp.bfloat16)
     plan_ref[...] = jnp.concatenate(
         [
             place_0.astype(jnp.float32),
@@ -76,6 +80,10 @@
         ],
         axis=0,
     )
+    for copy in copies:
+        copy.wait()
+    found = jnp.dot(pick, both_ref[...], preferred_element_type=jnp.float32)
+    send_ref[...] = (found * scale).astype(jnp.bfloat16)
 
 
 def tables(plan_ref, pick_ref, gate_ref):
@@ -112,19 +120,31 @@
 ):
     depth = w_in_ref.shape[2]
 
-    def copies(step):
-        cols = pl.ds(pl.multiple_of(step * depth, depth), depth)
+    part = depth // 2
+
+    def copies(step, first, size, slot):
+        cols = pl.ds(pl.multiple_of(step * depth + first, size), size)
+        near = pl.ds(first, size)
         return (
-            pltpu.make_async_copy(w_in_hbm.at[:, cols], w_in_ref.at[step], sem_in.at[step]),
-            pltpu.make_async_copy(w_out_hbm.at[cols, :], w_out_ref.at[step], sem_out.at[step]),
+            pltpu.make_async_copy(
+                w_in_hbm.at[:, cols], w_in_ref.at[step, :, near], sem_in.at[slot]
+            ),
+            pltpu.make_async_copy(
+                w_out_hbm.at[cols, :], w_out_ref.at[step, near, :], sem_out.at[slot]
+            ),
         )
 
-    def begin(step):
-        for copy in copies(step):
+    opening = [copies(0, 0, part, 0), copies(0, part, part, steps)]
+    for pair in opening:
+        for copy in pair:
             copy.start()
 
-    for step in range(min(AHEAD, steps)):
-        begin(step)
+    def begin(step, carry):
+        for copy in copies(step, 0, depth, step):
+            copy.start()
+        return carry
+
+    lax.fori_loop(1, steps, begin, 0)
     recv = recv_ref[...]
     x_pick, g_pick = row_picks(recv.shape[0])
     x_rows = jnp.dot(x_pick, recv, preferred_element_type=jnp.float32)
@@ -135,17 +155,17 @@
     out_acc[...] = jnp.zeros_like(out_acc)
     back_acc[...] = jnp.zeros_like(back_acc)
 
-    def front(step):
-        pre = jnp.dot(x_ref[...], w_in_ref[step], preferred_element_type=jnp.float32)
+    def front(step, cols):
+        pre = jnp.dot(x_ref[...], w_in_ref[step, :, cols], preferred_element_type=jnp.float32)
         d_act = lax.dot_general(
-            g_ref[...], w_out_ref[step], LAST_DIM, preferred_element_type=jnp.float32
+            g_ref[...], w_out_ref[step, cols, :], LAST_DIM, preferred_element_type=jnp.float32
         )
         return pre, d_act
 
-    def middle(step, pre, d_act):
+    def middle(step, cols, pre, d_act):
         value, slope = gelu_parts(pre)
-        act_ref[step] = value.astype(jnp.bfloat16)
-        d_pre_ref[step] = (d_act * slope).astype(jnp.bfloat16)
+        act_ref[step, :, cols] = value.astype(jnp.bfloat16)
+        d_pre_ref[step, :, cols] = (d_act * slope).astype(jnp.bfloat16)
 
     def back(step, act, d_pre):
         out_acc[...] += jnp.dot(act, w_out_ref[step], preferred_element_type=jnp.float32)
@@ -153,26 +173,20 @@
             d_pre, w_in_ref[step], LAST_DIM, preferred_element_type=jnp.float32
         )
 
-    def arrive(step):
-        for copy in copies(step):
+    for first, pair in zip((0, part), opening):
+        for copy in pair:
             copy.wait()
-
-    arrive(0)
-    if steps > AHEAD:
-        begin(AHEAD)
-    middle(0, *front(0))
+        cols = slice(first, first + part)
+        middle(0, cols, *front(0, cols))
 
     def body(step, carry):
-        arrive(step)
-
-        @pl.when(step + AHEAD < steps)
-        def _():
-            begin(step + AHEAD)
-
+        for copy in copies(step, 0, depth, step):
+            copy.wait()
+        cols = slice(0, depth)
         act, d_pre = act_ref[step - 1], d_pre_ref[step - 1]
-        found = front(step)
+        found = front(step, cols)
         back(step - 1, act, d_pre)
-        middle(step, *found)
+        middle(step, cols, *found)
         return carry
 
     lax.fori_loop(1, steps, body, 0)
@@ -198,8 +212,8 @@
 
 def grads_kernel(x_t_ref, g_ref, act_ref, d_pre_ref, d_in_ref, d_out_ref):
     act_t = jnp.transpose(act_ref[0].astype(jnp.float32), (1, 0)).astype(jnp.bfloat16)
-    product(d_in_ref, x_t_ref[...], d_pre_ref[0], 208, 256)
-    product(d_out_ref, act_t, g_ref[...], 256, 256)
+    product(d_in_ref, x_t_ref[...], d_pre_ref[0], 416, 256)
+    product(d_out_ref, act_t, g_ref[...], 512, 256)
 
 
 def combine_kernel(ret_ref, pick_ref, gate_ref, cot_ref, mixed_ref, d_tok_ref, d_gate_ref):
@@ -237,13 +251,22 @@
     hidden = w_in.shape[2]
     ids_t = jnp.transpose(expert_ids, (1, 0))
     gates_t = jnp.transpose(gates, (1, 0))
+    low = jnp.bfloat16
+    vmem = pl.BlockSpec(memory_space=pltpu.VMEM)
+    hbm = pl.BlockSpec(memory_space=pl.ANY)
     send, plan = pl.pallas_call(
         dispatch_kernel,
         out_shape=(
-            jax.ShapeDtypeStruct((slots, width), jnp.bfloat16),
+            pltpu.VMEM((slots, width), low),
             pltpu.VMEM((8, count), jnp.float32),
         ),
-        compiler_params=params(60),
+        in_specs=[vmem] * 3 + [hbm] * 2,
+        out_specs=(vmem,) * 2,
+        scratch_shapes=[
+            pltpu.VMEM((2 * count, width), low),
+            pltpu.SemaphoreType.DMA((2,)),
+        ],
+        compiler_params=params(56),
         name="dispatch",
     )(ids_t, priority, gates_t, tokens, cotangent)
     send = jnp.tile(send.reshape(EXPERTS, PAIR, width), (repl, 1, 1))
@@ -251,15 +274,13 @@
     rows = recv.shape[0] * PAIR
     recv = recv.reshape(rows, width)
     half = rows // 2
-    chunk = chunk_of(hidden, 512)
+    chunk = chunk_of(hidden, 1024)
     steps = hidden // chunk
-    vmem = pl.BlockSpec(memory_space=pltpu.VMEM)
-    hbm = pl.BlockSpec(memory_space=pl.ANY)
-    low = jnp.bfloat16
+    part = chunk // 2
     ret, x_t, g_rows, act, d_pre, pick, gate_cols = pl.pallas_call(
         functools.partial(forward_kernel, steps),
         out_shape=(
-            jax.ShapeDtypeStruct((rows, width), low),
+            pltpu.VMEM((rows, width), low),
             jax.ShapeDtypeStruct((width, half), low),
             jax.ShapeDtypeStruct((half, width), low),
             jax.ShapeDtypeStruct((steps, half, chunk), low),
@@ -275,8 +296,8 @@
             pltpu.VMEM((half, width), low),
             pltpu.VMEM((half, width), jnp.float32),
             pltpu.VMEM((half, width), jnp.float32),
-            pltpu.SemaphoreType.DMA((steps,)),
-            pltpu.SemaphoreType.DMA((steps,)),
+            pltpu.SemaphoreType.DMA((steps + 1,)),
+            pltpu.SemaphoreType.DMA((steps + 1,)),
         ],
         compiler_params=params(50),
         cost_estimate=pl.CostEstimate(
@@ -291,7 +312,7 @@
     ).reshape(rows, width)
     d_w_in, d_w_out = pl.pallas_call(
         grads_kernel,
-        grid=(steps,),
+        grid=(2 * steps,),
         out_shape=(
             jax.ShapeDtypeStruct((width, hidden), low),
             jax.ShapeDtypeStruct((hidden, width), low),
@@ -299,12 +320,12 @@
         in_specs=[
             pl.BlockSpec((width, half), lambda i: (0, 0)),
             pl.BlockSpec((half, width), lambda i: (0, 0)),
-            pl.BlockSpec((1, half, chunk), lambda i: (i, 0, 0)),
-            pl.BlockSpec((1, half, chunk), lambda i: (i, 0, 0)),
+            pl.BlockSpec((1, half, part), lambda i: (i // 2, 0, i % 2)),
+            pl.BlockSpec((1, half, part), lambda i: (i // 2, 0, i % 2)),
         ],
         out_specs=(
-            pl.BlockSpec((width, chunk), lambda i: (0, i)),
-            pl.BlockSpec((chunk, width), lambda i: (i, 0)),
+            pl.BlockSpec((width, part), lambda i: (0, i)),
+            pl.BlockSpec((part, width), lambda i: (i, 0)),
         ),
         compiler_params=params(24),
         cost_estimate=pl.CostEstimate(

time: 68.5 us -> 68.4 us (level)
  no operation moved by 1% of the time
where the time goes in v5:
time: 68.4 us; the launch traced here: 68.1 us
  Pallas kernels  43.9 us (64%)
  blocking collectives  19.9 us (29%)
  starting transfers between devices  3.7 us (5%)
    pallas_call x1, Pallas kernels, per_device(): pl.pallas_call(functools.partial(forward_kernel, steps), out_shape=(pltpu...  24.8 us
    all_to_all x1, blocking collectives, per_device(): lax.all_to_all(send, 'expert', split_axis=0, concat_axis=0, tiled=True)  19.9 us
    pallas_call x1, Pallas kernels, per_device(): pl.pallas_call(grads_kernel, grid=(2 * steps,), out_shape=(jax.ShapeDtype...  15.2 us
    all_to_all x1, starting transfers between devices, per_device(): lax.all_to_all(ret.reshape(rows // PAIR, PAIR, width), 'expert', split_ax...  3.7 us
    pallas_call x1, Pallas kernels, per_device(): pl.pallas_call(dispatch_kernel, out_shape=(pltpu.VMEM((slots, width), low...  2.41 us
    pallas_call x1, Pallas kernels, per_device(): pl.pallas_call(combine_kernel, out_shape=(jax.ShapeDtypeStruct((count, wi...  1.51 us
  transfers between devices with their start and end apart: 1, of which 0 were waited for; matrix products, arithmetic and copies ran while one was open for 0% of the time, Pallas kernels for 22%

profile of v5, /device:TPU:0, one launch (start us, length us, event | category | flops | bytes accessed | tf_op | source)
XLA Modules:
  0.0 68.1 jit_solution(8003009071548098807)
XLA Ops:
  0.6 2.4 %dispatch.1 = (bf16[128,1664]{1,0:T(8,128)(2,1)S(1)}, f32[8,128]{1,0:T(8,128)S(1)}) custom-call(s32[2,128]{1,0:T(2,128)} %bitcast.16, s32[1,128]{1,0:T(1,128)} %prio_ref.1, f32[2,128]{1,0:T(2,128)} %bitcast.17, bf16[128,1664]{1,0:T(8,128)(2,1)} %tok_hbm.1, bf16[128,1664]{1,0:T(8,128)(2,1)} %cot_ref.1), custom_call_target="tpu_custom_call" | custom-call | tf_op jit(solution)/shard_map/dispatch/pallas_call | solution.py:257
  3.1 19.9 %all_to_all.10 = bf16[16,8,1664]{2,1,0:T(8,128)(2,1)S(1)} all-to-all(bf16[16,8,1664]{2,1,0:T(8,128)(2,1)S(1)} %bitcast.13), channel_id=1, replica_groups=mesh['groups'=2,'expert'=16] {'expert'}, dimensions={0} | all-to-all | bytes 851968 | tf_op jit(solution)/shard_map/all_to_all | solution.py:273
  23.0 0.0 copy-start
  23.0 24.8 %forward.1 = (bf16[128,1664]{1,0:T(8,128)(2,1)}, bf16[1664,64]{1,0:T(8,128)(2,1)S(1)}, bf16[64,1664]{1,0:T(8,128)(2,1)S(1)}, bf16[6,64,1024]{2,1,0:T(8,128)(2,1)...) custom-call(bf16[128,1664]{1,0:T(8,128)(2,1)S(1)} %bitcast.11, ...), custom_call_target="tpu_custom_call" | custom-call | flops 5234491392 | bytes 40894464 | tf_op jit(solution)/shard_map/forward/pallas_call | solution.py:280
  47.7 3.7 %all-to-all-start.1 = ((bf16[16,8,1664]{2,1,0:T(8,128)(2,1)}), bf16[16,8,1664]{2,1,0:T(8,128)(2,1)S(1)}, u32[]{:S(2)}, u32[]{:S(2)}) async-start(bf16[16,8,1664]{2,1,0:T(8,128)(2,1)} %bitcast.6), calls=%async_computation.1 | async-start | bytes 851968 | tf_op jit(solution)/shard_map/all_to_all | solution.py:310
  51.5 15.2 %grads.1 = (bf16[1664,6144]{1,0:T(8,128)(2,1)}, bf16[6144,1664]{1,0:T(8,128)(2,1)}) custom-call(bf16[1664,64]{1,0:T(8,128)(2,1)S(1)} %get-tuple-element.27.x_t_ref, bf16[64,1664]{1,0:T(8,128)(2,1)S(1)} %get-tuple-element.28.g_ref, bf16[6,64,1024]{2,1,0:T(8,128)(2,1)S(1)} %get-tuple-element.29.act_ref, bf16[6,64,1024]{2,1,0:T(8,128)(2,1)S(1)} %get-tuple-element.30.d_pre_ref), custom_call_target="tpu_custom_call" | custom-call | flops 2617245696 | bytes 40894464 | tf_op jit(solution)/shard_map/grads/pallas_call | solution.py:313
  66.6 0.0 all-to-all-done.1
  66.6 0.0 copy-done
  66.6 1.5 %combine.1 = (bf16[128,1664]{1,0:T(8,128)(2,1)}, bf16[128,1664]{1,0:T(8,128)(2,1)}, f32[2,128]{1,0:T(2,128)}) custom-call(bf16[128,1664]{1,0:T(8,128)(2,1)S(1)} %bitcast.12, bf16[384,128]{1,0:T(8,128)(2,1)S(1)} %get-tuple-element.22.pick_ref, f32[128,8]{1,0:T(8,128)S(1)} %get-tuple-element.23.gate_ref, bf16[128,1664]{1,0:T(8,128)(2,1)S(1)} %copy-done), custom_call_target="tpu_custom_call" | custom-call | tf_op jit(solution)/shard_map/combine/pallas_call | solution.py:338
Async XLA Ops:
  23.0 43.7 %copy-start = (bf16[128,1664]{1,0:T(8,128)(2,1)S(1)}, bf16[128,1664]{1,0:T(8,128)(2,1)}, u32[]{:S(2)}) copy-start(bf16[128,1664]{1,0:T(8,128)(2,1)} %cot_ref.1) | copy-start | bytes 1277956
  47.7 18.9 %all-to-all-start.1 = ((bf16[16,8,1664]{2,1,0:T(8,128)(2,1)}), bf16[16,8,1664]{2,1,0:T(8,128)(2,1)S(1)}, u32[]{:S(2)}, u32[]{:S(2)}) async-start(bf16[16,8,1664]{2,1,0:T(8,128)(2,1)} %bitcast.6), calls=%async_computation.1 | async-start | bytes 851968 | tf_op jit(solution)/shard_map/all_to_all | solution.py:310

commit v6 on v5

--- a/solution.py
+++ b/solution.py
@@ -115,88 +115,157 @@
 
 def forward_kernel(
     steps, recv_ref, plan_ref, w_in_hbm, w_out_hbm,
-    ret_ref, x_t_ref, g_ref, act_ref, d_pre_ref, pick_ref, gate_ref,
-    w_in_ref, w_out_ref, x_ref, out_acc, back_acc, sem_in, sem_out,
+    ret_ref, x_t_ref, d_pre_ref, pick_ref, gate_ref, d_out_hbm,
+    w_in_ref, w_out_ref, x_ref, g_ref, act_ref, act_t_ref, stage, out_acc, back_acc,
+    sem_in, sem_out, sem_left,
 ):
-    depth = w_in_ref.shape[2]
-
-    part = depth // 2
-
-    def copies(step, first, size, slot):
-        cols = pl.ds(pl.multiple_of(step * depth + first, size), size)
-        near = pl.ds(first, size)
+    width, depth = w_in_ref.shape[1:]
+    low = jnp.bfloat16
+
+    def copies(step):
+        cols = pl.ds(pl.multiple_of(step * depth, depth), depth)
         return (
-            pltpu.make_async_copy(
-                w_in_hbm.at[:, cols], w_in_ref.at[step, :, near], sem_in.at[slot]
-            ),
-            pltpu.make_async_copy(
-                w_out_hbm.at[cols, :], w_out_ref.at[step, near, :], sem_out.at[slot]
-            ),
+            pltpu.make_async_copy(w_in_hbm.at[:, cols], w_in_ref.at[step], sem_in.at[step]),
+            pltpu.make_async_copy(w_out_hbm.at[cols, :], w_out_ref.at[step], sem_out.at[step]),
         )
 
-    opening = [copies(0, 0, part, 0), copies(0, part, part, steps)]
-    for pair in opening:
-        for copy in pair:
-            copy.start()
+    def leave(step):
+        rows = pl.ds(pl.multiple_of(step * depth, depth), depth)
+        slot = lax.rem(step, 2)
+        return pltpu.make_async_copy(stage.at[slot], d_out_hbm.at[rows, :], sem_left.at[slot])
 
     def begin(step, carry):
-        for copy in copies(step, 0, depth, step):
+        for copy in copies(step):
             copy.start()
         return carry
 
-    lax.fori_loop(1, steps, begin, 0)
+    lax.fori_loop(0, steps, begin, 0)
     recv = recv_ref[...]
     x_pick, g_pick = row_picks(recv.shape[0])
     x_rows = jnp.dot(x_pick, recv, preferred_element_type=jnp.float32)
-    x_ref[...] = x_rows.astype(jnp.bfloat16)
-    x_t_ref[...] = jnp.transpose(x_rows, (1, 0)).astype(jnp.bfloat16)
-    g_ref[...] = jnp.dot(g_pick, recv, preferred_element_type=jnp.float32).astype(jnp.bfloat16)
+    x_ref[...] = x_rows.astype(low)
+    x_t_ref[...] = jnp.transpose(x_rows, (1, 0)).astype(low)
+    g_ref[...] = jnp.dot(g_pick, recv, preferred_element_type=jnp.float32).astype(low)
     tables(plan_ref, pick_ref, gate_ref)
     out_acc[...] = jnp.zeros_like(out_acc)
     back_acc[...] = jnp.zeros_like(back_acc)
 
-    def front(step, cols):
-        pre = jnp.dot(x_ref[...], w_in_ref[step, :, cols], preferred_element_type=jnp.float32)
-        d_act = lax.dot_general(
-            g_ref[...], w_out_ref[step, cols, :], LAST_DIM, preferred_element_type=jnp.float32
+    def front_dots(step, found):
+        for first in range(0, depth, 256):
+            cols = slice(first, min(first + 256, depth))
+            pre = []
+
+            def one(cols=cols, pre=pre):
+                pre.append(
+                    jnp.dot(
+                        x_ref[...], w_in_ref[step, :, cols], preferred_element_type=jnp.float32
+                    )
+                )
+
+            def two(cols=cols, pre=pre):
+                d_act = lax.dot_general(
+                    g_ref[...],
+                    w_out_ref[step, cols, :],
+                    LAST_DIM,
+                    preferred_element_type=jnp.float32,
+                )
+                found.append((cols, pre[0], d_act))
+
+            yield one
+            yield two
+
+    def back_dots(step, act, d_pre):
+        for first in range(0, width, 256):
+            cols = slice(first, min(first + 256, width))
+
+            def one(cols=cols):
+                out_acc[:, cols] += jnp.dot(
+                    act, w_out_ref[step, :, cols], preferred_element_type=jnp.float32
+                )
+
+            def two(cols=cols):
+                back_acc[:, cols] += lax.dot_general(
+                    d_pre,
+                    w_in_ref[step, cols, :],
+                    LAST_DIM,
+                    preferred_element_type=jnp.float32,
+                )
+
+            yield one
+            yield two
+
+    def grad_dots(step, act_t):
+        slot = lax.rem(step, 2)
+        for first in range(0, width, 256):
+            cols = slice(first, min(first + 256, width))
+            for top in range(0, depth, 256):
+                rows = slice(top, min(top + 256, depth))
+
+                def one(cols=cols, rows=rows):
+                    stage[slot, rows, cols] = jnp.dot(
+                        act_t[rows], g_ref[:, cols], preferred_element_type=jnp.float32
+                    ).astype(low)
+
+                yield one
+
+    def middle(step, found):
+        for cols, pre, d_act in found:
+            value, slope = gelu_parts(pre)
+            act_ref[:, cols] = value.astype(low)
+            act_t_ref[cols, :] = jnp.transpose(value, (1, 0)).astype(low)
+            d_pre_ref[step, :, cols] = (d_act * slope).astype(low)
+
+    def arrive(step):
+        for copy in copies(step):
+            copy.wait()
+
+    def run(first, second):
+        done = 0
+        for index, thunk in enumerate(first):
+            thunk()
+            due = (index + 1) * len(second) // len(first)
+            for other in second[done:due]:
+                other()
+            done = due
+
+    arrive(0)
+    found = []
+    for thunk in front_dots(0, found):
+        thunk()
+    middle(0, found)
+
+    def body(step, carry):
+        arrive(step)
+
+        @pl.when(step > 2)
+        def _():
+            leave(step - 3).wait()
+
+        act, act_t, d_pre = act_ref[...], act_t_ref[...], d_pre_ref[step - 1]
+        found = []
+        run(
+            [*front_dots(step, found), *back_dots(step - 1, act, d_pre)],
+            [*grad_dots(step - 1, act_t)],
         )
-        return pre, d_act
-
-    def middle(step, cols, pre, d_act):
-        value, slope = gelu_parts(pre)
-        act_ref[step, :, cols] = value.astype(jnp.bfloat16)
-        d_pre_ref[step, :, cols] = (d_act * slope).astype(jnp.bfloat16)
-
-    def back(step, act, d_pre):
-        out_acc[...] += jnp.dot(act, w_out_ref[step], preferred_element_type=jnp.float32)
-        back_acc[...] += lax.dot_general(
-            d_pre, w_in_ref[step], LAST_DIM, preferred_element_type=jnp.float32
-        )
-
-    for first, pair in zip((0, part), opening):
-        for copy in pair:
-            copy.wait()
-        cols = slice(first, first + part)
-        middle(0, cols, *front(0, cols))
-
-    def body(step, carry):
-        for copy in copies(step, 0, depth, step):
-            copy.wait()
-        cols = slice(0, depth)
-        act, d_pre = act_ref[step - 1], d_pre_ref[step - 1]
-        found = front(step, cols)
-        back(step - 1, act, d_pre)
-        middle(step, cols, *found)
+        middle(step, found)
+        leave(step - 1).start()
         return carry
 
     lax.fori_loop(1, steps, body, 0)
-    back(steps - 1, act_ref[steps - 1], d_pre_ref[steps - 1])
+    last = steps - 1
+    if steps > 2:
+        leave(last - 2).wait()
+    run([*back_dots(last, act_ref[...], d_pre_ref[last])], [*grad_dots(last, act_t_ref[...])])
+    leave(last).start()
     ret = lax.dot_general(
-        x_pick, out_acc[...].astype(jnp.bfloat16), ROWS_DIM, preferred_element_type=jnp.float32
+        x_pick, out_acc[...].astype(low), ROWS_DIM, preferred_element_type=jnp.float32
     ) + lax.dot_general(
-        g_pick, back_acc[...].astype(jnp.bfloat16), ROWS_DIM, preferred_element_type=jnp.float32
+        g_pick, back_acc[...].astype(low), ROWS_DIM, preferred_element_type=jnp.float32
     )
-    ret_ref[...] = ret.astype(jnp.bfloat16)
+    ret_ref[...] = ret.astype(low)
+    if steps > 1:
+        leave(last - 1).wait()
+    leave(last).wait()
 
 
 def product(out_ref, left, right, tall, wide):
@@ -210,10 +279,8 @@
             ).astype(jnp.bfloat16)
 
 
-def grads_kernel(x_t_ref, g_ref, act_ref, d_pre_ref, d_in_ref, d_out_ref):
-    act_t = jnp.transpose(act_ref[0].astype(jnp.float32), (1, 0)).astype(jnp.bfloat16)
-    product(d_in_ref, x_t_ref[...], d_pre_ref[0], 416, 256)
-    product(d_out_ref, act_t, g_ref[...], 512, 256)
+def grads_kernel(x_t_ref, d_pre_ref, d_in_ref):
+    product(d_in_ref, x_t_ref[...], d_pre_ref[0], 208, 256)
 
 
 def combine_kernel(ret_ref, pick_ref, gate_ref, cot_ref, mixed_ref, d_tok_ref, d_gate_ref):
@@ -274,35 +341,38 @@
     rows = recv.shape[0] * PAIR
     recv = recv.reshape(rows, width)
     half = rows // 2
-    chunk = chunk_of(hidden, 1024)
+    chunk = chunk_of(hidden, 512)
     steps = hidden // chunk
-    part = chunk // 2
-    ret, x_t, g_rows, act, d_pre, pick, gate_cols = pl.pallas_call(
+    ret, x_t, d_pre, pick, gate_cols, d_w_out = pl.pallas_call(
         functools.partial(forward_kernel, steps),
         out_shape=(
             pltpu.VMEM((rows, width), low),
             jax.ShapeDtypeStruct((width, half), low),
-            jax.ShapeDtypeStruct((half, width), low),
-            jax.ShapeDtypeStruct((steps, half, chunk), low),
             jax.ShapeDtypeStruct((steps, half, chunk), low),
             jax.ShapeDtypeStruct((3 * count, slots), low),
             jax.ShapeDtypeStruct((count, 8), jnp.float32),
+            jax.ShapeDtypeStruct((hidden, width), low),
         ),
         in_specs=[vmem] * 2 + [hbm] * 2,
-        out_specs=(vmem,) * 7,
+        out_specs=(vmem,) * 5 + (hbm,),
         scratch_shapes=[
             pltpu.VMEM((steps, width, chunk), low),
             pltpu.VMEM((steps, chunk, width), low),
             pltpu.VMEM((half, width), low),
+            pltpu.VMEM((half, width), low),
+            pltpu.VMEM((half, chunk), low),
+            pltpu.VMEM((chunk, half), low),
+            pltpu.VMEM((2, chunk, width), low),
             pltpu.VMEM((half, width), jnp.float32),
             pltpu.VMEM((half, width), jnp.float32),
-            pltpu.SemaphoreType.DMA((steps + 1,)),
-            pltpu.SemaphoreType.DMA((steps + 1,)),
+            pltpu.SemaphoreType.DMA((steps,)),
+            pltpu.SemaphoreType.DMA((steps,)),
+            pltpu.SemaphoreType.DMA((2,)),
         ],
-        compiler_params=params(50),
+        compiler_params=params(48),
         cost_estimate=pl.CostEstimate(
-            flops=8 * half * width * hidden,
-            bytes_accessed=4 * width * hidden,
+            flops=10 * half * width * hidden,
+            bytes_accessed=6 * width * hidden,
             transcendentals=half * hidden,
         ),
         name="forward",
@@ -310,31 +380,23 @@
     ret = lax.all_to_all(
         ret.reshape(rows // PAIR, PAIR, width), "expert", split_axis=0, concat_axis=0, tiled=True
     ).reshape(rows, width)
-    d_w_in, d_w_out = pl.pallas_call(
+    d_w_in = pl.pallas_call(
         grads_kernel,
-        grid=(2 * steps,),
-        out_shape=(
-            jax.ShapeDtypeStruct((width, hidden), low),
-            jax.ShapeDtypeStruct((hidden, width), low),
-        ),
+        grid=(steps,),
+        out_shape=jax.ShapeDtypeStruct((width, hidden), low),
         in_specs=[
             pl.BlockSpec((width, half), lambda i: (0, 0)),
-            pl.BlockSpec((half, width), lambda i: (0, 0)),
-            pl.BlockSpec((1, half, part), lambda i: (i // 2, 0, i % 2)),
-            pl.BlockSpec((1, half, part), lambda i: (i // 2, 0, i % 2)),
+            pl.BlockSpec((1, half, chunk), lambda i: (i, 0, 0)),
         ],
-        out_specs=(
-            pl.BlockSpec((width, part), lambda i: (0, i)),
-            pl.BlockSpec((part, width), lambda i: (i, 0)),
-        ),
+        out_specs=pl.BlockSpec((width, chunk), lambda i: (0, i)),
         compiler_params=params(24),
         cost_estimate=pl.CostEstimate(
-            flops=4 * half * width * hidden,
-            bytes_accessed=4 * width * hidden,
+            flops=2 * half * width * hidden,
+            bytes_accessed=2 * width * hidden,
             transcendentals=0,
         ),
         name="grads",
-    )(x_t, g_rows, act, d_pre)
+    )(x_t, d_pre)
     mixed, d_tokens, d_gates_t = pl.pallas_call(
         combine_kernel,
         out_shape=(

time: 68.4 us -> 68.4 us (level)
  Pallas kernels: 43.9 us -> 42.2 us
  waiting for transfers between devices: 0.01 us -> 1.51 us
    pallas_call x1, Pallas kernels: 15.2 us -> 11.2 us  [per_device(): pl.pallas_call(grads_kernel, grid=(steps,), out_shape=jax.ShapeDtypeStruc...]
    pallas_call x1, Pallas kernels: 24.8 us -> 27 us  [per_device(): pl.pallas_call(functools.partial(forward_kernel, steps), out_shape=(pltpu...]
    all_to_all x1, waiting for transfers between devices: 0.01 us -> 1.51 us  [per_device(): lax.all_to_all(ret.reshape(rows // PAIR, PAIR, width), 'expert', split_ax...]
  transfers between devices with their start and end apart: 1 -> 1, of which waited for: 0 -> 1; matrix products, arithmetic and copies ran while one was open for 0% -> 0% of each run, Pallas kernels for 22% -> 16%
where the time goes in v6:
time: 68.4 us; the launch traced here: 68.1 us
  Pallas kernels  42.2 us (62%)
  blocking collectives  19.9 us (29%)
  starting transfers between devices  3.84 us (6%)
  waiting for transfers between devices  1.51 us (2%)
    pallas_call x1, Pallas kernels, per_device(): pl.pallas_call(functools.partial(forward_kernel, steps), out_shape=(pltpu...  27 us
    all_to_all x1, blocking collectives, per_device(): lax.all_to_all(send, 'expert', split_axis=0, concat_axis=0, tiled=True)  19.9 us
    pallas_call x1, Pallas kernels, per_device(): pl.pallas_call(grads_kernel, grid=(steps,), out_shape=jax.ShapeDtypeStruc...  11.2 us
    all_to_all x1, starting transfers between devices, per_device(): lax.all_to_all(ret.reshape(rows // PAIR, PAIR, width), 'expert', split_ax...  3.84 us
    pallas_call x1, Pallas kernels, per_device(): pl.pallas_call(dispatch_kernel, out_shape=(pltpu.VMEM((slots, width), low...  2.41 us
    all_to_all x1, waiting for transfers between devices, per_device(): lax.all_to_all(ret.reshape(rows // PAIR, PAIR, width), 'expert', split_ax...  1.51 us
    pallas_call x1, Pallas kernels, per_device(): pl.pallas_call(combine_kernel, out_shape=(jax.ShapeDtypeStruct((count, wi...  1.51 us
  transfers between devices with their start and end apart: 1, of which 1 were waited for; matrix products, arithmetic and copies ran while one was open for 0% of the time, Pallas kernels for 16%

profile of v6, /device:TPU:0, one launch (start us, length us, event | category | flops | bytes accessed | tf_op | source)
XLA Modules:
  0.0 68.1 jit_solution(9959475139095320254)
XLA Ops:
  0.6 2.4 %dispatch.1 = (bf16[128,1664]{1,0:T(8,128)(2,1)S(1)}, f32[8,128]{1,0:T(8,128)S(1)}) custom-call(s32[2,128]{1,0:T(2,128)} %bitcast.17, s32[1,128]{1,0:T(1,128)} %prio_ref.1, f32[2,128]{1,0:T(2,128)} %bitcast.18, bf16[128,1664]{1,0:T(8,128)(2,1)} %tok_hbm.1, bf16[128,1664]{1,0:T(8,128)(2,1)} %cot_ref.1), custom_call_target="tpu_custom_call" | custom-call | tf_op jit(solution)/shard_map/dispatch/pallas_call | solution.py:324
  3.1 19.9 %all_to_all.10 = bf16[16,8,1664]{2,1,0:T(8,128)(2,1)S(1)} all-to-all(bf16[16,8,1664]{2,1,0:T(8,128)(2,1)S(1)} %bitcast.13), channel_id=1, replica_groups=mesh['groups'=2,'expert'=16] {'expert'}, dimensions={0} | all-to-all | bytes 851968 | tf_op jit(solution)/shard_map/all_to_all | solution.py:340
  23.0 27.0 %forward.1 = (bf16[128,1664]{1,0:T(8,128)(2,1)}, bf16[1664,64]{1,0:T(8,128)(2,1)S(1)}, bf16[12,64,512]{2,1,0:T(8,128)(2,1)S(1)}, bf16[384,128]{1,0:T(8,128)(2,1)...) custom-call(bf16[128,1664]{1,0:T(8,128)(2,1)S(1)} %bitcast.11, f32[8,128]{1,0:T(8,128)S(1)} %get-tuple-element.17.plan_ref, ...), custom_call_target="tpu_custom_call" | custom-call | flops 6543114240 | bytes 61341696 | tf_op jit(solution)/shard_map/forward/pallas_call | solution.py:346
  50.0 0.0 copy-start
  50.0 3.8 %all-to-all-start.1 = ((bf16[16,8,1664]{2,1,0:T(8,128)(2,1)}), bf16[16,8,1664]{2,1,0:T(8,128)(2,1)S(1)}, u32[]{:S(2)}, u32[]{:S(2)}) async-start(bf16[16,8,1664]{2,1,0:T(8,128)(2,1)} %bitcast.6), calls=%async_computation.1 | async-start | bytes 851968 | tf_op jit(solution)/shard_map/all_to_all | solution.py:380
  53.9 11.2 %grads.1 = bf16[1664,6144]{1,0:T(8,128)(2,1)} custom-call(bf16[1664,64]{1,0:T(8,128)(2,1)S(1)} %get-tuple-element.24.x_t_ref, bf16[12,64,512]{2,1,0:T(8,128)(2,1)S(1)} %get-tuple-element.25.d_pre_ref), custom_call_target="tpu_custom_call" | custom-call | flops 1308622848 | bytes 20447232 | tf_op jit(solution)/shard_map/grads/pallas_call | solution.py:383
  65.1 1.5 %all-to-all-done.1 = bf16[16,8,1664]{2,1,0:T(8,128)(2,1)S(1)} async-done(((bf16[16,8,1664]{2,1,0:T(8,128)(2,1)}), bf16[16,8,1664]{2,1,0:T(8,128)(2,1)S(1)}, u32[]{:S(2)}, u32[]{:S(2)}) %all-to-all-start.1) | async-done | bytes 426016 | tf_op jit(solution)/shard_map/all_to_all | solution.py:380
  66.6 0.0 copy-done
  66.6 1.5 %combine.1 = (bf16[128,1664]{1,0:T(8,128)(2,1)}, bf16[128,1664]{1,0:T(8,128)(2,1)}, f32[2,128]{1,0:T(2,128)}) custom-call(bf16[128,1664]{1,0:T(8,128)(2,1)S(1)} %bitcast.12, bf16[384,128]{1,0:T(8,128)(2,1)S(1)} %get-tuple-element.19.pick_ref, f32[128,8]{1,0:T(8,128)S(1)} %get-tuple-element.20.gate_ref, bf16[128,1664]{1,0:T(8,128)(2,1)S(1)} %copy-done), custom_call_target="tpu_custom_call" | custom-call | tf_op jit(solution)/shard_map/combine/pallas_call | solution.py:400
Async XLA Ops:
  50.0 16.6 %copy-start = (bf16[128,1664]{1,0:T(8,128)(2,1)S(1)}, bf16[128,1664]{1,0:T(8,128)(2,1)}, u32[]{:S(2)}) copy-start(bf16[128,1664]{1,0:T(8,128)(2,1)} %cot_ref.1) | copy-start | bytes 1277956
  50.0 16.6 %all-to-all-start.1 = ((bf16[16,8,1664]{2,1,0:T(8,128)(2,1)}), bf16[16,8,1664]{2,1,0:T(8,128)(2,1)S(1)}, u32[]{:S(2)}, u32[]{:S(2)}) async-start(bf16[16,8,1664]{2,1,0:T(8,128)(2,1)} %bitcast.6), calls=%async_computation.1 | async-start | bytes 851968 | tf_op jit(solution)/shard_map/all_to_all | solution.py:380

commit v7 on v6

--- a/solution.py
+++ b/solution.py
@@ -115,9 +115,8 @@
 
 def forward_kernel(
     steps, recv_ref, plan_ref, w_in_hbm, w_out_hbm,
-    ret_ref, x_t_ref, d_pre_ref, pick_ref, gate_ref, d_out_hbm,
-    w_in_ref, w_out_ref, x_ref, g_ref, act_ref, act_t_ref, stage, out_acc, back_acc,
-    sem_in, sem_out, sem_left,
+    ret_ref, x_t_ref, g_ref, act_t_ref, d_pre_ref, pick_ref, gate_ref,
+    w_in_ref, w_out_ref, x_ref, act_ref, out_acc, back_acc, sem_in, sem_out,
 ):
     width, depth = w_in_ref.shape[1:]
     low = jnp.bfloat16
@@ -128,11 +127,6 @@
             pltpu.make_async_copy(w_in_hbm.at[:, cols], w_in_ref.at[step], sem_in.at[step]),
             pltpu.make_async_copy(w_out_hbm.at[cols, :], w_out_ref.at[step], sem_out.at[step]),
         )
-
-    def leave(step):
-        rows = pl.ds(pl.multiple_of(step * depth, depth), depth)
-        slot = lax.rem(step, 2)
-        return pltpu.make_async_copy(stage.at[slot], d_out_hbm.at[rows, :], sem_left.at[slot])
 
     def begin(step, carry):
         for copy in copies(step):
@@ -194,39 +188,16 @@
             yield one
             yield two
 
-    def grad_dots(step, act_t):
-        slot = lax.rem(step, 2)
-        for first in range(0, width, 256):
-            cols = slice(first, min(first + 256, width))
-            for top in range(0, depth, 256):
-                rows = slice(top, min(top + 256, depth))
-
-                def one(cols=cols, rows=rows):
-                    stage[slot, rows, cols] = jnp.dot(
-                        act_t[rows], g_ref[:, cols], preferred_element_type=jnp.float32
-                    ).astype(low)
-
-                yield one
-
     def middle(step, found):
         for cols, pre, d_act in found:
             value, slope = gelu_parts(pre)
             act_ref[:, cols] = value.astype(low)
-            act_t_ref[cols, :] = jnp.transpose(value, (1, 0)).astype(low)
+            act_t_ref[step, cols, :] = jnp.transpose(value, (1, 0)).astype(low)
             d_pre_ref[step, :, cols] = (d_act * slope).astype(low)
 
     def arrive(step):
         for copy in copies(step):
             copy.wait()
-
-    def run(first, second):
-        done = 0
-        for index, thunk in enumerate(first):
-            thunk()
-            due = (index + 1) * len(second) // len(first)
-            for other in second[done:due]:
-                other()
-            done = due
 
     arrive(0)
     found = []
@@ -236,36 +207,22 @@
 
     def body(step, carry):
         arrive(step)
-
-        @pl.when(step > 2)
-        def _():
-            leave(step - 3).wait()
-
-        act, act_t, d_pre = act_ref[...], act_t_ref[...], d_pre_ref[step - 1]
+        act, d_pre = act_ref[...], d_pre_ref[step - 1]
         found = []
-        run(
-            [*front_dots(step, found), *back_dots(step - 1, act, d_pre)],
-            [*grad_dots(step - 1, act_t)],
-        )
+        for thunk in [*front_dots(step, found), *back_dots(step - 1, act, d_pre)]:
+            thunk()
         middle(step, found)
-        leave(step - 1).start()
         return carry
 
     lax.fori_loop(1, steps, body, 0)
-    last = steps - 1
-    if steps > 2:
-        leave(last - 2).wait()
-    run([*back_dots(last, act_ref[...], d_pre_ref[last])], [*grad_dots(last, act_t_ref[...])])
-    leave(last).start()
+    for thunk in back_dots(steps - 1, act_ref[...], d_pre_ref[steps - 1]):
+        thunk()
     ret = lax.dot_general(
         x_pick, out_acc[...].astype(low), ROWS_DIM, preferred_element_type=jnp.float32
     ) + lax.dot_general(
         g_pick, back_acc[...].astype(low), ROWS_DIM, preferred_element_type=jnp.float32
     )
     ret_ref[...] = ret.astype(low)
-    if steps > 1:
-        leave(last - 1).wait()
-    leave(last).wait()
 
 
 def product(out_ref, left, right, tall, wide):
@@ -279,8 +236,48 @@
             ).astype(jnp.bfloat16)
 
 
-def grads_kernel(x_t_ref, d_pre_ref, d_in_ref):
-    product(d_in_ref, x_t_ref[...], d_pre_ref[0], 208, 256)
+def grads_kernel(
+    x_t_ref, g_ref, act_t_ref, d_pre_ref, d_in_hbm, d_out_hbm, d_in_stage, d_out_stage, sem
+):
+    steps, depth = act_t_ref.shape[:2]
+    width = x_t_ref.shape[0]
+    slots = d_in_stage.shape[0]
+
+    def leave(step):
+        slot = lax.rem(step, slots)
+        cols = pl.ds(pl.multiple_of(step * depth, depth), depth)
+        pairs = []
+        for index in range(2):
+            some = pl.ds(index * (width // 2), width // 2)
+            pairs.append((d_in_stage.at[slot, some], d_in_hbm.at[some, cols]))
+        for index in range(2):
+            here = pl.ds(index * (depth // 2), depth // 2)
+            there = pl.ds(pl.multiple_of(step * depth + index * (depth // 2), 64), depth // 2)
+            pairs.append((d_out_stage.at[slot, here], d_out_hbm.at[there]))
+        return [
+            pltpu.make_async_copy(*pair, sem.at[slot, index]) for index, pair in enumerate(pairs)
+        ]
+
+    def work(step, carry):
+        @pl.when(step >= slots)
+        def _():
+            for copy in leave(step - slots):
+                copy.wait()
+
+        slot = lax.rem(step, slots)
+        copies = leave(step)
+        product(d_in_stage.at[slot], x_t_ref[...], d_pre_ref[step], 208, 256)
+        for copy in copies[:2]:
+            copy.start()
+        product(d_out_stage.at[slot], act_t_ref[step], g_ref[...], 256, 256)
+        for copy in copies[2:]:
+            copy.start()
+        return carry
+
+    lax.fori_loop(0, steps, work, 0)
+    for step in range(max(steps - slots, 0), steps):
+        for copy in leave(step):
+            copy.wait()
 
 
 def combine_kernel(ret_ref, pick_ref, gate_ref, cot_ref, mixed_ref, d_tok_ref, d_gate_ref):
@@ -343,36 +340,33 @@
     half = rows // 2
     chunk = chunk_of(hidden, 512)
     steps = hidden // chunk
-    ret, x_t, d_pre, pick, gate_cols, d_w_out = pl.pallas_call(
+    ret, x_t, g_rows, act_t, d_pre, pick, gate_cols = pl.pallas_call(
         functools.partial(forward_kernel, steps),
         out_shape=(
             pltpu.VMEM((rows, width), low),
             jax.ShapeDtypeStruct((width, half), low),
+            jax.ShapeDtypeStruct((half, width), low),
+            jax.ShapeDtypeStruct((steps, chunk, half), low),
             jax.ShapeDtypeStruct((steps, half, chunk), low),
             jax.ShapeDtypeStruct((3 * count, slots), low),
             jax.ShapeDtypeStruct((count, 8), jnp.float32),
-            jax.ShapeDtypeStruct((hidden, width), low),
         ),
         in_specs=[vmem] * 2 + [hbm] * 2,
-        out_specs=(vmem,) * 5 + (hbm,),
+        out_specs=(vmem,) * 7,
         scratch_shapes=[
             pltpu.VMEM((steps, width, chunk), low),
             pltpu.VMEM((steps, chunk, width), low),
             pltpu.VMEM((half, width), low),
-            pltpu.VMEM((half, width), low),
             pltpu.VMEM((half, chunk), low),
-            pltpu.VMEM((chunk, half), low),
-            pltpu.VMEM((2, chunk, width), low),
             pltpu.VMEM((half, width), jnp.float32),
             pltpu.VMEM((half, width), jnp.float32),
             pltpu.SemaphoreType.DMA((steps,)),
             pltpu.SemaphoreType.DMA((steps,)),
-            pltpu.SemaphoreType.DMA((2,)),
         ],
-        compiler_params=params(48),
+        compiler_params=params(46),
         cost_estimate=pl.CostEstimate(
-            flops=10 * half * width * hidden,
-            bytes_accessed=6 * width * hidden,
+            flops=8 * half * width * hidden,
+            bytes_accessed=4 * width * hidden,
             transcendentals=half * hidden,
         ),
         name="forward",
@@ -380,23 +374,27 @@
     ret = lax.all_to_all(
         ret.reshape(rows // PAIR, PAIR, width), "expert", split_axis=0, concat_axis=0, tiled=True
     ).reshape(rows, width)
-    d_w_in = pl.pallas_call(
+    d_w_in, d_w_out = pl.pallas_call(
         grads_kernel,
-        grid=(steps,),
-        out_shape=jax.ShapeDtypeStruct((width, hidden), low),
-        in_specs=[
-            pl.BlockSpec((width, half), lambda i: (0, 0)),
-            pl.BlockSpec((1, half, chunk), lambda i: (i, 0, 0)),
+        out_shape=(
+            jax.ShapeDtypeStruct((width, hidden), low),
+            jax.ShapeDtypeStruct((hidden, width), low),
+        ),
+        in_specs=[vmem] * 4,
+        out_specs=(hbm,) * 2,
+        scratch_shapes=[
+            pltpu.VMEM((3, width, chunk), low),
+            pltpu.VMEM((3, chunk, width), low),
+            pltpu.SemaphoreType.DMA((3, 4)),
         ],
-        out_specs=pl.BlockSpec((width, chunk), lambda i: (0, i)),
         compiler_params=params(24),
         cost_estimate=pl.CostEstimate(
-            flops=2 * half * width * hidden,
-            bytes_accessed=2 * width * hidden,
+            flops=4 * half * width * hidden,
+            bytes_accessed=4 * width * hidden,
             transcendentals=0,
         ),
         name="grads",
-    )(x_t, d_pre)
+    )(x_t, g_rows, act_t, d_pre)
     mixed, d_tokens, d_gates_t = pl.pallas_call(
         combine_kernel,
         out_shape=(

time: 68.4 us -> 69.7 us (1.019)
  local copies, waits for them, and re-layouts: 0.01 us -> 3.37 us
  waiting for transfers between devices: 1.51 us -> 0.01 us
    pallas_call x1, Pallas kernels: 27 us -> 23.6 us  [per_device(): pl.pallas_call(functools.partial(forward_kernel, steps), out_shape=(pltpu...]
    unnamed x2 -> x10, local copies, waits for them, and re-layouts: 0.01 us -> 3.37 us
    pallas_call x1, Pallas kernels: 11.2 us -> 14 us  [per_device(): pl.pallas_call(grads_kernel, out_shape=(jax.ShapeDtypeStruct((width, hidd...]
    all_to_all x1, waiting for transfers between devices: 1.51 us -> 0.01 us  [per_device(): lax.all_to_all(ret.reshape(rows // PAIR, PAIR, width), 'expert', split_ax...]
  transfers between devices with their start and end apart: 1 -> 1, of which waited for: 1 -> 0; matrix products, arithmetic and copies ran while one was open for 0% -> 0% of each run, Pallas kernels for 16% -> 20%
where the time goes in v7:
time: 69.7 us; the launch traced here: 69.3 us
  Pallas kernels  41.6 us (60%)
  blocking collectives  19.9 us (29%)
  starting transfers between devices  3.7 us (5%)
  local copies, waits for them, and re-layouts  3.37 us (5%)
  between operations  0.7 us (1%)
    pallas_call x1, Pallas kernels, per_device(): pl.pallas_call(functools.partial(forward_kernel, steps), out_shape=(pltpu...  23.6 us
    all_to_all x1, blocking collectives, per_device(): lax.all_to_all(send, 'expert', split_axis=0, concat_axis=0, tiled=True)  19.9 us
    pallas_call x1, Pallas kernels, per_device(): pl.pallas_call(grads_kernel, out_shape=(jax.ShapeDtypeStruct((width, hidd...  14 us
    all_to_all x1, starting transfers between devices, per_device(): lax.all_to_all(ret.reshape(rows // PAIR, PAIR, width), 'expert', split_ax...  3.7 us
    unnamed x10, local copies, waits for them, and re-layouts  3.37 us
    pallas_call x1, Pallas kernels, per_device(): pl.pallas_call(dispatch_kernel, out_shape=(pltpu.VMEM((slots, width), low...  2.41 us
    pallas_call x1, Pallas kernels, per_device(): pl.pallas_call(combine_kernel, out_shape=(jax.ShapeDtypeStruct((count, wi...  1.51 us
  transfers between devices with their start and end apart: 1, of which 0 were waited for; matrix products, arithmetic and copies ran while one was open for 0% of the time, Pallas kernels for 20%

profile of v7, /device:TPU:0, one launch (start us, length us, event | category | flops | bytes accessed | tf_op | source)
XLA Modules:
  0.0 69.3 jit_solution(6242827428936758451)
XLA Ops:
  0.6 2.4 %dispatch.1 = (bf16[128,1664]{1,0:T(8,128)(2,1)S(1)}, f32[8,128]{1,0:T(8,128)S(1)}) custom-call(s32[2,128]{1,0:T(2,128)} %bitcast.16, s32[1,128]{1,0:T(1,128)} %prio_ref.1, f32[2,128]{1,0:T(2,128)} %bitcast.17, bf16[128,1664]{1,0:T(8,128)(2,1)} %tok_hbm.1, bf16[128,1664]{1,0:T(8,128)(2,1)} %cot_ref.1), custom_call_target="tpu_custom_call" | custom-call | tf_op jit(solution)/shard_map/dispatch/pallas_call | solution.py:321
  3.1 19.9 %all_to_all.10 = bf16[16,8,1664]{2,1,0:T(8,128)(2,1)S(1)} all-to-all(bf16[16,8,1664]{2,1,0:T(8,128)(2,1)S(1)} %bitcast.13), channel_id=1, replica_groups=mesh['groups'=2,'expert'=16] {'expert'}, dimensions={0} | all-to-all | bytes 851968 | tf_op jit(solution)/shard_map/all_to_all | solution.py:337
  23.0 0.0 copy-start
  23.0 23.6 %forward.1 = (bf16[128,1664]{1,0:T(8,128)(2,1)}, bf16[1664,64]{1,0:T(8,128)(2,1)S(1)}, bf16[64,1664]{1,0:T(8,128)(2,1)S(1)}, bf16[12,512,64]{2,1,0:T(8,128)(2,1)...) custom-call(bf16[128,1664]{1,0:T(8,128)(2,1)S(1)} %bitcast.11, ...), custom_call_target="tpu_custom_call" | custom-call | flops 5234491392 | bytes 40894464 | tf_op jit(solution)/shard_map/forward/pallas_call | solution.py:343
  46.6 0.0 copy-start.1
  46.6 0.7 %copy-done.1 = bf16[1664,64]{1,0:T(8,128)(2,1)} copy-done((bf16[1664,64]{1,0:T(8,128)(2,1)}, bf16[1664,64]{1,0:T(8,128)(2,1)S(1)}, u32[]{:S(2)}) %copy-start.1) | copy-done | bytes 213016
  47.4 0.0 copy-start.3
  47.4 0.7 copy-done.3
  48.1 3.7 %all-to-all-start.1 = ((bf16[16,8,1664]{2,1,0:T(8,128)(2,1)}), bf16[16,8,1664]{2,1,0:T(8,128)(2,1)S(1)}, u32[]{:S(2)}, u32[]{:S(2)}) async-start(bf16[16,8,1664]{2,1,0:T(8,128)(2,1)} %bitcast.6), calls=%async_computation.1 | async-start | bytes 851968 | tf_op jit(solution)/shard_map/all_to_all | solution.py:374
  51.8 0.0 copy-start.2
  51.8 1.0 %copy-done.2 = bf16[1664,64]{1,0:T(8,128)(2,1)S(1)} copy-done((bf16[1664,64]{1,0:T(8,128)(2,1)S(1)}, bf16[1664,64]{1,0:T(8,128)(2,1)}, u32[]{:S(2)}) %copy-start.2) | copy-done | bytes 213016
  52.8 0.0 copy-start.4
  52.8 0.9 %copy-done.4 = bf16[64,1664]{1,0:T(8,128)(2,1)S(1)} copy-done((bf16[64,1664]{1,0:T(8,128)(2,1)S(1)}, bf16[64,1664]{1,0:T(8,128)(2,1)}, u32[]{:S(2)}) %copy-start.4) | copy-done | bytes 213016
  53.7 14.0 %grads.1 = (bf16[1664,6144]{1,0:T(8,128)(2,1)}, bf16[6144,1664]{1,0:T(8,128)(2,1)}) custom-call(bf16[1664,64]{1,0:T(8,128)(2,1)S(1)} %copy-done.2, bf16[64,1664]{1,0:T(8,128)(2,1)S(1)} %copy-done.4, bf16[12,512,64]{2,1,0:T(8,128)(2,1)S(1)} %get-tuple-element.29.act_t_ref, bf16[12,64,512]{2,1,0:T(8,128)(2,1)S(1)} %get-tuple-element.30.d_pre_ref), custom_call_target="tpu_custom_call" | custom-call | flops 2617245696 | bytes 40894464 | tf_op jit(solution)/shard_map/grads/pallas_call | solution.py:377
  67.8 0.0 all-to-all-done.1
  67.8 0.0 copy-done
  67.8 1.5 %combine.1 = (bf16[128,1664]{1,0:T(8,128)(2,1)}, bf16[128,1664]{1,0:T(8,128)(2,1)}, f32[2,128]{1,0:T(2,128)}) custom-call(bf16[128,1664]{1,0:T(8,128)(2,1)S(1)} %bitcast.12, bf16[384,128]{1,0:T(8,128)(2,1)S(1)} %get-tuple-element.22.pick_ref, f32[128,8]{1,0:T(8,128)S(1)} %get-tuple-element.23.gate_ref, bf16[128,1664]{1,0:T(8,128)(2,1)S(1)} %copy-done), custom_call_target="tpu_custom_call" | custom-call | tf_op jit(solution)/shard_map/combine/pallas_call | solution.py:398
Async XLA Ops:
  23.0 44.8 %copy-start = (bf16[128,1664]{1,0:T(8,128)(2,1)S(1)}, bf16[128,1664]{1,0:T(8,128)(2,1)}, u32[]{:S(2)}) copy-start(bf16[128,1664]{1,0:T(8,128)(2,1)} %cot_ref.1) | copy-start | bytes 1277956
  46.6 0.8 %copy-start.1 = (bf16[1664,64]{1,0:T(8,128)(2,1)}, bf16[1664,64]{1,0:T(8,128)(2,1)S(1)}, u32[]{:S(2)}) copy-start(bf16[1664,64]{1,0:T(8,128)(2,1)S(1)} %get-tuple-element.27.x_t_ref) | copy-start | bytes 638980
  47.4 0.7 copy-start.3
  48.1 19.7 %all-to-all-start.1 = ((bf16[16,8,1664]{2,1,0:T(8,128)(2,1)}), bf16[16,8,1664]{2,1,0:T(8,128)(2,1)S(1)}, u32[]{:S(2)}, u32[]{:S(2)}) async-start(bf16[16,8,1664]{2,1,0:T(8,128)(2,1)} %bitcast.6), calls=%async_computation.1 | async-start | bytes 851968 | tf_op jit(solution)/shard_map/all_to_all | solution.py:374
  51.8 1.0 %copy-start.2 = (bf16[1664,64]{1,0:T(8,128)(2,1)S(1)}, bf16[1664,64]{1,0:T(8,128)(2,1)}, u32[]{:S(2)}) copy-start(bf16[1664,64]{1,0:T(8,128)(2,1)} %copy-done.1) | copy-start | bytes 638980
  52.8 0.9 %copy-start.4 = (bf16[64,1664]{1,0:T(8,128)(2,1)S(1)}, bf16[64,1664]{1,0:T(8,128)(2,1)}, u32[]{:S(2)}) copy-start(bf16[64,1664]{1,0:T(8,128)(2,1)} %copy-done.3) | copy-start | bytes 638980

commit v8 on v7

--- a/solution.py
+++ b/solution.py
@@ -11,6 +11,7 @@
 EXPERTS = 16
 CAP = 4
 PAIR = 2 * CAP
+EARLY = 128
 ROWS_DIM = (((0,), (0,)), ((), ()))
 LAST_DIM = (((1,), (1,)), ((), ()))
 
@@ -48,15 +49,26 @@
 
 
 def dispatch_kernel(
-    ids_ref, prio_ref, gates_ref, tok_hbm, cot_hbm, send_ref, plan_ref, both_ref, sem
+    ids_hbm, prio_hbm, gates_hbm, tok_hbm, cot_hbm, w_in_hbm, w_out_hbm,
+    send_ref, plan_ref, w_in_ref, w_out_ref,
+    ids_ref, prio_ref, gates_ref, both_ref, sem,
 ):
     count = tok_hbm.shape[0]
-    copies = (
-        pltpu.make_async_copy(tok_hbm, both_ref.at[0:count], sem.at[0]),
-        pltpu.make_async_copy(cot_hbm, both_ref.at[count:2 * count], sem.at[1]),
+    depth = w_in_ref.shape[1]
+    pairs = (
+        (ids_hbm, ids_ref),
+        (prio_hbm, prio_ref),
+        (gates_hbm, gates_ref),
+        (tok_hbm, both_ref.at[0:count]),
+        (cot_hbm, both_ref.at[count:2 * count]),
+        (w_in_hbm.at[:, 0:depth], w_in_ref),
+        (w_out_hbm.at[0:depth, :], w_out_ref),
     )
+    copies = [pltpu.make_async_copy(*pair, sem.at[index]) for index, pair in enumerate(pairs)]
     for copy in copies:
         copy.start()
+    for copy in copies[:3]:
+        copy.wait()
     place_0, place_1 = place_rows(ids_ref[...], prio_ref[...])
     rows = EXPERTS * PAIR
     row = lax.broadcasted_iota(jnp.int32, (rows, count), 0)
@@ -80,10 +92,12 @@
         ],
         axis=0,
     )
-    for copy in copies:
+    for copy in copies[3:5]:
         copy.wait()
     found = jnp.dot(pick, both_ref[...], preferred_element_type=jnp.float32)
     send_ref[...] = (found * scale).astype(jnp.bfloat16)
+    for copy in copies[5:]:
+        copy.wait()
 
 
 def tables(plan_ref, pick_ref, gate_ref):
@@ -114,37 +128,47 @@
 
 
 def forward_kernel(
-    steps, recv_ref, plan_ref, w_in_hbm, w_out_hbm,
-    ret_ref, x_t_ref, g_ref, act_t_ref, d_pre_ref, pick_ref, gate_ref,
-    w_in_ref, w_out_ref, x_ref, act_ref, out_acc, back_acc, sem_in, sem_out,
+    steps, recv_ref, plan_ref, w_in_0, w_out_0, w_in_hbm, w_out_hbm,
+    ret_ref, x_t_ref, g_ref, act_ref, d_pre_ref, pick_ref, gate_ref, d_out_hbm,
+    w_in_ref, w_out_ref, x_ref, act_t_ref, stage, out_acc, back_acc, sem_in, sem_out, sem_left,
 ):
-    width, depth = w_in_ref.shape[1:]
+    width, depth = w_in_0.shape
     low = jnp.bfloat16
 
     def copies(step):
         cols = pl.ds(pl.multiple_of(step * depth, depth), depth)
+        slot = step - 1
         return (
-            pltpu.make_async_copy(w_in_hbm.at[:, cols], w_in_ref.at[step], sem_in.at[step]),
-            pltpu.make_async_copy(w_out_hbm.at[cols, :], w_out_ref.at[step], sem_out.at[step]),
+            pltpu.make_async_copy(w_in_hbm.at[:, cols], w_in_ref.at[slot], sem_in.at[slot]),
+            pltpu.make_async_copy(w_out_hbm.at[cols, :], w_out_ref.at[slot], sem_out.at[slot]),
         )
+
+    def leave(step):
+        rows = pl.ds(pl.multiple_of(step * depth, depth), EARLY)
+        slot = lax.rem(step, 2)
+        return pltpu.make_async_copy(stage.at[slot], d_out_hbm.at[rows, :], sem_left.at[slot])
 
     def begin(step, carry):
         for copy in copies(step):
             copy.start()
         return carry
 
-    lax.fori_loop(0, steps, begin, 0)
+    lax.fori_loop(1, steps, begin, 0)
     recv = recv_ref[...]
     x_pick, g_pick = row_picks(recv.shape[0])
     x_rows = jnp.dot(x_pick, recv, preferred_element_type=jnp.float32)
     x_ref[...] = x_rows.astype(low)
-    x_t_ref[...] = jnp.transpose(x_rows, (1, 0)).astype(low)
     g_ref[...] = jnp.dot(g_pick, recv, preferred_element_type=jnp.float32).astype(low)
-    tables(plan_ref, pick_ref, gate_ref)
     out_acc[...] = jnp.zeros_like(out_acc)
     back_acc[...] = jnp.zeros_like(back_acc)
 
+    def weights(step):
+        if isinstance(step, int) and step == 0:
+            return w_in_0, w_out_0
+        return w_in_ref.at[step - 1], w_out_ref.at[step - 1]
+
     def front_dots(step, found):
+        w_first, w_second = weights(step)
         for first in range(0, depth, 256):
             cols = slice(first, min(first + 256, depth))
             pre = []
@@ -152,14 +176,14 @@
             def one(cols=cols, pre=pre):
                 pre.append(
                     jnp.dot(
-                        x_ref[...], w_in_ref[step, :, cols], preferred_element_type=jnp.float32
+                        x_ref[...], w_first[:, cols], preferred_element_type=jnp.float32
                     )
                 )
 
             def two(cols=cols, pre=pre):
                 d_act = lax.dot_general(
                     g_ref[...],
-                    w_out_ref[step, cols, :],
+                    w_second[cols, :],
                     LAST_DIM,
                     preferred_element_type=jnp.float32,
                 )
@@ -169,18 +193,19 @@
             yield two
 
     def back_dots(step, act, d_pre):
+        w_first, w_second = weights(step)
         for first in range(0, width, 256):
             cols = slice(first, min(first + 256, width))
 
             def one(cols=cols):
                 out_acc[:, cols] += jnp.dot(
-                    act, w_out_ref[step, :, cols], preferred_element_type=jnp.float32
+                    act, w_second[:, cols], preferred_element_type=jnp.float32
                 )
 
             def two(cols=cols):
                 back_acc[:, cols] += lax.dot_general(
                     d_pre,
-                    w_in_ref[step, cols, :],
+                    w_first[cols, :],
                     LAST_DIM,
                     preferred_element_type=jnp.float32,
                 )
@@ -188,41 +213,82 @@
             yield one
             yield two
 
+    def grad_dots(step, act_t):
+        slot = lax.rem(step, 2)
+        for first in range(0, width, 256):
+            cols = slice(first, min(first + 256, width))
+
+            def one(cols=cols):
+                stage[slot, :, cols] = jnp.dot(
+                    act_t, g_ref[:, cols], preferred_element_type=jnp.float32
+                ).astype(low)
+
+            yield one
+
     def middle(step, found):
         for cols, pre, d_act in found:
             value, slope = gelu_parts(pre)
-            act_ref[:, cols] = value.astype(low)
-            act_t_ref[step, cols, :] = jnp.transpose(value, (1, 0)).astype(low)
+            act_ref[step, :, cols] = value.astype(low)
             d_pre_ref[step, :, cols] = (d_act * slope).astype(low)
-
-    def arrive(step):
+            if cols.start == 0:
+                act_t_ref[...] = jnp.transpose(value[:, 0:EARLY], (1, 0)).astype(low)
+
+    def run(first, second):
+        done = 0
+        for index, thunk in enumerate(first):
+            thunk()
+            due = (index + 1) * len(second) // len(first)
+            for other in second[done:due]:
+                other()
+            done = due
+
+    def both(step):
         for copy in copies(step):
             copy.wait()
-
-    arrive(0)
+        act, act_t, d_pre = act_ref[step - 1], act_t_ref[...], d_pre_ref[step - 1]
+        found = []
+        run(
+            [*front_dots(step, found), *back_dots(step - 1, act, d_pre)],
+            [*grad_dots(step - 1, act_t)],
+        )
+        middle(step, found)
+        leave(step - 1).start()
+
     found = []
     for thunk in front_dots(0, found):
         thunk()
     middle(0, found)
+    if steps > 1:
+        both(1)
+    x_t_ref[...] = jnp.transpose(x_rows, (1, 0)).astype(low)
+    tables(plan_ref, pick_ref, gate_ref)
 
     def body(step, carry):
-        arrive(step)
-        act, d_pre = act_ref[...], d_pre_ref[step - 1]
-        found = []
-        for thunk in [*front_dots(step, found), *back_dots(step - 1, act, d_pre)]:
-            thunk()
-        middle(step, found)
+        @pl.when(step > 2)
+        def _():
+            leave(step - 3).wait()
+
+        both(step)
         return carry
 
-    lax.fori_loop(1, steps, body, 0)
-    for thunk in back_dots(steps - 1, act_ref[...], d_pre_ref[steps - 1]):
-        thunk()
+    lax.fori_loop(2, steps, body, 0)
+    last = steps - 1
+    if steps > 2:
+        leave(last - 2).wait()
+    run(
+        [*back_dots(last, act_ref[last], d_pre_ref[last])],
+        [*grad_dots(last, act_t_ref[...])],
+    )
+    leave(last).start()
     ret = lax.dot_general(
         x_pick, out_acc[...].astype(low), ROWS_DIM, preferred_element_type=jnp.float32
     ) + lax.dot_general(
         g_pick, back_acc[...].astype(low), ROWS_DIM, preferred_element_type=jnp.float32
     )
     ret_ref[...] = ret.astype(low)
+    if steps > 1:
+        leave(last - 1).wait()
+    leave(last).wait()
 
 
 def product(out_ref, left, right, tall, wide):
@@ -237,11 +303,12 @@
 
 
 def grads_kernel(
-    x_t_ref, g_ref, act_t_ref, d_pre_ref, d_in_hbm, d_out_hbm, d_in_stage, d_out_stage, sem
+    x_t_ref, g_ref, act_ref, d_pre_ref, _, d_in_hbm, d_out_hbm, d_in_stage, d_out_stage, sem
 ):
-    steps, depth = act_t_ref.shape[:2]
+    steps, _, depth = act_ref.shape
     width = x_t_ref.shape[0]
     slots = d_in_stage.shape[0]
+    later = depth - EARLY
 
     def leave(step):
         slot = lax.rem(step, slots)
@@ -251,8 +318,9 @@
             some = pl.ds(index * (width // 2), width // 2)
             pairs.append((d_in_stage.at[slot, some], d_in_hbm.at[some, cols]))
         for index in range(2):
-            here = pl.ds(index * (depth // 2), depth // 2)
-            there = pl.ds(pl.multiple_of(step * depth + index * (depth // 2), 64), depth // 2)
+            first = index * (later // 2)
+            here = pl.ds(first, later // 2)
+            there = pl.ds(pl.multiple_of(step * depth + EARLY + first, 64), later // 2)
             pairs.append((d_out_stage.at[slot, here], d_out_hbm.at[there]))
         return [
             pltpu.make_async_copy(*pair, sem.at[slot, index]) for index, pair in enumerate(pairs)
@@ -266,10 +334,11 @@
 
         slot = lax.rem(step, slots)
         copies = leave(step)
+        act_t = jnp.transpose(act_ref[step].astype(jnp.float32), (1, 0)).astype(jnp.bfloat16)
         product(d_in_stage.at[slot], x_t_ref[...], d_pre_ref[step], 208, 256)
         for copy in copies[:2]:
             copy.start()
-        product(d_out_stage.at[slot], act_t_ref[step], g_ref[...], 256, 256)
+        product(d_out_stage.at[slot], act_t[EARLY:], g_ref[...], 192, 256)
         for copy in copies[2:]:
             copy.start()
         return carry
@@ -318,59 +387,69 @@
     low = jnp.bfloat16
     vmem = pl.BlockSpec(memory_space=pltpu.VMEM)
     hbm = pl.BlockSpec(memory_space=pl.ANY)
-    send, plan = pl.pallas_call(
+    chunk = chunk_of(hidden, 512)
+    steps = hidden // chunk
+    send, plan, w_in_0, w_out_0 = pl.pallas_call(
         dispatch_kernel,
         out_shape=(
             pltpu.VMEM((slots, width), low),
             pltpu.VMEM((8, count), jnp.float32),
-        ),
-        in_specs=[vmem] * 3 + [hbm] * 2,
-        out_specs=(vmem,) * 2,
+            pltpu.VMEM((width, chunk), low),
+            pltpu.VMEM((chunk, width), low),
+        ),
+        in_specs=[hbm] * 7,
+        out_specs=(vmem,) * 4,
         scratch_shapes=[
+            pltpu.VMEM((2, count), jnp.int32),
+            pltpu.VMEM((1, count), jnp.int32),
+            pltpu.VMEM((2, count), jnp.float32),
             pltpu.VMEM((2 * count, width), low),
-            pltpu.SemaphoreType.DMA((2,)),
+            pltpu.SemaphoreType.DMA((7,)),
         ],
-        compiler_params=params(56),
+        compiler_params=params(50),
         name="dispatch",
-    )(ids_t, priority, gates_t, tokens, cotangent)
+    )(*(pltpu.with_memory_space_constraint(array, pltpu.HBM) for array in (
+        ids_t, priority, gates_t, tokens, cotangent, w_in[0], w_out[0]
+    )))
     send = jnp.tile(send.reshape(EXPERTS, PAIR, width), (repl, 1, 1))
     recv = lax.all_to_all(send, "expert", split_axis=0, concat_axis=0, tiled=True)
     rows = recv.shape[0] * PAIR
     recv = recv.reshape(rows, width)
     half = rows // 2
-    chunk = chunk_of(hidden, 512)
-    steps = hidden // chunk
-    ret, x_t, g_rows, act_t, d_pre, pick, gate_cols = pl.pallas_call(
+    ret, x_t, g_rows, act, d_pre, pick, gate_cols, d_w_out = pl.pallas_call(
         functools.partial(forward_kernel, steps),
         out_shape=(
             pltpu.VMEM((rows, width), low),
             jax.ShapeDtypeStruct((width, half), low),
             jax.ShapeDtypeStruct((half, width), low),
-            jax.ShapeDtypeStruct((steps, chunk, half), low),
+            jax.ShapeDtypeStruct((steps, half, chunk), low),
             jax.ShapeDtypeStruct((steps, half, chunk), low),
             jax.ShapeDtypeStruct((3 * count, slots), low),
             jax.ShapeDtypeStruct((count, 8), jnp.float32),
-        ),
-        in_specs=[vmem] * 2 + [hbm] * 2,
-        out_specs=(vmem,) * 7,
+            jax.ShapeDtypeStruct((hidden, width), low),
+        ),
+        in_specs=[vmem] * 4 + [hbm] * 2,
+        out_specs=(vmem,) * 7 + (hbm,),
         scratch_shapes=[
-            pltpu.VMEM((steps, width, chunk), low),
-            pltpu.VMEM((steps, chunk, width), low),
+            pltpu.VMEM((max(steps - 1, 1), width, chunk), low),
+            pltpu.VMEM((max(steps - 1, 1), chunk, width), low),
             pltpu.VMEM((half, width), low),
-            pltpu.VMEM((half, chunk), low),
+            pltpu.VMEM((EARLY, half), low),
+            pltpu.VMEM((2, EARLY, width), low),
             pltpu.VMEM((half, width), jnp.float32),
             pltpu.VMEM((half, width), jnp.float32),
-            pltpu.SemaphoreType.DMA((steps,)),
-            pltpu.SemaphoreType.DMA((steps,)),
+            pltpu.SemaphoreType.DMA((max(steps - 1, 1),)),
+            pltpu.SemaphoreType.DMA((max(steps - 1, 1),)),
+            pltpu.SemaphoreType.DMA((2,)),
         ],
-        compiler_params=params(46),
+        compiler_params=params(43),
         cost_estimate=pl.CostEstimate(
             flops=8 * half * width * hidden,
             bytes_accessed=4 * width * hidden,
             transcendentals=half * hidden,
         ),
         name="forward",
-    )(recv, plan, w_in[0], w_out[0])
+    )(recv, plan, w_in_0, w_out_0, w_in[0], w_out[0])
     ret = lax.all_to_all(
         ret.reshape(rows // PAIR, PAIR, width), "expert", split_axis=0, concat_axis=0, tiled=True
     ).reshape(rows, width)
@@ -380,11 +459,12 @@
             jax.ShapeDtypeStruct((width, hidden), low),
             jax.ShapeDtypeStruct((hidden, width), low),
         ),
-        in_specs=[vmem] * 4,
+        in_specs=[vmem] * 4 + [hbm],
         out_specs=(hbm,) * 2,
+        input_output_aliases={4: 1},
         scratch_shapes=[
             pltpu.VMEM((3, width, chunk), low),
-            pltpu.VMEM((3, chunk, width), low),
+            pltpu.VMEM((3, chunk - EARLY, width), low),
             pltpu.SemaphoreType.DMA((3, 4)),
         ],
         compiler_params=params(24),
@@ -394,7 +474,7 @@
             transcendentals=0,
         ),
         name="grads",
-    )(x_t, g_rows, act_t, d_pre)
+    )(x_t, g_rows, act, d_pre, d_w_out)
     mixed, d_tokens, d_gates_t = pl.pallas_call(
         combine_kernel,
         out_shape=(

time: 69.7 us -> 64.7 us (0.928)
  local copies, waits for them, and re-layouts: 3.37 us -> 0.01 us
  Pallas kernels: 41.6 us -> 39.7 us
    unnamed x10 -> x2, local copies, waits for them, and re-layouts: 3.37 us -> 0.01 us
    pallas_call x1, Pallas kernels: 14 us -> 12.4 us  [per_device(): pl.pallas_call(grads_kernel, out_shape=(jax.ShapeDtypeStruct((width, hidd...]
  transfers between devices with their start and end apart: 1 -> 1, of which waited for: 0 -> 1; matrix products, arithmetic and copies ran while one was open for 0% -> 0% of each run, Pallas kernels for 20% -> 19%
where the time goes in v8:
time: 64.7 us; the launch traced here: 64.4 us
  Pallas kernels  39.7 us (61%)
  blocking collectives  19.9 us (31%)
  starting transfers between devices  3.84 us (6%)
  between operations  0.67 us (1%)
    pallas_call x1, Pallas kernels, per_device(): pl.pallas_call(functools.partial(forward_kernel, steps), out_shape=(pltpu...  23.4 us
    all_to_all x1, blocking collectives, per_device(): lax.all_to_all(send, 'expert', split_axis=0, concat_axis=0, tiled=True)  19.9 us
    pallas_call x1, Pallas kernels, per_device(): pl.pallas_call(grads_kernel, out_shape=(jax.ShapeDtypeStruct((width, hidd...  12.4 us
    all_to_all x1, starting transfers between devices, per_device(): lax.all_to_all(ret.reshape(rows // PAIR, PAIR, width), 'expert', split_ax...  3.84 us
    pallas_call x1, Pallas kernels, per_device(): pl.pallas_call(dispatch_kernel, out_shape=(pltpu.VMEM((slots, width), low...  2.35 us
    pallas_call x1, Pallas kernels, per_device(): pl.pallas_call(combine_kernel, out_shape=(jax.ShapeDtypeStruct((count, wi...  1.51 us
  transfers between devices with their start and end apart: 1, of which 1 were waited for; matrix products, arithmetic and copies ran while one was open for 0% of the time, Pallas kernels for 19%

profile of v8, /device:TPU:0, one launch (start us, length us, event | category | flops | bytes accessed | tf_op | source)
XLA Modules:
  0.0 64.4 jit_solution(15235961553926133954)
XLA Ops:
  0.6 2.4 %dispatch.1 = (bf16[128,1664]{1,0:T(8,128)(2,1)S(1)}, f32[8,128]{1,0:T(8,128)S(1)}, bf16[1664,512]{1,0:T(8,128)(2,1)S(1)}, bf16[512,1664]{1,0:T(8,128)(2,1)S(1)}) custom-call(s32[2,128]{1,0:T(2,128)} %bitcast.19, s32[1,128]{1,0:T(1,128)} %prio_hbm.1, f32[2,128]{1,0:T(2,128)} %bitcast.20, bf16[128,1664]{1,0:T(8,128)(2,1)} %tok_hbm.1, ...), custom_call_target="tpu_custom_call" | custom-call | tf_op jit(solution)/shard_map/dispatch/pallas_call | solution.py:392
  3.0 19.9 %all_to_all.10 = bf16[16,8,1664]{2,1,0:T(8,128)(2,1)S(1)} all-to-all(bf16[16,8,1664]{2,1,0:T(8,128)(2,1)S(1)} %bitcast.13), channel_id=1, replica_groups=mesh['groups'=2,'expert'=16] {'expert'}, dimensions={0} | all-to-all | bytes 851968 | tf_op jit(solution)/shard_map/all_to_all | solution.py:415
  22.9 23.4 %forward.1 = (bf16[128,1664]{1,0:T(8,128)(2,1)}, bf16[1664,64]{1,0:T(8,128)(2,1)S(1)}, bf16[64,1664]{1,0:T(8,128)(2,1)S(1)}, bf16[12,64,512]{2,1,0:T(8,128)(2,1)...) custom-call(bf16[128,1664]{1,0:T(8,128)(2,1)S(1)} %bitcast.11, ...), custom_call_target="tpu_custom_call" | custom-call | flops 5234491392 | bytes 40894464 | tf_op jit(solution)/shard_map/forward/pallas_call | solution.py:419
  46.3 0.0 copy-start
  46.4 3.8 %all-to-all-start.1 = ((bf16[16,8,1664]{2,1,0:T(8,128)(2,1)}), bf16[16,8,1664]{2,1,0:T(8,128)(2,1)S(1)}, u32[]{:S(2)}, u32[]{:S(2)}) async-start(bf16[16,8,1664]{2,1,0:T(8,128)(2,1)} %bitcast.6), calls=%async_computation.1 | async-start | bytes 851968 | tf_op jit(solution)/shard_map/all_to_all | solution.py:453
  50.2 12.4 %grads.1 = (bf16[1664,6144]{1,0:T(8,128)(2,1)}, bf16[6144,1664]{1,0:T(8,128)(2,1)}) custom-call(bf16[1664,64]{1,0:T(8,128)(2,1)S(1)} %get-tuple-element.32.x_t_ref, bf16[64,1664]{1,0:T(8,128)(2,1)S(1)} %get-tuple-element.33.g_ref, bf16[12,64,512]{2,1,0:T(8,128)(2,1)S(1)} %get-tuple-element.34.act_ref, ...), custom_call_target="tpu_custom_call", output_to_operand_aliasing={{1}: (4, {})} | custom-call | flops 2617245696 | bytes 40894464 | tf_op jit(solution)/shard_map/grads/pallas_call | solution.py:456
  62.6 0.3 all-to-all-done.1
  62.9 0.0 copy-done
  62.9 1.5 %combine.1 = (bf16[128,1664]{1,0:T(8,128)(2,1)}, bf16[128,1664]{1,0:T(8,128)(2,1)}, f32[2,128]{1,0:T(2,128)}) custom-call(bf16[128,1664]{1,0:T(8,128)(2,1)S(1)} %bitcast.12, bf16[384,128]{1,0:T(8,128)(2,1)S(1)} %get-tuple-element.27.pick_ref, f32[128,8]{1,0:T(8,128)S(1)} %get-tuple-element.28.gate_ref, bf16[128,1664]{1,0:T(8,128)(2,1)S(1)} %copy-done), custom_call_target="tpu_custom_call" | custom-call | tf_op jit(solution)/shard_map/combine/pallas_call | solution.py:478
Async XLA Ops:
  46.3 16.6 %copy-start = (bf16[128,1664]{1,0:T(8,128)(2,1)S(1)}, bf16[128,1664]{1,0:T(8,128)(2,1)}, u32[]{:S(2)}) copy-start(bf16[128,1664]{1,0:T(8,128)(2,1)} %cot_ref.1) | copy-start | bytes 1277956
  46.4 16.6 %all-to-all-start.1 = ((bf16[16,8,1664]{2,1,0:T(8,128)(2,1)}), bf16[16,8,1664]{2,1,0:T(8,128)(2,1)S(1)}, u32[]{:S(2)}, u32[]{:S(2)}) async-start(bf16[16,8,1664]{2,1,0:T(8,128)(2,1)} %bitcast.6), calls=%async_computation.1 | async-start | bytes 851968 | tf_op jit(solution)/shard_map/all_to_all | solution.py:453

commit v9 on v8

--- a/solution.py
+++ b/solution.py
@@ -247,11 +247,17 @@
             copy.wait()
         act, act_t, d_pre = act_ref[step - 1], act_t_ref[...], d_pre_ref[step - 1]
         found = []
-        run(
-            [*front_dots(step, found), *back_dots(step - 1, act, d_pre)],
-            [*grad_dots(step - 1, act_t)],
-        )
-        middle(step, found)
+        fronts = [*front_dots(step, found)]
+        backs = [*back_dots(step - 1, act, d_pre)]
+        blocks = len(fronts) // 2
+        share = len(backs) // (blocks + 1)
+        order = []
+        for block in range(blocks):
+            order += fronts[2 * block:2 * block + 2]
+            order += backs[share * block:share * (block + 1)]
+            order.append(lambda block=block: middle(step, found[block:block + 1]))
+        order += backs[share * blocks:]
+        run(order, [*grad_dots(step - 1, act_t)])
         leave(step - 1).start()
 
     found = []
@@ -349,24 +355,42 @@
             copy.wait()
 
 
-def combine_kernel(ret_ref, pick_ref, gate_ref, cot_ref, mixed_ref, d_tok_ref, d_gate_ref):
-    count = cot_ref.shape[0]
+def combine_kernel(
+    ret_ref, pick_ref, gate_ref, cot_ref, mixed_hbm, d_tok_hbm, d_gate_ref,
+    mixed_ref, d_tok_ref, sem,
+):
+    count, width = cot_ref.shape
     rows = pick_ref.shape[1]
-    found = None
-    for first in range(0, ret_ref.shape[0], rows):
-        part = jnp.dot(
-            pick_ref[...], ret_ref[first:first + rows, :], preferred_element_type=jnp.float32
-        )
-        found = part if found is None else found + part
-    o_0, o_1 = found[:count], found[count:2 * count]
-    mixed_ref[...] = (gate_ref[:, 2:3] * o_0 + gate_ref[:, 3:4] * o_1).astype(jnp.bfloat16)
-    d_tok_ref[...] = found[2 * count:].astype(jnp.bfloat16)
-    cot = cot_ref[...].astype(jnp.float32)
-    d_0 = jnp.sum(cot * o_0, axis=1, keepdims=True)
-    d_1 = jnp.sum(cot * o_1, axis=1, keepdims=True)
+    d_0 = jnp.zeros((count, 1), jnp.float32)
+    d_1 = jnp.zeros((count, 1), jnp.float32)
+    copies = []
+    for block, left in enumerate(range(0, width, 512)):
+        cols = slice(left, min(left + 512, width))
+        found = None
+        for first in range(0, ret_ref.shape[0], rows):
+            part = jnp.dot(
+                pick_ref[...],
+                ret_ref[first:first + rows, cols],
+                preferred_element_type=jnp.float32,
+            )
+            found = part if found is None else found + part
+        o_0, o_1 = found[:count], found[count:2 * count]
+        mixed_ref[:, cols] = (gate_ref[:, 2:3] * o_0 + gate_ref[:, 3:4] * o_1).astype(jnp.bfloat16)
+        d_tok_ref[:, cols] = found[2 * count:].astype(jnp.bfloat16)
+        copies += [
+            pltpu.make_async_copy(mixed_ref.at[:, cols], mixed_hbm.at[:, cols], sem.at[block, 0]),
+            pltpu.make_async_copy(d_tok_ref.at[:, cols], d_tok_hbm.at[:, cols], sem.at[block, 1]),
+        ]
+        for copy in copies[-2:]:
+            copy.start()
+        cot = cot_ref[:, cols].astype(jnp.float32)
+        d_0 += jnp.sum(cot * o_0, axis=1, keepdims=True)
+        d_1 += jnp.sum(cot * o_1, axis=1, keepdims=True)
     lane = lax.broadcasted_iota(jnp.int32, (count, 8), 1)
     both = jnp.where(lane == 0, d_0, jnp.where(lane == 1, d_1, 0.0))
     d_gate_ref[...] = jnp.transpose(both, (1, 0))[0:2, :]
+    for copy in copies:
+        copy.wait()
 
 
 def params(mib):
@@ -482,6 +506,13 @@
             jax.ShapeDtypeStruct((count, width), low),
             jax.ShapeDtypeStruct((2, count), jnp.float32),
         ),
+        in_specs=[vmem] * 4,
+        out_specs=(hbm, hbm, vmem),
+        scratch_shapes=[
+            pltpu.VMEM((count, width), low),
+            pltpu.VMEM((count, width), low),
+            pltpu.SemaphoreType.DMA((pl.cdiv(width, 512), 2)),
+        ],
         compiler_params=params(12),
         name="combine",
     )(ret, pick, gate_cols, cotangent)

time: 64.7 us -> 65.2 us (level)
  no operation moved by 1% of the time
where the time goes in v9:
time: 65.2 us; the launch traced here: 64.9 us
  Pallas kernels  40.2 us (62%)
  blocking collectives  19.9 us (31%)
  starting transfers between devices  3.84 us (6%)
  between operations  0.67 us (1%)
    pallas_call x1, Pallas kernels, per_device(): pl.pallas_call(functools.partial(forward_kernel, steps), out_shape=(pltpu...  23.4 us
    all_to_all x1, blocking collectives, per_device(): lax.all_to_all(send, 'expert', split_axis=0, concat_axis=0, tiled=True)  19.9 us
    pallas_call x1, Pallas kernels, per_device(): pl.pallas_call(grads_kernel, out_shape=(jax.ShapeDtypeStruct((width, hidd...  12.4 us
    all_to_all x1, starting transfers between devices, per_device(): lax.all_to_all(ret.reshape(rows // PAIR, PAIR, width), 'expert', split_ax...  3.84 us
    pallas_call x1, Pallas kernels, per_device(): pl.pallas_call(dispatch_kernel, out_shape=(pltpu.VMEM((slots, width), low...  2.35 us
    pallas_call x1, Pallas kernels, per_device(): pl.pallas_call(combine_kernel, out_shape=(jax.ShapeDtypeStruct((count, wi...  2.09 us
  transfers between devices with their start and end apart: 1, of which 1 were waited for; matrix products, arithmetic and copies ran while one was open for 0% of the time, Pallas kernels for 19%

profile of v9, /device:TPU:0, one launch (start us, length us, event | category | flops | bytes accessed | tf_op | source)
XLA Modules:
  0.0 64.9 jit_solution(9641944192434412063)
XLA Ops:
  0.6 2.4 %dispatch.1 = (bf16[128,1664]{1,0:T(8,128)(2,1)S(1)}, f32[8,128]{1,0:T(8,128)S(1)}, bf16[1664,512]{1,0:T(8,128)(2,1)S(1)}, bf16[512,1664]{1,0:T(8,128)(2,1)S(1)}) custom-call(s32[2,128]{1,0:T(2,128)} %bitcast.19, s32[1,128]{1,0:T(1,128)} %prio_hbm.1, f32[2,128]{1,0:T(2,128)} %bitcast.20, bf16[128,1664]{1,0:T(8,128)(2,1)} %tok_hbm.1, ...), custom_call_target="tpu_custom_call" | custom-call | tf_op jit(solution)/shard_map/dispatch/pallas_call | solution.py:416
  3.0 19.9 %all_to_all.10 = bf16[16,8,1664]{2,1,0:T(8,128)(2,1)S(1)} all-to-all(bf16[16,8,1664]{2,1,0:T(8,128)(2,1)S(1)} %bitcast.13), channel_id=1, replica_groups=mesh['groups'=2,'expert'=16] {'expert'}, dimensions={0} | all-to-all | bytes 851968 | tf_op jit(solution)/shard_map/all_to_all | solution.py:439
  22.9 23.4 %forward.1 = (bf16[128,1664]{1,0:T(8,128)(2,1)}, bf16[1664,64]{1,0:T(8,128)(2,1)S(1)}, bf16[64,1664]{1,0:T(8,128)(2,1)S(1)}, bf16[12,64,512]{2,1,0:T(8,128)(2,1)...) custom-call(bf16[128,1664]{1,0:T(8,128)(2,1)S(1)} %bitcast.11, ...), custom_call_target="tpu_custom_call" | custom-call | flops 5234491392 | bytes 40894464 | tf_op jit(solution)/shard_map/forward/pallas_call | solution.py:443
  46.3 0.0 copy-start
  46.3 3.8 %all-to-all-start.1 = ((bf16[16,8,1664]{2,1,0:T(8,128)(2,1)}), bf16[16,8,1664]{2,1,0:T(8,128)(2,1)S(1)}, u32[]{:S(2)}, u32[]{:S(2)}) async-start(bf16[16,8,1664]{2,1,0:T(8,128)(2,1)} %bitcast.6), calls=%async_computation.1 | async-start | bytes 851968 | tf_op jit(solution)/shard_map/all_to_all | solution.py:477
  50.1 12.4 %grads.1 = (bf16[1664,6144]{1,0:T(8,128)(2,1)}, bf16[6144,1664]{1,0:T(8,128)(2,1)}) custom-call(bf16[1664,64]{1,0:T(8,128)(2,1)S(1)} %get-tuple-element.32.x_t_ref, bf16[64,1664]{1,0:T(8,128)(2,1)S(1)} %get-tuple-element.33.g_ref, bf16[12,64,512]{2,1,0:T(8,128)(2,1)S(1)} %get-tuple-element.34.act_ref, ...), custom_call_target="tpu_custom_call", output_to_operand_aliasing={{1}: (4, {})} | custom-call | flops 2617245696 | bytes 40894464 | tf_op jit(solution)/shard_map/grads/pallas_call | solution.py:480
  62.5 0.3 all-to-all-done.1
  62.8 0.0 copy-done
  62.8 2.1 %combine.1 = (bf16[128,1664]{1,0:T(8,128)(2,1)}, bf16[128,1664]{1,0:T(8,128)(2,1)}, f32[2,128]{1,0:T(2,128)}) custom-call(bf16[128,1664]{1,0:T(8,128)(2,1)S(1)} %bitcast.12, bf16[384,128]{1,0:T(8,128)(2,1)S(1)} %get-tuple-element.27.pick_ref, f32[128,8]{1,0:T(8,128)S(1)} %get-tuple-element.28.gate_ref, bf16[128,1664]{1,0:T(8,128)(2,1)S(1)} %copy-done), custom_call_target="tpu_custom_call" | custom-call | tf_op jit(solution)/shard_map/combine/pallas_call | solution.py:502
Async XLA Ops:
  46.3 16.6 %copy-start = (bf16[128,1664]{1,0:T(8,128)(2,1)S(1)}, bf16[128,1664]{1,0:T(8,128)(2,1)}, u32[]{:S(2)}) copy-start(bf16[128,1664]{1,0:T(8,128)(2,1)} %cot_ref.1) | copy-start | bytes 1277956
  46.3 16.6 %all-to-all-start.1 = ((bf16[16,8,1664]{2,1,0:T(8,128)(2,1)}), bf16[16,8,1664]{2,1,0:T(8,128)(2,1)S(1)}, u32[]{:S(2)}, u32[]{:S(2)}) async-start(bf16[16,8,1664]{2,1,0:T(8,128)(2,1)} %bitcast.6), calls=%async_computation.1 | async-start | bytes 851968 | tf_op jit(solution)/shard_map/all_to_all | solution.py:477

commit v10 on v8

--- a/solution.py
+++ b/solution.py
@@ -48,6 +48,11 @@
     return place_0, place_1
 
 
+def row_slots(count):
+    row = lax.broadcasted_iota(jnp.int32, (EXPERTS * PAIR, count), 0)
+    return ((row >> 3) << 2) | (row & (CAP - 1)), (row & CAP) == 0
+
+
 def dispatch_kernel(
     ids_hbm, prio_hbm, gates_hbm, tok_hbm, cot_hbm, w_in_hbm, w_out_hbm,
     send_ref, plan_ref, w_in_ref, w_out_ref,
@@ -65,15 +70,14 @@
         (w_out_hbm.at[0:depth, :], w_out_ref),
     )
     copies = [pltpu.make_async_copy(*pair, sem.at[index]) for index, pair in enumerate(pairs)]
-    for copy in copies:
+    for copy in copies[:5]:
         copy.start()
     for copy in copies[:3]:
         copy.wait()
+    for copy in copies[5:]:
+        copy.start()
     place_0, place_1 = place_rows(ids_ref[...], prio_ref[...])
-    rows = EXPERTS * PAIR
-    row = lax.broadcasted_iota(jnp.int32, (rows, count), 0)
-    slot = row // PAIR * CAP + row % CAP
-    is_x = row % PAIR < CAP
+    slot, is_x = row_slots(count)
     hit_0 = slot == place_0
     hit_1 = slot == place_1
     hit = jnp.where(hit_0 | hit_1, 1.0, 0.0)
@@ -104,10 +108,7 @@
     place_0 = plan_ref[0:1, :].astype(jnp.int32)
     place_1 = plan_ref[1:2, :].astype(jnp.int32)
     count = place_0.shape[1]
-    rows = EXPERTS * PAIR
-    row = lax.broadcasted_iota(jnp.int32, (rows, count), 0)
-    slot = row // PAIR * CAP + row % CAP
-    is_x = row % PAIR < CAP
+    slot, is_x = row_slots(count)
     hit_0 = jnp.where(slot == place_0, 1.0, 0.0)
     hit_1 = jnp.where(slot == place_1, 1.0, 0.0)
     pick_0 = jnp.transpose(jnp.where(is_x, hit_0, 0.0), (1, 0))
@@ -121,7 +122,7 @@
     half = rows // 2
     out = lax.broadcasted_iota(jnp.int32, (half, rows), 0)
     col = lax.broadcasted_iota(jnp.int32, (half, rows), 1)
-    source = out // CAP * PAIR + out % CAP
+    source = ((out >> 2) << 3) | (out & (CAP - 1))
     x_pick = jnp.where(col == source, 1.0, 0.0).astype(jnp.bfloat16)
     g_pick = jnp.where(col == source + CAP, 1.0, 0.0).astype(jnp.bfloat16)
     return x_pick, g_pick
@@ -242,26 +243,37 @@
                 other()
             done = due
 
-    def both(step):
+    def both(step, extra=()):
         for copy in copies(step):
             copy.wait()
         act, act_t, d_pre = act_ref[step - 1], act_t_ref[...], d_pre_ref[step - 1]
         found = []
-        run(
-            [*front_dots(step, found), *back_dots(step - 1, act, d_pre)],
-            [*grad_dots(step - 1, act_t)],
-        )
-        middle(step, found)
+        fronts = [*front_dots(step, found)]
+        backs = [*back_dots(step - 1, act, d_pre)]
+        blocks = len(fronts) // 2
+        share = len(backs) // (blocks + 1)
+        order = []
+        for block in range(blocks):
+            order += fronts[2 * block:2 * block + 2]
+            order += backs[share * block:share * (block + 1)]
+            order.append(lambda block=block: middle(step, found[block:block + 1]))
+        order += [*extra, *backs[share * blocks:]]
+        run(order, [*grad_dots(step - 1, act_t)])
         leave(step - 1).start()
 
     found = []
     for thunk in front_dots(0, found):
         thunk()
     middle(0, found)
+
+    def aside():
+        x_t_ref[...] = jnp.transpose(x_rows, (1, 0)).astype(low)
+        tables(plan_ref, pick_ref, gate_ref)
+
     if steps > 1:
-        both(1)
-    x_t_ref[...] = jnp.transpose(x_rows, (1, 0)).astype(low)
-    tables(plan_ref, pick_ref, gate_ref)
+        both(1, (aside,))
+    else:
+        aside()
 
     def body(step, carry):
         @pl.when(step > 2)
@@ -275,11 +287,11 @@
     last = steps - 1
     if steps > 2:
         leave(last - 2).wait()
-    run(
-        [*back_dots(last, act_ref[last], d_pre_ref[last])],
-        [*grad_dots(last, act_t_ref[...])],
-    )
+    for thunk in grad_dots(last, act_t_ref[...]):
+        thunk()
     leave(last).start()
+    for thunk in back_dots(last, act_ref[last], d_pre_ref[last]):
+        thunk()
     ret = lax.dot_general(
         x_pick, out_acc[...].astype(low), ROWS_DIM, preferred_element_type=jnp.float32
     ) + lax.dot_general(

time: 64.7 us -> 65 us (level)
    pallas_call x1, Pallas kernels: 2.35 us -> 3.06 us  [per_device(): pl.pallas_call(dispatch_kernel, out_shape=(pltpu.VMEM((slots, width), low...]
where the time goes in v10:
time: 65 us; the launch traced here: 64.7 us
  Pallas kernels  39.9 us (61%)
  blocking collectives  19.9 us (31%)
  starting transfers between devices  3.84 us (6%)
  between operations  0.67 us (1%)
    pallas_call x1, Pallas kernels, per_device(): pl.pallas_call(functools.partial(forward_kernel, steps), out_shape=(pltpu...  23 us
    all_to_all x1, blocking collectives, per_device(): lax.all_to_all(send, 'expert', split_axis=0, concat_axis=0, tiled=True)  19.9 us
    pallas_call x1, Pallas kernels, per_device(): pl.pallas_call(grads_kernel, out_shape=(jax.ShapeDtypeStruct((width, hidd...  12.4 us
    all_to_all x1, starting transfers between devices, per_device(): lax.all_to_all(ret.reshape(rows // PAIR, PAIR, width), 'expert', split_ax...  3.84 us
    pallas_call x1, Pallas kernels, per_device(): pl.pallas_call(dispatch_kernel, out_shape=(pltpu.VMEM((slots, width), low...  3.06 us
    pallas_call x1, Pallas kernels, per_device(): pl.pallas_call(combine_kernel, out_shape=(jax.ShapeDtypeStruct((count, wi...  1.51 us
  transfers between devices with their start and end apart: 1, of which 1 were waited for; matrix products, arithmetic and copies ran while one was open for 0% of the time, Pallas kernels for 19%

profile of v10, /device:TPU:0, one launch (start us, length us, event | category | flops | bytes accessed | tf_op | source)
XLA Modules:
  0.0 64.7 jit_solution(1576770945917013217)
XLA Ops:
  0.6 3.1 %dispatch.1 = (bf16[128,1664]{1,0:T(8,128)(2,1)S(1)}, f32[8,128]{1,0:T(8,128)S(1)}, bf16[1664,512]{1,0:T(8,128)(2,1)S(1)}, bf16[512,1664]{1,0:T(8,128)(2,1)S(1)}) custom-call(s32[2,128]{1,0:T(2,128)} %bitcast.19, s32[1,128]{1,0:T(1,128)} %prio_hbm.1, f32[2,128]{1,0:T(2,128)} %bitcast.20, bf16[128,1664]{1,0:T(8,128)(2,1)} %tok_hbm.1, ...), custom_call_target="tpu_custom_call" | custom-call | tf_op jit(solution)/shard_map/dispatch/pallas_call | solution.py:404
  3.7 19.9 %all_to_all.10 = bf16[16,8,1664]{2,1,0:T(8,128)(2,1)S(1)} all-to-all(bf16[16,8,1664]{2,1,0:T(8,128)(2,1)S(1)} %bitcast.13), channel_id=1, replica_groups=mesh['groups'=2,'expert'=16] {'expert'}, dimensions={0} | all-to-all | bytes 851968 | tf_op jit(solution)/shard_map/all_to_all | solution.py:427
  23.6 23.0 %forward.1 = (bf16[128,1664]{1,0:T(8,128)(2,1)}, bf16[1664,64]{1,0:T(8,128)(2,1)S(1)}, bf16[64,1664]{1,0:T(8,128)(2,1)S(1)}, bf16[12,64,512]{2,1,0:T(8,128)(2,1)...) custom-call(bf16[128,1664]{1,0:T(8,128)(2,1)S(1)} %bitcast.11, ...), custom_call_target="tpu_custom_call" | custom-call | flops 5234491392 | bytes 40894464 | tf_op jit(solution)/shard_map/forward/pallas_call | solution.py:431
  46.6 0.0 copy-start
  46.6 3.8 %all-to-all-start.1 = ((bf16[16,8,1664]{2,1,0:T(8,128)(2,1)}), bf16[16,8,1664]{2,1,0:T(8,128)(2,1)S(1)}, u32[]{:S(2)}, u32[]{:S(2)}) async-start(bf16[16,8,1664]{2,1,0:T(8,128)(2,1)} %bitcast.6), calls=%async_computation.1 | async-start | bytes 851968 | tf_op jit(solution)/shard_map/all_to_all | solution.py:465
  50.4 12.4 %grads.1 = (bf16[1664,6144]{1,0:T(8,128)(2,1)}, bf16[6144,1664]{1,0:T(8,128)(2,1)}) custom-call(bf16[1664,64]{1,0:T(8,128)(2,1)S(1)} %get-tuple-element.32.x_t_ref, bf16[64,1664]{1,0:T(8,128)(2,1)S(1)} %get-tuple-element.33.g_ref, bf16[12,64,512]{2,1,0:T(8,128)(2,1)S(1)} %get-tuple-element.34.act_ref, ...), custom_call_target="tpu_custom_call", output_to_operand_aliasing={{1}: (4, {})} | custom-call | flops 2617245696 | bytes 40894464 | tf_op jit(solution)/shard_map/grads/pallas_call | solution.py:468
  62.8 0.3 all-to-all-done.1
  63.2 0.0 copy-done
  63.2 1.5 %combine.1 = (bf16[128,1664]{1,0:T(8,128)(2,1)}, bf16[128,1664]{1,0:T(8,128)(2,1)}, f32[2,128]{1,0:T(2,128)}) custom-call(bf16[128,1664]{1,0:T(8,128)(2,1)S(1)} %bitcast.12, bf16[384,128]{1,0:T(8,128)(2,1)S(1)} %get-tuple-element.27.pick_ref, f32[128,8]{1,0:T(8,128)S(1)} %get-tuple-element.28.gate_ref, bf16[128,1664]{1,0:T(8,128)(2,1)S(1)} %copy-done), custom_call_target="tpu_custom_call" | custom-call | tf_op jit(solution)/shard_map/combine/pallas_call | solution.py:490
Async XLA Ops:
  46.6 16.6 %copy-start = (bf16[128,1664]{1,0:T(8,128)(2,1)S(1)}, bf16[128,1664]{1,0:T(8,128)(2,1)}, u32[]{:S(2)}) copy-start(bf16[128,1664]{1,0:T(8,128)(2,1)} %cot_ref.1) | copy-start | bytes 1277956
  46.6 16.6 %all-to-all-start.1 = ((bf16[16,8,1664]{2,1,0:T(8,128)(2,1)}), bf16[16,8,1664]{2,1,0:T(8,128)(2,1)S(1)}, u32[]{:S(2)}, u32[]{:S(2)}) async-start(bf16[16,8,1664]{2,1,0:T(8,128)(2,1)} %bitcast.6), calls=%async_computation.1 | async-start | bytes 851968 | tf_op jit(solution)/shard_map/all_to_all | solution.py:465

commit v11 on v10

--- a/solution.py
+++ b/solution.py
@@ -70,12 +70,10 @@
         (w_out_hbm.at[0:depth, :], w_out_ref),
     )
     copies = [pltpu.make_async_copy(*pair, sem.at[index]) for index, pair in enumerate(pairs)]
-    for copy in copies[:5]:
+    for copy in copies:
         copy.start()
     for copy in copies[:3]:
         copy.wait()
-    for copy in copies[5:]:
-        copy.start()
     place_0, place_1 = place_rows(ids_ref[...], prio_ref[...])
     slot, is_x = row_slots(count)
     hit_0 = slot == place_0
@@ -118,14 +116,13 @@
     gate_ref[...] = jnp.transpose(plan_ref[...], (1, 0))
 
 
-def row_picks(rows):
+def row_order(rows):
     half = rows // 2
-    out = lax.broadcasted_iota(jnp.int32, (half, rows), 0)
-    col = lax.broadcasted_iota(jnp.int32, (half, rows), 1)
-    source = ((out >> 2) << 3) | (out & (CAP - 1))
-    x_pick = jnp.where(col == source, 1.0, 0.0).astype(jnp.bfloat16)
-    g_pick = jnp.where(col == source + CAP, 1.0, 0.0).astype(jnp.bfloat16)
-    return x_pick, g_pick
+    out = lax.broadcasted_iota(jnp.int32, (rows, rows), 0)
+    col = lax.broadcasted_iota(jnp.int32, (rows, rows), 1)
+    place = jnp.where(out < half, out, out - half)
+    source = ((place >> 2) << 3) | (place & (CAP - 1)) | jnp.where(out < half, 0, CAP)
+    return jnp.where(col == source, 1.0, 0.0).astype(jnp.bfloat16)
 
 
 def forward_kernel(
@@ -155,11 +152,12 @@
         return carry
 
     lax.fori_loop(1, steps, begin, 0)
-    recv = recv_ref[...]
-    x_pick, g_pick = row_picks(recv.shape[0])
-    x_rows = jnp.dot(x_pick, recv, preferred_element_type=jnp.float32)
+    order = row_order(recv_ref.shape[0])
+    half = recv_ref.shape[0] // 2
+    found = jnp.dot(order, recv_ref[...], preferred_element_type=jnp.float32)
+    x_rows = found[:half]
     x_ref[...] = x_rows.astype(low)
-    g_ref[...] = jnp.dot(g_pick, recv, preferred_element_type=jnp.float32).astype(low)
+    g_ref[...] = found[half:].astype(low)
     out_acc[...] = jnp.zeros_like(out_acc)
     back_acc[...] = jnp.zeros_like(back_acc)
 
@@ -252,13 +250,13 @@
         backs = [*back_dots(step - 1, act, d_pre)]
         blocks = len(fronts) // 2
         share = len(backs) // (blocks + 1)
-        order = []
+        turns = []
         for block in range(blocks):
-            order += fronts[2 * block:2 * block + 2]
-            order += backs[share * block:share * (block + 1)]
-            order.append(lambda block=block: middle(step, found[block:block + 1]))
-        order += [*extra, *backs[share * blocks:]]
-        run(order, [*grad_dots(step - 1, act_t)])
+            turns += fronts[2 * block:2 * block + 2]
+            turns += backs[share * block:share * (block + 1)]
+            turns.append(lambda block=block: middle(step, found[block:block + 1]))
+        turns += [*extra, *backs[share * blocks:]]
+        run(turns, [*grad_dots(step - 1, act_t)])
         leave(step - 1).start()
 
     found = []
@@ -292,11 +290,8 @@
     leave(last).start()
     for thunk in back_dots(last, act_ref[last], d_pre_ref[last]):
         thunk()
-    ret = lax.dot_general(
-        x_pick, out_acc[...].astype(low), ROWS_DIM, preferred_element_type=jnp.float32
-    ) + lax.dot_general(
-        g_pick, back_acc[...].astype(low), ROWS_DIM, preferred_element_type=jnp.float32
-    )
+    sums = jnp.concatenate([out_acc[...], back_acc[...]], axis=0).astype(low)
+    ret = lax.dot_general(order, sums, ROWS_DIM, preferred_element_type=jnp.float32)
     ret_ref[...] = ret.astype(low)
     if steps > 1:
         leave(last - 1).wait()

time: 65 us -> 64.5 us (level)
    pallas_call x1, Pallas kernels: 3.06 us -> 2.35 us  [per_device(): pl.pallas_call(dispatch_kernel, out_shape=(pltpu.VMEM((slots, width), low...]
where the time goes in v11:
time: 64.5 us; the launch traced here: 64.2 us
  Pallas kernels  39.4 us (61%)
  blocking collectives  19.9 us (31%)
  starting transfers between devices  3.84 us (6%)
  between operations  0.67 us (1%)
    pallas_call x1, Pallas kernels, per_device(): pl.pallas_call(functools.partial(forward_kernel, steps), out_shape=(pltpu...  23.2 us
    all_to_all x1, blocking collectives, per_device(): lax.all_to_all(send, 'expert', split_axis=0, concat_axis=0, tiled=True)  19.9 us
    pallas_call x1, Pallas kernels, per_device(): pl.pallas_call(grads_kernel, out_shape=(jax.ShapeDtypeStruct((width, hidd...  12.4 us
    all_to_all x1, starting transfers between devices, per_device(): lax.all_to_all(ret.reshape(rows // PAIR, PAIR, width), 'expert', split_ax...  3.84 us
    pallas_call x1, Pallas kernels, per_device(): pl.pallas_call(dispatch_kernel, out_shape=(pltpu.VMEM((slots, width), low...  2.35 us
    pallas_call x1, Pallas kernels, per_device(): pl.pallas_call(combine_kernel, out_shape=(jax.ShapeDtypeStruct((count, wi...  1.52 us
  transfers between devices with their start and end apart: 1, of which 1 were waited for; matrix products, arithmetic and copies ran while one was open for 0% of the time, Pallas kernels for 19%

profile of v11, /device:TPU:0, one launch (start us, length us, event | category | flops | bytes accessed | tf_op | source)
XLA Modules:
  0.0 64.2 jit_solution(7097731210014979470)
XLA Ops:
  0.6 2.4 %dispatch.1 = (bf16[128,1664]{1,0:T(8,128)(2,1)S(1)}, f32[8,128]{1,0:T(8,128)S(1)}, bf16[1664,512]{1,0:T(8,128)(2,1)S(1)}, bf16[512,1664]{1,0:T(8,128)(2,1)S(1)}) custom-call(s32[2,128]{1,0:T(2,128)} %bitcast.19, s32[1,128]{1,0:T(1,128)} %prio_hbm.1, f32[2,128]{1,0:T(2,128)} %bitcast.20, bf16[128,1664]{1,0:T(8,128)(2,1)} %tok_hbm.1, ...), custom_call_target="tpu_custom_call" | custom-call | tf_op jit(solution)/shard_map/dispatch/pallas_call | solution.py:399
  3.0 19.9 %all_to_all.10 = bf16[16,8,1664]{2,1,0:T(8,128)(2,1)S(1)} all-to-all(bf16[16,8,1664]{2,1,0:T(8,128)(2,1)S(1)} %bitcast.13), channel_id=1, replica_groups=mesh['groups'=2,'expert'=16] {'expert'}, dimensions={0} | all-to-all | bytes 851968 | tf_op jit(solution)/shard_map/all_to_all | solution.py:422
  22.9 23.2 %forward.1 = (bf16[128,1664]{1,0:T(8,128)(2,1)}, bf16[1664,64]{1,0:T(8,128)(2,1)S(1)}, bf16[64,1664]{1,0:T(8,128)(2,1)S(1)}, bf16[12,64,512]{2,1,0:T(8,128)(2,1)...) custom-call(bf16[128,1664]{1,0:T(8,128)(2,1)S(1)} %bitcast.11, ...), custom_call_target="tpu_custom_call" | custom-call | flops 5234491392 | bytes 40894464 | tf_op jit(solution)/shard_map/forward/pallas_call | solution.py:426
  46.1 0.0 copy-start
  46.1 3.8 %all-to-all-start.1 = ((bf16[16,8,1664]{2,1,0:T(8,128)(2,1)}), bf16[16,8,1664]{2,1,0:T(8,128)(2,1)S(1)}, u32[]{:S(2)}, u32[]{:S(2)}) async-start(bf16[16,8,1664]{2,1,0:T(8,128)(2,1)} %bitcast.6), calls=%async_computation.1 | async-start | bytes 851968 | tf_op jit(solution)/shard_map/all_to_all | solution.py:460
  50.0 12.4 %grads.1 = (bf16[1664,6144]{1,0:T(8,128)(2,1)}, bf16[6144,1664]{1,0:T(8,128)(2,1)}) custom-call(bf16[1664,64]{1,0:T(8,128)(2,1)S(1)} %get-tuple-element.32.x_t_ref, bf16[64,1664]{1,0:T(8,128)(2,1)S(1)} %get-tuple-element.33.g_ref, bf16[12,64,512]{2,1,0:T(8,128)(2,1)S(1)} %get-tuple-element.34.act_ref, ...), custom_call_target="tpu_custom_call", output_to_operand_aliasing={{1}: (4, {})} | custom-call | flops 2617245696 | bytes 40894464 | tf_op jit(solution)/shard_map/grads/pallas_call | solution.py:463
  62.3 0.4 all-to-all-done.1
  62.7 0.0 copy-done
  62.7 1.5 %combine.1 = (bf16[128,1664]{1,0:T(8,128)(2,1)}, bf16[128,1664]{1,0:T(8,128)(2,1)}, f32[2,128]{1,0:T(2,128)}) custom-call(bf16[128,1664]{1,0:T(8,128)(2,1)S(1)} %bitcast.12, bf16[384,128]{1,0:T(8,128)(2,1)S(1)} %get-tuple-element.27.pick_ref, f32[128,8]{1,0:T(8,128)S(1)} %get-tuple-element.28.gate_ref, bf16[128,1664]{1,0:T(8,128)(2,1)S(1)} %copy-done), custom_call_target="tpu_custom_call" | custom-call | tf_op jit(solution)/shard_map/combine/pallas_call | solution.py:485
Async XLA Ops:
  46.1 16.6 %copy-start = (bf16[128,1664]{1,0:T(8,128)(2,1)S(1)}, bf16[128,1664]{1,0:T(8,128)(2,1)}, u32[]{:S(2)}) copy-start(bf16[128,1664]{1,0:T(8,128)(2,1)} %cot_ref.1) | copy-start | bytes 1277956
  46.1 16.6 %all-to-all-start.1 = ((bf16[16,8,1664]{2,1,0:T(8,128)(2,1)}), bf16[16,8,1664]{2,1,0:T(8,128)(2,1)S(1)}, u32[]{:S(2)}, u32[]{:S(2)}) async-start(bf16[16,8,1664]{2,1,0:T(8,128)(2,1)} %bitcast.6), calls=%async_computation.1 | async-start | bytes 851968 | tf_op jit(solution)/shard_map/all_to_all | solution.py:460

commit v12 on v11

--- a/solution.py
+++ b/solution.py
@@ -12,7 +12,6 @@
 CAP = 4
 PAIR = 2 * CAP
 EARLY = 128
-ROWS_DIM = (((0,), (0,)), ((), ()))
 LAST_DIM = (((1,), (1,)), ((), ()))
 
 
@@ -116,10 +115,10 @@
     gate_ref[...] = jnp.transpose(plan_ref[...], (1, 0))
 
 
-def row_order(rows):
+def row_order(rows, dim):
     half = rows // 2
-    out = lax.broadcasted_iota(jnp.int32, (rows, rows), 0)
-    col = lax.broadcasted_iota(jnp.int32, (rows, rows), 1)
+    out = lax.broadcasted_iota(jnp.int32, (rows, rows), dim)
+    col = lax.broadcasted_iota(jnp.int32, (rows, rows), 1 - dim)
     place = jnp.where(out < half, out, out - half)
     source = ((place >> 2) << 3) | (place & (CAP - 1)) | jnp.where(out < half, 0, CAP)
     return jnp.where(col == source, 1.0, 0.0).astype(jnp.bfloat16)
@@ -146,15 +145,15 @@
         slot = lax.rem(step, 2)
         return pltpu.make_async_copy(stage.at[slot], d_out_hbm.at[rows, :], sem_left.at[slot])
 
-    def begin(step, carry):
+    def begin(step):
         for copy in copies(step):
             copy.start()
-        return carry
-
-    lax.fori_loop(1, steps, begin, 0)
-    order = row_order(recv_ref.shape[0])
-    half = recv_ref.shape[0] // 2
-    found = jnp.dot(order, recv_ref[...], preferred_element_type=jnp.float32)
+
+    for step in range(1, min(4, steps)):
+        begin(step)
+    rows = recv_ref.shape[0]
+    half = rows // 2
+    found = jnp.dot(row_order(rows, 0), recv_ref[...], preferred_element_type=jnp.float32)
     x_rows = found[:half]
     x_ref[...] = x_rows.astype(low)
     g_ref[...] = found[half:].astype(low)
@@ -260,8 +259,10 @@
         leave(step - 1).start()
 
     found = []
-    for thunk in front_dots(0, found):
-        thunk()
+    run(
+        [*front_dots(0, found)],
+        [lambda step=step: begin(step) for step in range(4, steps)],
+    )
     middle(0, found)
 
     def aside():
@@ -291,7 +292,7 @@
     for thunk in back_dots(last, act_ref[last], d_pre_ref[last]):
         thunk()
     sums = jnp.concatenate([out_acc[...], back_acc[...]], axis=0).astype(low)
-    ret = lax.dot_general(order, sums, ROWS_DIM, preferred_element_type=jnp.float32)
+    ret = jnp.dot(row_order(rows, 1), sums, preferred_element_type=jnp.float32)
     ret_ref[...] = ret.astype(low)
     if steps > 1:
         leave(last - 1).wait()

time: 64.5 us -> 64.9 us (level)
  no operation moved by 1% of the time
where the time goes in v12:
time: 64.9 us; the launch traced here: 64.6 us
  Pallas kernels  39.8 us (61%)
  blocking collectives  19.9 us (31%)
  starting transfers between devices  3.84 us (6%)
  between operations  0.67 us (1%)
    pallas_call x1, Pallas kernels, per_device(): pl.pallas_call(functools.partial(forward_kernel, steps), out_shape=(pltpu...  23.6 us
    all_to_all x1, blocking collectives, per_device(): lax.all_to_all(send, 'expert', split_axis=0, concat_axis=0, tiled=True)  19.9 us
    pallas_call x1, Pallas kernels, per_device(): pl.pallas_call(grads_kernel, out_shape=(jax.ShapeDtypeStruct((width, hidd...  12.4 us
    all_to_all x1, starting transfers between devices, per_device(): lax.all_to_all(ret.reshape(rows // PAIR, PAIR, width), 'expert', split_ax...  3.84 us
    pallas_call x1, Pallas kernels, per_device(): pl.pallas_call(dispatch_kernel, out_shape=(pltpu.VMEM((slots, width), low...  2.35 us
    pallas_call x1, Pallas kernels, per_device(): pl.pallas_call(combine_kernel, out_shape=(jax.ShapeDtypeStruct((count, wi...  1.51 us
  transfers between devices with their start and end apart: 1, of which 1 were waited for; matrix products, arithmetic and copies ran while one was open for 0% of the time, Pallas kernels for 19%

profile of v12, /device:TPU:0, one launch (start us, length us, event | category | flops | bytes accessed | tf_op | source)
XLA Modules:
  0.0 64.6 jit_solution(11432997815924582429)
XLA Ops:
  0.6 2.4 %dispatch.1 = (bf16[128,1664]{1,0:T(8,128)(2,1)S(1)}, f32[8,128]{1,0:T(8,128)S(1)}, bf16[1664,512]{1,0:T(8,128)(2,1)S(1)}, bf16[512,1664]{1,0:T(8,128)(2,1)S(1)}) custom-call(s32[2,128]{1,0:T(2,128)} %bitcast.19, s32[1,128]{1,0:T(1,128)} %prio_hbm.1, f32[2,128]{1,0:T(2,128)} %bitcast.20, bf16[128,1664]{1,0:T(8,128)(2,1)} %tok_hbm.1, ...), custom_call_target="tpu_custom_call" | custom-call | tf_op jit(solution)/shard_map/dispatch/pallas_call | solution.py:400
  3.0 19.9 %all_to_all.10 = bf16[16,8,1664]{2,1,0:T(8,128)(2,1)S(1)} all-to-all(bf16[16,8,1664]{2,1,0:T(8,128)(2,1)S(1)} %bitcast.13), channel_id=1, replica_groups=mesh['groups'=2,'expert'=16] {'expert'}, dimensions={0} | all-to-all | bytes 851968 | tf_op jit(solution)/shard_map/all_to_all | solution.py:423
  22.9 23.6 %forward.1 = (bf16[128,1664]{1,0:T(8,128)(2,1)}, bf16[1664,64]{1,0:T(8,128)(2,1)S(1)}, bf16[64,1664]{1,0:T(8,128)(2,1)S(1)}, bf16[12,64,512]{2,1,0:T(8,128)(2,1)...) custom-call(bf16[128,1664]{1,0:T(8,128)(2,1)S(1)} %bitcast.11, ...), custom_call_target="tpu_custom_call" | custom-call | flops 5234491392 | bytes 40894464 | tf_op jit(solution)/shard_map/forward/pallas_call | solution.py:427
  46.5 0.0 copy-start
  46.5 3.8 %all-to-all-start.1 = ((bf16[16,8,1664]{2,1,0:T(8,128)(2,1)}), bf16[16,8,1664]{2,1,0:T(8,128)(2,1)S(1)}, u32[]{:S(2)}, u32[]{:S(2)}) async-start(bf16[16,8,1664]{2,1,0:T(8,128)(2,1)} %bitcast.6), calls=%async_computation.1 | async-start | bytes 851968 | tf_op jit(solution)/shard_map/all_to_all | solution.py:461
  50.4 12.4 %grads.1 = (bf16[1664,6144]{1,0:T(8,128)(2,1)}, bf16[6144,1664]{1,0:T(8,128)(2,1)}) custom-call(bf16[1664,64]{1,0:T(8,128)(2,1)S(1)} %get-tuple-element.32.x_t_ref, bf16[64,1664]{1,0:T(8,128)(2,1)S(1)} %get-tuple-element.33.g_ref, bf16[12,64,512]{2,1,0:T(8,128)(2,1)S(1)} %get-tuple-element.34.act_ref, ...), custom_call_target="tpu_custom_call", output_to_operand_aliasing={{1}: (4, {})} | custom-call | flops 2617245696 | bytes 40894464 | tf_op jit(solution)/shard_map/grads/pallas_call | solution.py:464
  62.8 0.3 all-to-all-done.1
  63.1 0.0 copy-done
  63.1 1.5 %combine.1 = (bf16[128,1664]{1,0:T(8,128)(2,1)}, bf16[128,1664]{1,0:T(8,128)(2,1)}, f32[2,128]{1,0:T(2,128)}) custom-call(bf16[128,1664]{1,0:T(8,128)(2,1)S(1)} %bitcast.12, bf16[384,128]{1,0:T(8,128)(2,1)S(1)} %get-tuple-element.27.pick_ref, f32[128,8]{1,0:T(8,128)S(1)} %get-tuple-element.28.gate_ref, bf16[128,1664]{1,0:T(8,128)(2,1)S(1)} %copy-done), custom_call_target="tpu_custom_call" | custom-call | tf_op jit(solution)/shard_map/combine/pallas_call | solution.py:486
Async XLA Ops:
  46.5 16.6 %copy-start = (bf16[128,1664]{1,0:T(8,128)(2,1)S(1)}, bf16[128,1664]{1,0:T(8,128)(2,1)}, u32[]{:S(2)}) copy-start(bf16[128,1664]{1,0:T(8,128)(2,1)} %cot_ref.1) | copy-start | bytes 1277956
  46.5 16.6 %all-to-all-start.1 = ((bf16[16,8,1664]{2,1,0:T(8,128)(2,1)}), bf16[16,8,1664]{2,1,0:T(8,128)(2,1)S(1)}, u32[]{:S(2)}, u32[]{:S(2)}) async-start(bf16[16,8,1664]{2,1,0:T(8,128)(2,1)} %bitcast.6), calls=%async_computation.1 | async-start | bytes 851968 | tf_op jit(solution)/shard_map/all_to_all | solution.py:461

commit v13 on v12

--- a/solution.py
+++ b/solution.py
@@ -145,12 +145,12 @@
         slot = lax.rem(step, 2)
         return pltpu.make_async_copy(stage.at[slot], d_out_hbm.at[rows, :], sem_left.at[slot])
 
-    def begin(step):
+    def begin(step, carry):
         for copy in copies(step):
             copy.start()
-
-    for step in range(1, min(4, steps)):
-        begin(step)
+        return carry
+
+    lax.fori_loop(1, steps, begin, 0)
     rows = recv_ref.shape[0]
     half = rows // 2
     found = jnp.dot(row_order(rows, 0), recv_ref[...], preferred_element_type=jnp.float32)
@@ -167,8 +167,8 @@
 
     def front_dots(step, found):
         w_first, w_second = weights(step)
-        for first in range(0, depth, 256):
-            cols = slice(first, min(first + 256, depth))
+        for first in range(0, depth, 512):
+            cols = slice(first, min(first + 512, depth))
             pre = []
 
             def one(cols=cols, pre=pre):
@@ -259,10 +259,8 @@
         leave(step - 1).start()
 
     found = []
-    run(
-        [*front_dots(0, found)],
-        [lambda step=step: begin(step) for step in range(4, steps)],
-    )
+    for thunk in front_dots(0, found):
+        thunk()
     middle(0, found)
 
     def aside():
@@ -314,46 +312,72 @@
     x_t_ref, g_ref, act_ref, d_pre_ref, _, d_in_hbm, d_out_hbm, d_in_stage, d_out_stage, sem
 ):
     steps, _, depth = act_ref.shape
-    width = x_t_ref.shape[0]
-    slots = d_in_stage.shape[0]
+    slots, strip, _ = d_in_stage.shape
+    strips = x_t_ref.shape[0] // strip
     later = depth - EARLY
 
-    def leave(step):
+    def leave_in(step):
         slot = lax.rem(step, slots)
-        cols = pl.ds(pl.multiple_of(step * depth, depth), depth)
-        pairs = []
+        copies = []
         for index in range(2):
-            some = pl.ds(index * (width // 2), width // 2)
-            pairs.append((d_in_stage.at[slot, some], d_in_hbm.at[some, cols]))
+            first = index * (strip // 2)
+            here = pl.ds(first, strip // 2)
+            there = pl.ds(pl.multiple_of(step * strip + first, 64), strip // 2)
+            copies.append(
+                pltpu.make_async_copy(
+                    d_in_stage.at[slot, here], d_in_hbm.at[there], sem.at[slot, index]
+                )
+            )
+        return copies
+
+    def leave_out(step):
+        slot = lax.rem(step, slots)
+        copies = []
         for index in range(2):
             first = index * (later // 2)
             here = pl.ds(first, later // 2)
             there = pl.ds(pl.multiple_of(step * depth + EARLY + first, 64), later // 2)
-            pairs.append((d_out_stage.at[slot, here], d_out_hbm.at[there]))
-        return [
-            pltpu.make_async_copy(*pair, sem.at[slot, index]) for index, pair in enumerate(pairs)
-        ]
+            copies.append(
+                pltpu.make_async_copy(
+                    d_out_stage.at[slot, here], d_out_hbm.at[there], sem.at[slot, 2 + index]
+                )
+            )
+        return copies
 
     def work(step, carry):
         @pl.when(step >= slots)
         def _():
-            for copy in leave(step - slots):
+            for copy in leave_in(step - slots):
                 copy.wait()
 
         slot = lax.rem(step, slots)
-        copies = leave(step)
-        act_t = jnp.transpose(act_ref[step].astype(jnp.float32), (1, 0)).astype(jnp.bfloat16)
-        product(d_in_stage.at[slot], x_t_ref[...], d_pre_ref[step], 208, 256)
-        for copy in copies[:2]:
+        x_t = x_t_ref[pl.ds(pl.multiple_of(step * strip, strip), strip), :]
+        for part in range(steps):
+            cols = pl.ds(part * depth, depth)
+            product(d_in_stage.at[slot, :, cols], x_t, d_pre_ref[part], strip, 256)
+        for copy in leave_in(step):
             copy.start()
-        product(d_out_stage.at[slot], act_t[EARLY:], g_ref[...], 192, 256)
-        for copy in copies[2:]:
-            copy.start()
+
+        @pl.when((step >= slots) & (step < steps + slots))
+        def _():
+            for copy in leave_out(step - slots):
+                copy.wait()
+
+        @pl.when(step < steps)
+        def _():
+            act_t = jnp.transpose(act_ref[step].astype(jnp.float32), (1, 0)).astype(jnp.bfloat16)
+            product(d_out_stage.at[slot], act_t[EARLY:], g_ref[...], later, 256)
+            for copy in leave_out(step):
+                copy.start()
+
         return carry
 
-    lax.fori_loop(0, steps, work, 0)
-    for step in range(max(steps - slots, 0), steps):
-        for copy in leave(step):
+    lax.fori_loop(0, strips, work, 0)
+    for step in range(max(strips - slots, 0), strips):
+        for copy in leave_in(step):
+            copy.wait()
+    for step in range(max(strips - slots, 0), steps):
+        for copy in leave_out(step):
             copy.wait()
 
 
@@ -471,7 +495,7 @@
         out_specs=(hbm,) * 2,
         input_output_aliases={4: 1},
         scratch_shapes=[
-            pltpu.VMEM((3, width, chunk), low),
+            pltpu.VMEM((3, 128, hidden), low),
             pltpu.VMEM((3, chunk - EARLY, width), low),
             pltpu.SemaphoreType.DMA((3, 4)),
         ],

time: 64.9 us -> 67.5 us (1.040)
  Pallas kernels: 39.8 us -> 42.8 us
    pallas_call x1, Pallas kernels: 12.4 us -> 15.1 us  [per_device(): pl.pallas_call(grads_kernel, out_shape=(jax.ShapeDtypeStruct((width, hidd...]
  transfers between devices with their start and end apart: 1 -> 1, of which waited for: 1 -> 0; matrix products, arithmetic and copies ran while one was open for 0% -> 0% of each run, Pallas kernels for 19% -> 22%
where the time goes in v13:
time: 67.5 us; the launch traced here: 67.3 us
  Pallas kernels  42.8 us (63%)
  blocking collectives  19.9 us (29%)
  starting transfers between devices  3.84 us (6%)
  between operations  0.69 us (1%)
    pallas_call x1, Pallas kernels, per_device(): pl.pallas_call(functools.partial(forward_kernel, steps), out_shape=(pltpu...  23.8 us
    all_to_all x1, blocking collectives, per_device(): lax.all_to_all(send, 'expert', split_axis=0, concat_axis=0, tiled=True)  19.9 us
    pallas_call x1, Pallas kernels, per_device(): pl.pallas_call(grads_kernel, out_shape=(jax.ShapeDtypeStruct((width, hidd...  15.1 us
    all_to_all x1, starting transfers between devices, per_device(): lax.all_to_all(ret.reshape(rows // PAIR, PAIR, width), 'expert', split_ax...  3.84 us
    pallas_call x1, Pallas kernels, per_device(): pl.pallas_call(dispatch_kernel, out_shape=(pltpu.VMEM((slots, width), low...  2.35 us
    pallas_call x1, Pallas kernels, per_device(): pl.pallas_call(combine_kernel, out_shape=(jax.ShapeDtypeStruct((count, wi...  1.51 us
  transfers between devices with their start and end apart: 1, of which 0 were waited for; matrix products, arithmetic and copies ran while one was open for 0% of the time, Pallas kernels for 22%

profile of v13, /device:TPU:0, one launch (start us, length us, event | category | flops | bytes accessed | tf_op | source)
XLA Modules:
  0.0 67.3 jit_solution(17920521774805509676)
XLA Ops:
  0.6 2.4 %dispatch.1 = (bf16[128,1664]{1,0:T(8,128)(2,1)S(1)}, f32[8,128]{1,0:T(8,128)S(1)}, bf16[1664,512]{1,0:T(8,128)(2,1)S(1)}, bf16[512,1664]{1,0:T(8,128)(2,1)S(1)}) custom-call(s32[2,128]{1,0:T(2,128)} %bitcast.19, s32[1,128]{1,0:T(1,128)} %prio_hbm.1, f32[2,128]{1,0:T(2,128)} %bitcast.20, bf16[128,1664]{1,0:T(8,128)(2,1)} %tok_hbm.1, ...), custom_call_target="tpu_custom_call" | custom-call | tf_op jit(solution)/shard_map/dispatch/pallas_call | solution.py:424
  3.0 19.9 %all_to_all.10 = bf16[16,8,1664]{2,1,0:T(8,128)(2,1)S(1)} all-to-all(bf16[16,8,1664]{2,1,0:T(8,128)(2,1)S(1)} %bitcast.13), channel_id=1, replica_groups=mesh['groups'=2,'expert'=16] {'expert'}, dimensions={0} | all-to-all | bytes 851968 | tf_op jit(solution)/shard_map/all_to_all | solution.py:447
  22.9 23.8 %forward.1 = (bf16[128,1664]{1,0:T(8,128)(2,1)}, bf16[1664,64]{1,0:T(8,128)(2,1)S(1)}, bf16[64,1664]{1,0:T(8,128)(2,1)S(1)}, bf16[12,64,512]{2,1,0:T(8,128)(2,1)...) custom-call(bf16[128,1664]{1,0:T(8,128)(2,1)S(1)} %bitcast.11, ...), custom_call_target="tpu_custom_call" | custom-call | flops 5234491392 | bytes 40894464 | tf_op jit(solution)/shard_map/forward/pallas_call | solution.py:451
  46.7 0.0 copy-start
  46.8 3.8 %all-to-all-start.1 = ((bf16[16,8,1664]{2,1,0:T(8,128)(2,1)}), bf16[16,8,1664]{2,1,0:T(8,128)(2,1)S(1)}, u32[]{:S(2)}, u32[]{:S(2)}) async-start(bf16[16,8,1664]{2,1,0:T(8,128)(2,1)} %bitcast.6), calls=%async_computation.1 | async-start | bytes 851968 | tf_op jit(solution)/shard_map/all_to_all | solution.py:485
  50.6 15.1 %grads.1 = (bf16[1664,6144]{1,0:T(8,128)(2,1)}, bf16[6144,1664]{1,0:T(8,128)(2,1)}) custom-call(bf16[1664,64]{1,0:T(8,128)(2,1)S(1)} %get-tuple-element.32.x_t_ref, bf16[64,1664]{1,0:T(8,128)(2,1)S(1)} %get-tuple-element.33.g_ref, bf16[12,64,512]{2,1,0:T(8,128)(2,1)S(1)} %get-tuple-element.34.act_ref, ...), custom_call_target="tpu_custom_call", output_to_operand_aliasing={{1}: (4, {})} | custom-call | flops 2617245696 | bytes 40894464 | tf_op jit(solution)/shard_map/grads/pallas_call | solution.py:488
  65.7 0.0 all-to-all-done.1
  65.8 0.0 copy-done
  65.8 1.5 %combine.1 = (bf16[128,1664]{1,0:T(8,128)(2,1)}, bf16[128,1664]{1,0:T(8,128)(2,1)}, f32[2,128]{1,0:T(2,128)}) custom-call(bf16[128,1664]{1,0:T(8,128)(2,1)S(1)} %bitcast.12, bf16[384,128]{1,0:T(8,128)(2,1)S(1)} %get-tuple-element.27.pick_ref, f32[128,8]{1,0:T(8,128)S(1)} %get-tuple-element.28.gate_ref, bf16[128,1664]{1,0:T(8,128)(2,1)S(1)} %copy-done), custom_call_target="tpu_custom_call" | custom-call | tf_op jit(solution)/shard_map/combine/pallas_call | solution.py:510
Async XLA Ops:
  46.7 19.0 %copy-start = (bf16[128,1664]{1,0:T(8,128)(2,1)S(1)}, bf16[128,1664]{1,0:T(8,128)(2,1)}, u32[]{:S(2)}) copy-start(bf16[128,1664]{1,0:T(8,128)(2,1)} %cot_ref.1) | copy-start | bytes 1277956
  46.8 19.0 %all-to-all-start.1 = ((bf16[16,8,1664]{2,1,0:T(8,128)(2,1)}), bf16[16,8,1664]{2,1,0:T(8,128)(2,1)S(1)}, u32[]{:S(2)}, u32[]{:S(2)}) async-start(bf16[16,8,1664]{2,1,0:T(8,128)(2,1)} %bitcast.6), calls=%async_computation.1 | async-start | bytes 851968 | tf_op jit(solution)/shard_map/all_to_all | solution.py:485

commit v14 on v12

--- a/solution.py
+++ b/solution.py
@@ -11,7 +11,7 @@
 EXPERTS = 16
 CAP = 4
 PAIR = 2 * CAP
-EARLY = 128
+EARLY = 64
 LAST_DIM = (((1,), (1,)), ((), ()))
 
 
@@ -145,12 +145,12 @@
         slot = lax.rem(step, 2)
         return pltpu.make_async_copy(stage.at[slot], d_out_hbm.at[rows, :], sem_left.at[slot])
 
-    def begin(step):
+    def begin(step, carry):
         for copy in copies(step):
             copy.start()
-
-    for step in range(1, min(4, steps)):
-        begin(step)
+        return carry
+
+    lax.fori_loop(1, steps, begin, 0)
     rows = recv_ref.shape[0]
     half = rows // 2
     found = jnp.dot(row_order(rows, 0), recv_ref[...], preferred_element_type=jnp.float32)
@@ -259,10 +259,8 @@
         leave(step - 1).start()
 
     found = []
-    run(
-        [*front_dots(0, found)],
-        [lambda step=step: begin(step) for step in range(4, steps)],
-    )
+    for thunk in front_dots(0, found):
+        thunk()
     middle(0, found)
 
     def aside():
@@ -328,7 +326,7 @@
         for index in range(2):
             first = index * (later // 2)
             here = pl.ds(first, later // 2)
-            there = pl.ds(pl.multiple_of(step * depth + EARLY + first, 64), later // 2)
+            there = pl.ds(pl.multiple_of(step * depth + EARLY + first, 32), later // 2)
             pairs.append((d_out_stage.at[slot, here], d_out_hbm.at[there]))
         return [
             pltpu.make_async_copy(*pair, sem.at[slot, index]) for index, pair in enumerate(pairs)
@@ -395,7 +393,7 @@
     low = jnp.bfloat16
     vmem = pl.BlockSpec(memory_space=pltpu.VMEM)
     hbm = pl.BlockSpec(memory_space=pl.ANY)
-    chunk = chunk_of(hidden, 512)
+    chunk = chunk_of(hidden, 256)
     steps = hidden // chunk
     send, plan, w_in_0, w_out_0 = pl.pallas_call(
         dispatch_kernel,

time: 64.9 us -> 67.8 us (1.045)
  Pallas kernels: 39.8 us -> 43.1 us
    pallas_call x1, Pallas kernels: 23.6 us -> 25.9 us  [per_device(): pl.pallas_call(functools.partial(forward_kernel, steps), out_shape=(pltpu...]
    pallas_call x1, Pallas kernels: 12.4 us -> 13.9 us  [per_device(): pl.pallas_call(grads_kernel, out_shape=(jax.ShapeDtypeStruct((width, hidd...]
  transfers between devices with their start and end apart: 1 -> 1, of which waited for: 1 -> 0; matrix products, arithmetic and copies ran while one was open for 0% -> 0% of each run, Pallas kernels for 19% -> 21%
where the time goes in v14:
time: 67.8 us; the launch traced here: 67.5 us
  Pallas kernels  43.1 us (64%)
  blocking collectives  19.9 us (29%)
  starting transfers between devices  3.84 us (6%)
  between operations  0.69 us (1%)
    pallas_call x1, Pallas kernels, per_device(): pl.pallas_call(functools.partial(forward_kernel, steps), out_shape=(pltpu...  25.9 us
    all_to_all x1, blocking collectives, per_device(): lax.all_to_all(send, 'expert', split_axis=0, concat_axis=0, tiled=True)  19.9 us
    pallas_call x1, Pallas kernels, per_device(): pl.pallas_call(grads_kernel, out_shape=(jax.ShapeDtypeStruct((width, hidd...  13.9 us
    all_to_all x1, starting transfers between devices, per_device(): lax.all_to_all(ret.reshape(rows // PAIR, PAIR, width), 'expert', split_ax...  3.84 us
    pallas_call x1, Pallas kernels, per_device(): pl.pallas_call(dispatch_kernel, out_shape=(pltpu.VMEM((slots, width), low...  1.79 us
    pallas_call x1, Pallas kernels, per_device(): pl.pallas_call(combine_kernel, out_shape=(jax.ShapeDtypeStruct((count, wi...  1.51 us
  transfers between devices with their start and end apart: 1, of which 0 were waited for; matrix products, arithmetic and copies ran while one was open for 0% of the time, Pallas kernels for 21%

profile of v14, /device:TPU:0, one launch (start us, length us, event | category | flops | bytes accessed | tf_op | source)
XLA Modules:
  0.0 67.5 jit_solution(11692830349834004403)
XLA Ops:
  0.6 1.8 %dispatch.1 = (bf16[128,1664]{1,0:T(8,128)(2,1)S(1)}, f32[8,128]{1,0:T(8,128)S(1)}, bf16[1664,256]{1,0:T(8,128)(2,1)S(1)}, bf16[256,1664]{1,0:T(8,128)(2,1)S(1)}) custom-call(s32[2,128]{1,0:T(2,128)} %bitcast.19, s32[1,128]{1,0:T(1,128)} %prio_hbm.1, f32[2,128]{1,0:T(2,128)} %bitcast.20, bf16[128,1664]{1,0:T(8,128)(2,1)} %tok_hbm.1, ...), custom_call_target="tpu_custom_call" | custom-call | tf_op jit(solution)/shard_map/dispatch/pallas_call | solution.py:398
  2.4 19.9 %all_to_all.10 = bf16[16,8,1664]{2,1,0:T(8,128)(2,1)S(1)} all-to-all(bf16[16,8,1664]{2,1,0:T(8,128)(2,1)S(1)} %bitcast.13), channel_id=1, replica_groups=mesh['groups'=2,'expert'=16] {'expert'}, dimensions={0} | all-to-all | bytes 851968 | tf_op jit(solution)/shard_map/all_to_all | solution.py:421
  22.3 25.9 %forward.1 = (bf16[128,1664]{1,0:T(8,128)(2,1)}, bf16[1664,64]{1,0:T(8,128)(2,1)S(1)}, bf16[64,1664]{1,0:T(8,128)(2,1)S(1)}, bf16[24,64,256]{2,1,0:T(8,128)(2,1)...) custom-call(bf16[128,1664]{1,0:T(8,128)(2,1)S(1)} %bitcast.11, ...), custom_call_target="tpu_custom_call" | custom-call | flops 5234491392 | bytes 40894464 | tf_op jit(solution)/shard_map/forward/pallas_call | solution.py:425
  48.3 0.0 copy-start
  48.3 3.8 %all-to-all-start.1 = ((bf16[16,8,1664]{2,1,0:T(8,128)(2,1)}), bf16[16,8,1664]{2,1,0:T(8,128)(2,1)S(1)}, u32[]{:S(2)}, u32[]{:S(2)}) async-start(bf16[16,8,1664]{2,1,0:T(8,128)(2,1)} %bitcast.6), calls=%async_computation.1 | async-start | bytes 851968 | tf_op jit(solution)/shard_map/all_to_all | solution.py:459
  52.1 13.9 %grads.1 = (bf16[1664,6144]{1,0:T(8,128)(2,1)}, bf16[6144,1664]{1,0:T(8,128)(2,1)}) custom-call(bf16[1664,64]{1,0:T(8,128)(2,1)S(1)} %get-tuple-element.32.x_t_ref, bf16[64,1664]{1,0:T(8,128)(2,1)S(1)} %get-tuple-element.33.g_ref, bf16[24,64,256]{2,1,0:T(8,128)(2,1)S(1)} %get-tuple-element.34.act_ref, ...), custom_call_target="tpu_custom_call", output_to_operand_aliasing={{1}: (4, {})} | custom-call | flops 2617245696 | bytes 40894464 | tf_op jit(solution)/shard_map/grads/pallas_call | solution.py:462
  66.0 0.0 all-to-all-done.1
  66.0 0.0 copy-done
  66.0 1.5 %combine.1 = (bf16[128,1664]{1,0:T(8,128)(2,1)}, bf16[128,1664]{1,0:T(8,128)(2,1)}, f32[2,128]{1,0:T(2,128)}) custom-call(bf16[128,1664]{1,0:T(8,128)(2,1)S(1)} %bitcast.12, bf16[384,128]{1,0:T(8,128)(2,1)S(1)} %get-tuple-element.27.pick_ref, f32[128,8]{1,0:T(8,128)S(1)} %get-tuple-element.28.gate_ref, bf16[128,1664]{1,0:T(8,128)(2,1)S(1)} %copy-done), custom_call_target="tpu_custom_call" | custom-call | tf_op jit(solution)/shard_map/combine/pallas_call | solution.py:484
Async XLA Ops:
  48.3 17.7 %copy-start = (bf16[128,1664]{1,0:T(8,128)(2,1)S(1)}, bf16[128,1664]{1,0:T(8,128)(2,1)}, u32[]{:S(2)}) copy-start(bf16[128,1664]{1,0:T(8,128)(2,1)} %cot_ref.1) | copy-start | bytes 1277956
  48.3 17.7 %all-to-all-start.1 = ((bf16[16,8,1664]{2,1,0:T(8,128)(2,1)}), bf16[16,8,1664]{2,1,0:T(8,128)(2,1)S(1)}, u32[]{:S(2)}, u32[]{:S(2)}) async-start(bf16[16,8,1664]{2,1,0:T(8,128)(2,1)} %bitcast.6), calls=%async_computation.1 | async-start | bytes 851968 | tf_op jit(solution)/shard_map/all_to_all | solution.py:459

commit v15 on v14

--- a/solution.py
+++ b/solution.py
@@ -11,7 +11,7 @@
 EXPERTS = 16
 CAP = 4
 PAIR = 2 * CAP
-EARLY = 64
+EARLY = 256
 LAST_DIM = (((1,), (1,)), ((), ()))
 
 
@@ -58,15 +58,15 @@
     ids_ref, prio_ref, gates_ref, both_ref, sem,
 ):
     count = tok_hbm.shape[0]
-    depth = w_in_ref.shape[1]
+    lead = w_in_ref.shape[1]
     pairs = (
         (ids_hbm, ids_ref),
         (prio_hbm, prio_ref),
         (gates_hbm, gates_ref),
         (tok_hbm, both_ref.at[0:count]),
         (cot_hbm, both_ref.at[count:2 * count]),
-        (w_in_hbm.at[:, 0:depth], w_in_ref),
-        (w_out_hbm.at[0:depth, :], w_out_ref),
+        (w_in_hbm.at[:, 0:lead], w_in_ref),
+        (w_out_hbm.at[0:lead, :], w_out_ref),
     )
     copies = [pltpu.make_async_copy(*pair, sem.at[index]) for index, pair in enumerate(pairs)]
     for copy in copies:
@@ -129,15 +129,23 @@
     ret_ref, x_t_ref, g_ref, act_ref, d_pre_ref, pick_ref, gate_ref, d_out_hbm,
     w_in_ref, w_out_ref, x_ref, act_t_ref, stage, out_acc, back_acc, sem_in, sem_out, sem_left,
 ):
-    width, depth = w_in_0.shape
+    width, lead = w_in_0.shape
+    depth = w_in_ref.shape[2]
     low = jnp.bfloat16
 
     def copies(step):
-        cols = pl.ds(pl.multiple_of(step * depth, depth), depth)
-        slot = step - 1
+        if isinstance(step, int) and step == 0:
+            cols = near = pl.ds(lead, depth - lead)
+        else:
+            cols = pl.ds(pl.multiple_of(step * depth, depth), depth)
+            near = pl.ds(0, depth)
         return (
-            pltpu.make_async_copy(w_in_hbm.at[:, cols], w_in_ref.at[slot], sem_in.at[slot]),
-            pltpu.make_async_copy(w_out_hbm.at[cols, :], w_out_ref.at[slot], sem_out.at[slot]),
+            pltpu.make_async_copy(
+                w_in_hbm.at[:, cols], w_in_ref.at[step, :, near], sem_in.at[step]
+            ),
+            pltpu.make_async_copy(
+                w_out_hbm.at[cols, :], w_out_ref.at[step, near, :], sem_out.at[step]
+            ),
         )
 
     def leave(step):
@@ -150,6 +158,7 @@
             copy.start()
         return carry
 
+    begin(0, 0)
     lax.fori_loop(1, steps, begin, 0)
     rows = recv_ref.shape[0]
     half = rows // 2
@@ -160,28 +169,39 @@
     out_acc[...] = jnp.zeros_like(out_acc)
     back_acc[...] = jnp.zeros_like(back_acc)
 
-    def weights(step):
+    def spans(step):
         if isinstance(step, int) and step == 0:
-            return w_in_0, w_out_0
-        return w_in_ref.at[step - 1], w_out_ref.at[step - 1]
-
-    def front_dots(step, found):
-        w_first, w_second = weights(step)
-        for first in range(0, depth, 256):
-            cols = slice(first, min(first + 256, depth))
+            return [slice(0, lead), slice(lead, depth)]
+        return [slice(0, depth)]
+
+    def w_first(step, rows, cols):
+        if isinstance(step, int) and step == 0 and cols.stop <= lead:
+            return w_in_0[rows, cols]
+        return w_in_ref[step, rows, cols]
+
+    def w_second(step, rows, cols):
+        if isinstance(step, int) and step == 0 and rows.stop <= lead:
+            return w_out_0[rows, cols]
+        return w_out_ref[step, rows, cols]
+
+    every = slice(0, width)
+
+    def front_dots(step, found, span):
+        for first in range(span.start, span.stop, 256):
+            cols = slice(first, min(first + 256, span.stop))
             pre = []
 
             def one(cols=cols, pre=pre):
                 pre.append(
                     jnp.dot(
-                        x_ref[...], w_first[:, cols], preferred_element_type=jnp.float32
+                        x_ref[...], w_first(step, every, cols), preferred_element_type=jnp.float32
                     )
                 )
 
             def two(cols=cols, pre=pre):
                 d_act = lax.dot_general(
                     g_ref[...],
-                    w_second[cols, :],
+                    w_second(step, cols, every),
                     LAST_DIM,
                     preferred_element_type=jnp.float32,
                 )
@@ -191,22 +211,23 @@
             yield two
 
     def back_dots(step, act, d_pre):
-        w_first, w_second = weights(step)
         for first in range(0, width, 256):
             cols = slice(first, min(first + 256, width))
 
             def one(cols=cols):
-                out_acc[:, cols] += jnp.dot(
-                    act, w_second[:, cols], preferred_element_type=jnp.float32
-                )
+                for span in spans(step):
+                    out_acc[:, cols] += jnp.dot(
+                        act[:, span], w_second(step, span, cols), preferred_element_type=jnp.float32
+                    )
 
             def two(cols=cols):
-                back_acc[:, cols] += lax.dot_general(
-                    d_pre,
-                    w_first[cols, :],
-                    LAST_DIM,
-                    preferred_element_type=jnp.float32,
-                )
+                for span in spans(step):
+                    back_acc[:, cols] += lax.dot_general(
+                        d_pre[:, span],
+                        w_first(step, cols, span),
+                        LAST_DIM,
+                        preferred_element_type=jnp.float32,
+                    )
 
             yield one
             yield two
@@ -215,13 +236,15 @@
         slot = lax.rem(step, 2)
         for first in range(0, width, 256):
             cols = slice(first, min(first + 256, width))
-
-            def one(cols=cols):
-                stage[slot, :, cols] = jnp.dot(
-                    act_t, g_ref[:, cols], preferred_element_type=jnp.float32
-                ).astype(low)
-
-            yield one
+            for top in range(0, EARLY, 128):
+                some = slice(top, top + 128)
+
+                def one(cols=cols, some=some):
+                    stage[slot, some, cols] = jnp.dot(
+                        act_t[some], g_ref[:, cols], preferred_element_type=jnp.float32
+                    ).astype(low)
+
+                yield one
 
     def middle(step, found):
         for cols, pre, d_act in found:
@@ -245,7 +268,7 @@
             copy.wait()
         act, act_t, d_pre = act_ref[step - 1], act_t_ref[...], d_pre_ref[step - 1]
         found = []
-        fronts = [*front_dots(step, found)]
+        fronts = [*front_dots(step, found, slice(0, depth))]
         backs = [*back_dots(step - 1, act, d_pre)]
         blocks = len(fronts) // 2
         share = len(backs) // (blocks + 1)
@@ -258,10 +281,14 @@
         run(turns, [*grad_dots(step - 1, act_t)])
         leave(step - 1).start()
 
-    found = []
-    for thunk in front_dots(0, found):
-        thunk()
-    middle(0, found)
+    for part, span in enumerate(spans(0)):
+        if part:
+            for copy in copies(0):
+                copy.wait()
+        found = []
+        for thunk in front_dots(0, found, span):
+            thunk()
+        middle(0, found)
 
     def aside():
         x_t_ref[...] = jnp.transpose(x_rows, (1, 0)).astype(low)
@@ -326,7 +353,7 @@
         for index in range(2):
             first = index * (later // 2)
             here = pl.ds(first, later // 2)
-            there = pl.ds(pl.multiple_of(step * depth + EARLY + first, 32), later // 2)
+            there = pl.ds(pl.multiple_of(step * depth + EARLY + first, 64), later // 2)
             pairs.append((d_out_stage.at[slot, here], d_out_hbm.at[there]))
         return [
             pltpu.make_async_copy(*pair, sem.at[slot, index]) for index, pair in enumerate(pairs)
@@ -393,15 +420,15 @@
     low = jnp.bfloat16
     vmem = pl.BlockSpec(memory_space=pltpu.VMEM)
     hbm = pl.BlockSpec(memory_space=pl.ANY)
-    chunk = chunk_of(hidden, 256)
+    chunk = chunk_of(hidden, 1024)
     steps = hidden // chunk
     send, plan, w_in_0, w_out_0 = pl.pallas_call(
         dispatch_kernel,
         out_shape=(
             pltpu.VMEM((slots, width), low),
             pltpu.VMEM((8, count), jnp.float32),
-            pltpu.VMEM((width, chunk), low),
-            pltpu.VMEM((chunk, width), low),
+            pltpu.VMEM((width, chunk // 2), low),
+            pltpu.VMEM((chunk // 2, width), low),
         ),
         in_specs=[hbm] * 7,
         out_specs=(vmem,) * 4,
@@ -437,18 +464,18 @@
         in_specs=[vmem] * 4 + [hbm] * 2,
         out_specs=(vmem,) * 7 + (hbm,),
         scratch_shapes=[
-            pltpu.VMEM((max(steps - 1, 1), width, chunk), low),
-            pltpu.VMEM((max(steps - 1, 1), chunk, width), low),
+            pltpu.VMEM((steps, width, chunk), low),
+            pltpu.VMEM((steps, chunk, width), low),
             pltpu.VMEM((half, width), low),
             pltpu.VMEM((EARLY, half), low),
             pltpu.VMEM((2, EARLY, width), low),
             pltpu.VMEM((half, width), jnp.float32),
             pltpu.VMEM((half, width), jnp.float32),
-            pltpu.SemaphoreType.DMA((max(steps - 1, 1),)),
-            pltpu.SemaphoreType.DMA((max(steps - 1, 1),)),
+            pltpu.SemaphoreType.DMA((steps,)),
+            pltpu.SemaphoreType.DMA((steps,)),
             pltpu.SemaphoreType.DMA((2,)),
         ],
-        compiler_params=params(43),
+        compiler_params=params(45),
         cost_estimate=pl.CostEstimate(
             flops=8 * half * width * hidden,
             bytes_accessed=4 * width * hidden,
@@ -473,7 +500,7 @@
             pltpu.VMEM((3, chunk - EARLY, width), low),
             pltpu.SemaphoreType.DMA((3, 4)),
         ],
-        compiler_params=params(24),
+        compiler_params=params(28),
         cost_estimate=pl.CostEstimate(
             flops=4 * half * width * hidden,
             bytes_accessed=4 * width * hidden,

time: 67.8 us -> 64.4 us (0.950)
  Pallas kernels: 43.1 us -> 39.7 us
    pallas_call x1, Pallas kernels: 25.9 us -> 23.1 us  [per_device(): pl.pallas_call(functools.partial(forward_kernel, steps), out_shape=(pltpu...]
    pallas_call x1, Pallas kernels: 13.9 us -> 12.7 us  [per_device(): pl.pallas_call(grads_kernel, out_shape=(jax.ShapeDtypeStruct((width, hidd...]
  transfers between devices with their start and end apart: 1 -> 1, of which waited for: 0 -> 0; matrix products, arithmetic and copies ran while one was open for 0% -> 0% of each run, Pallas kernels for 21% -> 20%
where the time goes in v15:
time: 64.4 us; the launch traced here: 64.1 us
  Pallas kernels  39.7 us (62%)
  blocking collectives  19.9 us (31%)
  starting transfers between devices  3.84 us (6%)
  between operations  0.67 us (1%)
    pallas_call x1, Pallas kernels, per_device(): pl.pallas_call(functools.partial(forward_kernel, steps), out_shape=(pltpu...  23.1 us
    all_to_all x1, blocking collectives, per_device(): lax.all_to_all(send, 'expert', split_axis=0, concat_axis=0, tiled=True)  19.9 us
    pallas_call x1, Pallas kernels, per_device(): pl.pallas_call(grads_kernel, out_shape=(jax.ShapeDtypeStruct((width, hidd...  12.7 us
    all_to_all x1, starting transfers between devices, per_device(): lax.all_to_all(ret.reshape(rows // PAIR, PAIR, width), 'expert', split_ax...  3.84 us
    pallas_call x1, Pallas kernels, per_device(): pl.pallas_call(dispatch_kernel, out_shape=(pltpu.VMEM((slots, width), low...  2.35 us
    pallas_call x1, Pallas kernels, per_device(): pl.pallas_call(combine_kernel, out_shape=(jax.ShapeDtypeStruct((count, wi...  1.51 us
  transfers between devices with their start and end apart: 1, of which 0 were waited for; matrix products, arithmetic and copies ran while one was open for 0% of the time, Pallas kernels for 20%

profile of v15, /device:TPU:0, one launch (start us, length us, event | category | flops | bytes accessed | tf_op | source)
XLA Modules:
  0.0 64.1 jit_solution(6004856897291358772)
XLA Ops:
  0.6 2.4 %dispatch.1 = (bf16[128,1664]{1,0:T(8,128)(2,1)S(1)}, f32[8,128]{1,0:T(8,128)S(1)}, bf16[1664,512]{1,0:T(8,128)(2,1)S(1)}, bf16[512,1664]{1,0:T(8,128)(2,1)S(1)}) custom-call(s32[2,128]{1,0:T(2,128)} %bitcast.19, s32[1,128]{1,0:T(1,128)} %prio_hbm.1, f32[2,128]{1,0:T(2,128)} %bitcast.20, bf16[128,1664]{1,0:T(8,128)(2,1)} %tok_hbm.1, ...), custom_call_target="tpu_custom_call" | custom-call | tf_op jit(solution)/shard_map/dispatch/pallas_call | solution.py:425
  3.0 19.9 %all_to_all.10 = bf16[16,8,1664]{2,1,0:T(8,128)(2,1)S(1)} all-to-all(bf16[16,8,1664]{2,1,0:T(8,128)(2,1)S(1)} %bitcast.13), channel_id=1, replica_groups=mesh['groups'=2,'expert'=16] {'expert'}, dimensions={0} | all-to-all | bytes 851968 | tf_op jit(solution)/shard_map/all_to_all | solution.py:448
  22.9 23.1 %forward.1 = (bf16[128,1664]{1,0:T(8,128)(2,1)}, bf16[1664,64]{1,0:T(8,128)(2,1)S(1)}, bf16[64,1664]{1,0:T(8,128)(2,1)S(1)}, bf16[6,64,1024]{2,1,0:T(8,128)(2,1)...) custom-call(bf16[128,1664]{1,0:T(8,128)(2,1)S(1)} %bitcast.11, ...), custom_call_target="tpu_custom_call" | custom-call | flops 5234491392 | bytes 40894464 | tf_op jit(solution)/shard_map/forward/pallas_call | solution.py:452
  46.0 0.0 copy-start
  46.0 3.8 %all-to-all-start.1 = ((bf16[16,8,1664]{2,1,0:T(8,128)(2,1)}), bf16[16,8,1664]{2,1,0:T(8,128)(2,1)S(1)}, u32[]{:S(2)}, u32[]{:S(2)}) async-start(bf16[16,8,1664]{2,1,0:T(8,128)(2,1)} %bitcast.6), calls=%async_computation.1 | async-start | bytes 851968 | tf_op jit(solution)/shard_map/all_to_all | solution.py:486
  49.9 12.7 %grads.1 = (bf16[1664,6144]{1,0:T(8,128)(2,1)}, bf16[6144,1664]{1,0:T(8,128)(2,1)}) custom-call(bf16[1664,64]{1,0:T(8,128)(2,1)S(1)} %get-tuple-element.32.x_t_ref, bf16[64,1664]{1,0:T(8,128)(2,1)S(1)} %get-tuple-element.33.g_ref, bf16[6,64,1024]{2,1,0:T(8,128)(2,1)S(1)} %get-tuple-element.34.act_ref, ...), custom_call_target="tpu_custom_call", output_to_operand_aliasing={{1}: (4, {})} | custom-call | flops 2617245696 | bytes 40894464 | tf_op jit(solution)/shard_map/grads/pallas_call | solution.py:489
  62.6 0.0 all-to-all-done.1
  62.6 0.0 copy-done
  62.6 1.5 %combine.1 = (bf16[128,1664]{1,0:T(8,128)(2,1)}, bf16[128,1664]{1,0:T(8,128)(2,1)}, f32[2,128]{1,0:T(2,128)}) custom-call(bf16[128,1664]{1,0:T(8,128)(2,1)S(1)} %bitcast.12, bf16[384,128]{1,0:T(8,128)(2,1)S(1)} %get-tuple-element.27.pick_ref, f32[128,8]{1,0:T(8,128)S(1)} %get-tuple-element.28.gate_ref, bf16[128,1664]{1,0:T(8,128)(2,1)S(1)} %copy-done), custom_call_target="tpu_custom_call" | custom-call | tf_op jit(solution)/shard_map/combine/pallas_call | solution.py:511
Async XLA Ops:
  46.0 16.6 %copy-start = (bf16[128,1664]{1,0:T(8,128)(2,1)S(1)}, bf16[128,1664]{1,0:T(8,128)(2,1)}, u32[]{:S(2)}) copy-start(bf16[128,1664]{1,0:T(8,128)(2,1)} %cot_ref.1) | copy-start | bytes 1277956
  46.0 16.6 %all-to-all-start.1 = ((bf16[16,8,1664]{2,1,0:T(8,128)(2,1)}), bf16[16,8,1664]{2,1,0:T(8,128)(2,1)S(1)}, u32[]{:S(2)}, u32[]{:S(2)}) async-start(bf16[16,8,1664]{2,1,0:T(8,128)(2,1)} %bitcast.6), calls=%async_computation.1 | async-start | bytes 851968 | tf_op jit(solution)/shard_map/all_to_all | solution.py:486

commit v16 on v15

--- a/solution.py
+++ b/solution.py
@@ -382,24 +382,40 @@
             copy.wait()
 
 
-def combine_kernel(ret_ref, pick_ref, gate_ref, cot_ref, mixed_ref, d_tok_ref, d_gate_ref):
+def combine_kernel(
+    ret_ref, pick_ref, gate_ref, cot_ref, mixed_hbm, d_tok_hbm, d_gate_ref,
+    mixed_ref, d_tok_ref, sem,
+):
     count = cot_ref.shape[0]
     rows = pick_ref.shape[1]
-    found = None
-    for first in range(0, ret_ref.shape[0], rows):
-        part = jnp.dot(
-            pick_ref[...], ret_ref[first:first + rows, :], preferred_element_type=jnp.float32
-        )
-        found = part if found is None else found + part
-    o_0, o_1 = found[:count], found[count:2 * count]
+
+    def found(first, last):
+        total = None
+        for row in range(0, ret_ref.shape[0], rows):
+            part = jnp.dot(
+                pick_ref[first:last, :],
+                ret_ref[row:row + rows, :],
+                preferred_element_type=jnp.float32,
+            )
+            total = part if total is None else total + part
+        return total
+
+    d_tok_copy = pltpu.make_async_copy(d_tok_ref, d_tok_hbm, sem.at[0])
+    mixed_copy = pltpu.make_async_copy(mixed_ref, mixed_hbm, sem.at[1])
+    d_tok_ref[...] = found(2 * count, 3 * count).astype(jnp.bfloat16)
+    d_tok_copy.start()
+    picked = found(0, 2 * count)
+    o_0, o_1 = picked[:count], picked[count:]
     mixed_ref[...] = (gate_ref[:, 2:3] * o_0 + gate_ref[:, 3:4] * o_1).astype(jnp.bfloat16)
-    d_tok_ref[...] = found[2 * count:].astype(jnp.bfloat16)
+    mixed_copy.start()
     cot = cot_ref[...].astype(jnp.float32)
     d_0 = jnp.sum(cot * o_0, axis=1, keepdims=True)
     d_1 = jnp.sum(cot * o_1, axis=1, keepdims=True)
     lane = lax.broadcasted_iota(jnp.int32, (count, 8), 1)
     both = jnp.where(lane == 0, d_0, jnp.where(lane == 1, d_1, 0.0))
     d_gate_ref[...] = jnp.transpose(both, (1, 0))[0:2, :]
+    d_tok_copy.wait()
+    mixed_copy.wait()
 
 
 def params(mib):
@@ -515,6 +531,13 @@
             jax.ShapeDtypeStruct((count, width), low),
             jax.ShapeDtypeStruct((2, count), jnp.float32),
         ),
+        in_specs=[vmem] * 4,
+        out_specs=(hbm, hbm, vmem),
+        scratch_shapes=[
+            pltpu.VMEM((count, width), low),
+            pltpu.VMEM((count, width), low),
+            pltpu.SemaphoreType.DMA((2,)),
+        ],
         compiler_params=params(12),
         name="combine",
     )(ret, pick, gate_cols, cotangent)

time: 64.4 us -> 64.8 us (level)
  no operation moved by 1% of the time
where the time goes in v16:
time: 64.8 us; the launch traced here: 64.6 us
  Pallas kernels  40.1 us (62%)
  blocking collectives  19.9 us (31%)
  starting transfers between devices  3.84 us (6%)
  between operations  0.67 us (1%)
    pallas_call x1, Pallas kernels, per_device(): pl.pallas_call(functools.partial(forward_kernel, steps), out_shape=(pltpu...  23.1 us
    all_to_all x1, blocking collectives, per_device(): lax.all_to_all(send, 'expert', split_axis=0, concat_axis=0, tiled=True)  19.9 us
    pallas_call x1, Pallas kernels, per_device(): pl.pallas_call(grads_kernel, out_shape=(jax.ShapeDtypeStruct((width, hidd...  12.7 us
    all_to_all x1, starting transfers between devices, per_device(): lax.all_to_all(ret.reshape(rows // PAIR, PAIR, width), 'expert', split_ax...  3.84 us
    pallas_call x1, Pallas kernels, per_device(): pl.pallas_call(dispatch_kernel, out_shape=(pltpu.VMEM((slots, width), low...  2.35 us
    pallas_call x1, Pallas kernels, per_device(): pl.pallas_call(combine_kernel, out_shape=(jax.ShapeDtypeStruct((count, wi...  1.97 us
  transfers between devices with their start and end apart: 1, of which 0 were waited for; matrix products, arithmetic and copies ran while one was open for 0% of the time, Pallas kernels for 20%

profile of v16, /device:TPU:0, one launch (start us, length us, event | category | flops | bytes accessed | tf_op | source)
XLA Modules:
  0.0 64.6 jit_solution(11189198513608126394)
XLA Ops:
  0.6 2.4 %dispatch.1 = (bf16[128,1664]{1,0:T(8,128)(2,1)S(1)}, f32[8,128]{1,0:T(8,128)S(1)}, bf16[1664,512]{1,0:T(8,128)(2,1)S(1)}, bf16[512,1664]{1,0:T(8,128)(2,1)S(1)}) custom-call(s32[2,128]{1,0:T(2,128)} %bitcast.19, s32[1,128]{1,0:T(1,128)} %prio_hbm.1, f32[2,128]{1,0:T(2,128)} %bitcast.20, bf16[128,1664]{1,0:T(8,128)(2,1)} %tok_hbm.1, ...), custom_call_target="tpu_custom_call" | custom-call | tf_op jit(solution)/shard_map/dispatch/pallas_call | solution.py:441
  3.0 19.9 %all_to_all.10 = bf16[16,8,1664]{2,1,0:T(8,128)(2,1)S(1)} all-to-all(bf16[16,8,1664]{2,1,0:T(8,128)(2,1)S(1)} %bitcast.13), channel_id=1, replica_groups=mesh['groups'=2,'expert'=16] {'expert'}, dimensions={0} | all-to-all | bytes 851968 | tf_op jit(solution)/shard_map/all_to_all | solution.py:464
  22.9 23.1 %forward.1 = (bf16[128,1664]{1,0:T(8,128)(2,1)}, bf16[1664,64]{1,0:T(8,128)(2,1)S(1)}, bf16[64,1664]{1,0:T(8,128)(2,1)S(1)}, bf16[6,64,1024]{2,1,0:T(8,128)(2,1)...) custom-call(bf16[128,1664]{1,0:T(8,128)(2,1)S(1)} %bitcast.11, ...), custom_call_target="tpu_custom_call" | custom-call | flops 5234491392 | bytes 40894464 | tf_op jit(solution)/shard_map/forward/pallas_call | solution.py:468
  46.0 0.0 copy-start
  46.0 3.8 %all-to-all-start.1 = ((bf16[16,8,1664]{2,1,0:T(8,128)(2,1)}), bf16[16,8,1664]{2,1,0:T(8,128)(2,1)S(1)}, u32[]{:S(2)}, u32[]{:S(2)}) async-start(bf16[16,8,1664]{2,1,0:T(8,128)(2,1)} %bitcast.6), calls=%async_computation.1 | async-start | bytes 851968 | tf_op jit(solution)/shard_map/all_to_all | solution.py:502
  49.9 12.7 %grads.1 = (bf16[1664,6144]{1,0:T(8,128)(2,1)}, bf16[6144,1664]{1,0:T(8,128)(2,1)}) custom-call(bf16[1664,64]{1,0:T(8,128)(2,1)S(1)} %get-tuple-element.32.x_t_ref, bf16[64,1664]{1,0:T(8,128)(2,1)S(1)} %get-tuple-element.33.g_ref, bf16[6,64,1024]{2,1,0:T(8,128)(2,1)S(1)} %get-tuple-element.34.act_ref, ...), custom_call_target="tpu_custom_call", output_to_operand_aliasing={{1}: (4, {})} | custom-call | flops 2617245696 | bytes 40894464 | tf_op jit(solution)/shard_map/grads/pallas_call | solution.py:505
  62.6 0.0 all-to-all-done.1
  62.6 0.0 copy-done
  62.6 2.0 %combine.1 = (bf16[128,1664]{1,0:T(8,128)(2,1)}, bf16[128,1664]{1,0:T(8,128)(2,1)}, f32[2,128]{1,0:T(2,128)}) custom-call(bf16[128,1664]{1,0:T(8,128)(2,1)S(1)} %bitcast.12, bf16[384,128]{1,0:T(8,128)(2,1)S(1)} %get-tuple-element.27.pick_ref, f32[128,8]{1,0:T(8,128)S(1)} %get-tuple-element.28.gate_ref, bf16[128,1664]{1,0:T(8,128)(2,1)S(1)} %copy-done), custom_call_target="tpu_custom_call" | custom-call | tf_op jit(solution)/shard_map/combine/pallas_call | solution.py:527
Async XLA Ops:
  46.0 16.6 %copy-start = (bf16[128,1664]{1,0:T(8,128)(2,1)S(1)}, bf16[128,1664]{1,0:T(8,128)(2,1)}, u32[]{:S(2)}) copy-start(bf16[128,1664]{1,0:T(8,128)(2,1)} %cot_ref.1) | copy-start | bytes 1277956
  46.0 16.6 %all-to-all-start.1 = ((bf16[16,8,1664]{2,1,0:T(8,128)(2,1)}), bf16[16,8,1664]{2,1,0:T(8,128)(2,1)S(1)}, u32[]{:S(2)}, u32[]{:S(2)}) async-start(bf16[16,8,1664]{2,1,0:T(8,128)(2,1)} %bitcast.6), calls=%async_computation.1 | async-start | bytes 851968 | tf_op jit(solution)/shard_map/all_to_all | solution.py:502
